TPU v7x, 32 devices: a whole 2x2x4 slice. The times are simulated.
32 devices in a mesh: dp: 4 (over x, core), patch: 8 (over z, y).
Axes of the slice: x: 2, y: 2, z: 4, core: 2. Of those that a mesh axis runs over, the one named last changes fastest.
Arguments:
- rows: bfloat16 [22528, 1280], P(('dp', 'patch')), may hold values from -6 to 6
- grad_hidden: bfloat16 [22528, 2560], P(('dp', 'patch')), may hold values from -6 to 6
- counts: int32 [4, 8], P('dp'), may hold values from 1 to 704, 2816 in all within a row
- w_in: bfloat16 [2560, 1280], P('patch'), may hold values from -0.15625 to 0.15625
- b_in: bfloat16 [2560], P('patch'), may hold values from -3 to 3
- gamma: float32 [1280], replicated, may hold values from 0.1 to 1.9
- beta: float32 [1280], replicated, may hold values from -3 to 3
Outputs:
- grad_rows: bfloat16 [22528, 1280], P(('dp', 'patch'))
- grad_w_in: float32 [2560, 1280], P('patch')
Inputs may be any that keep to these rules, and one draw needn't show every extreme that they name: In each dp group the 8 counts sum to 2816, and one device of each group has exactly 704.
All inputs are finite; a program needn't handle non-finite values.
Results may differ from a plain program's by a relative error of at most 0.0056.
Values may be sent and summed in bfloat16 or wider, within the bound.
No kernel may reach another device: no remote copies, remote signals or barrier semaphores. Data moves between devices by JAX's collectives and lax.ppermute only.
A program may use at most 128 MiB of HBM per device.

v0:
```python
import math

import jax
import jax.numpy as jnp
from jax import lax
from jax.sharding import PartitionSpec as P

VIS_DEV = 352


def gelu_slope(pre_act):
    normal_cdf = 0.5 * (1.0 + jax.scipy.special.erf(pre_act * (1.0 / math.sqrt(2.0))))
    density = jnp.exp(-0.5 * pre_act * pre_act) * (1.0 / math.sqrt(2.0 * math.pi))
    return normal_cdf + pre_act * density


def normed(block, gamma, beta):
    as_float = block.astype(jnp.float32)
    mean_row = jnp.mean(as_float, axis=1, keepdims=True)
    centred = as_float - mean_row
    variance = jnp.mean(centred * centred, axis=1, keepdims=True)
    inverse = lax.rsqrt(variance + 1e-05)
    standard = centred * inverse
    normed_rows = (standard * gamma + beta).astype(jnp.bfloat16)
    return (standard, inverse, normed_rows)


def finish(normed_grad, standard, inverse, gamma):
    scaled = normed_grad * gamma
    first = jnp.mean(scaled, axis=1, keepdims=True)
    second = jnp.mean(scaled * standard, axis=1, keepdims=True)
    return inverse * (scaled - first - standard * second)


def per_device(rows, grad_hidden, counts, w_in, b_in, gamma, beta):
    patch_count = lax.axis_size("patch")
    data_count = lax.axis_size("dp")
    my_index = lax.axis_index("patch")
    per_dev = rows.shape[0]
    row_counts = counts[0]
    my_count = jnp.take(row_counts, my_index)
    live_rows = jnp.arange(per_dev, dtype=jnp.int32) < my_count
    standard, inverse, normed_rows = normed(rows, gamma, beta)
    w_piece = lax.all_gather(w_in, "patch", axis=0, tiled=True)
    b_piece = lax.all_gather(b_in, "patch", axis=0, tiled=True)
    pre_act = lax.dot_general(
        normed_rows, w_piece, (((1,), (1,)), ((), ())), preferred_element_type=jnp.float32
    ) + b_piece.astype(jnp.float32)
    slope_part = grad_hidden.astype(jnp.float32) * gelu_slope(pre_act)
    slope_part = jnp.where(live_rows[:, None], slope_part, 0.0)
    slope_part = slope_part.astype(jnp.bfloat16)
    normed_grad = jnp.dot(slope_part, w_piece, preferred_element_type=jnp.float32)
    normed_grad, hidden_grad = (normed_grad, slope_part)
    grad_here = finish(normed_grad, standard, inverse, gamma).astype(jnp.bfloat16)
    grad_rows = jnp.where(live_rows[:, None], grad_here, jnp.zeros((), jnp.bfloat16))
    grad_scale = 1.0 / math.sqrt(VIS_DEV * patch_count * data_count)
    partial_value = lax.psum_scatter(
        grad_scale
        * lax.dot_general(
            hidden_grad, normed_rows, (((0,), (0,)), ((), ())), preferred_element_type=jnp.float32
        ),
        "patch",
        scatter_dimension=0,
        tiled=True,
    )
    grad_w_in = lax.psum(partial_value, "dp")
    return (grad_rows, grad_w_in)


def solution(mesh):
    in_specs = (
        P(("dp", "patch"), None),
        P(("dp", "patch"), None),
        P("dp", None),
        P("patch", None),
        P("patch"),
        P(),
        P(),
    )
    out_specs = (P(("dp", "patch"), None), P("patch", None))
    return jax.shard_map(
        per_device, mesh=mesh, in_specs=in_specs, out_specs=out_specs, check_vma=False
    )
```

profile of v0, /device:TPU:0, one launch (start us, length us, event | category | flops | bytes accessed | tf_op | source)
XLA Modules:
  0.0 405.3 jit_solution(17538564858243758198)
XLA Ops:
  7.2 0.0 copy-start
  7.2 0.0 copy-start.1
  7.2 0.0 copy-start.3
  7.2 0.0 copy-start.2
  7.2 0.0 all-gather.2.cloned.1.call-start
  7.3 0.7 all-gather.2.cloned.1.call-update
  7.9 0.0 reduce-scatter.2.cloned.1.call-start
  8.0 0.0 copy-done
  8.0 0.6 constant_dynamic-slice_fusion
  8.6 1.2 dynamic-slice.4
  10.5 0.9 dynamic-update-slice.1
  11.4 23.9 %all-reduce = bf16[2560]{0:T(1024)(128)(2,1)S(1)} all-reduce(bf16[2560]{0:T(1024)(128)(2,1)S(1)} %dynamic-update-slice.1), channel_id=1, replica_groups=mesh['dp'=4,'patch'=8] {'patch'}, use_global_device_ids=true, to_apply=%add | all-reduce | flops 2560 | bytes 10240
  36.0 1.8 convert_reduce_fusion
  37.8 0.0 copy-done.1
  37.8 0.6 fusion.18
  38.4 77.0 %all-gather.2.cloned.1.call-done = bf16[2560,1280]{1,0:T(8,128)(2,1)} async-done(((bf16[320,1280]{1,0:T(8,128)(2,1)}), bf16[2560,1280]{1,0:T(8,128)(2,1)}) %all-gather.2.cloned.1.call-update) | async-done | bytes 6553616 | tf_op jit(solution)/shard_map/all_gather | solution.py:44
  115.5 0.0 copy-done.3
  115.5 0.0 copy-done.2
  115.5 11.4 %fusion.6 = bf16[704,2560]{1,0:T(8,128)(2,1)S(1)} fusion(bf16[704,2560]{1,0:T(8,128)(2,1)} %param.8, bf16[2560,1280]{1,0:T(8,128)(2,1)} %all-gather.2.cloned.1.call-done, f32[2560]{0:T(1024)S(1)} %convert_element_type.21, pred[704]{0:T(1024)(128)(4,1)S(1)} %iota_compare_fusion, bf16[704,1280]{1,0:T(8,128)(2,1)S(1)} %copy-done.1, f32[1280]{0:T(1024)S(1)} %copy-done.2, ...), kind=kOutput, calls=%fused_computation.8 | convolution fusion | flops 4642570240 | bytes 15591616 | tf_op jit(solution)/shard_map/dot_general | solution.py:46
  126.9 0.0 copy-start.4
  126.9 1.8 copy-done.4
  128.8 8.7 %convolution_multiply_fusion = f32[2560,1280]{1,0:T(8,128)} fusion(bf16[704,2560]{1,0:T(8,128)(2,1)S(1)} %fusion.6, bf16[704,1280]{1,0:T(8,128)(2,1)S(1)} %copy-done.1, f32[1280]{0:T(1024)S(1)} %copy-done.2, f32[1280]{0:T(1024)S(1)} %copy-done.3, f32[704]{0:T(1024)S(1)} %add_rsqrt_fusion, f32[704]{0:T(1024)S(1)} %broadcast_multiply_fusion.2), kind=kOutput, calls=%fused_computation | convolution fusion | flops 4622417920 | bytes 18529792 | tf_op jit(solution)/shard_map/dot_general | solution.py:59
  137.4 0.0 reduce-scatter.2.cloned.1.call-update
  137.5 0.2 all-reduce.3.cloned.1.call-start
  137.7 10.9 %fusion.22 = (f32[704]{0:T(1024)S(1)}, f32[704]{0:T(1024)S(1)}, f32[704,1280]{1,0:T(8,128)}) fusion(f32[704]{0:T(1024)S(1)} %add_rsqrt_fusion, f32[704]{0:T(1024)S(1)} %broadcast_multiply_fusion.2, bf16[704,1280]{1,0:T(8,128)(2,1)S(1)} %copy-done.1, f32[1280]{0:T(1024)S(1)} %copy-done.3, bf16[704,2560]{1,0:T(8,128)(2,1)} %copy-done.4, ...), kind=kOutput, calls=%fused_computation.31 | convolution fusion | flops 4620041216 | bytes 15581184 | tf_op jit(solution)/shard_map/dot_general | solution.py:52
  148.6 202.0 %reduce-scatter.2.cloned.1.call-done = f32[320,1280]{1,0:T(8,128)} async-done(((f32[2560,1280]{1,0:T(8,128)}), f32[320,1280]{1,0:T(8,128)}) %reduce-scatter.2.cloned.1.call-update) | async-done | bytes 1638416 | tf_op jit(solution)/shard_map/reduce_scatter | solution.py:57
  350.6 0.0 all-reduce.3.cloned.1.call-update
  350.7 3.7 fusion.19
  354.4 41.7 %all-reduce.3.cloned.1.call-done = f32[320,1280]{1,0:T(8,128)} async-done(((f32[320,1280]{1,0:T(8,128)}), f32[320,1280]{1,0:T(8,128)}) %all-reduce.3.cloned.1.call-update) | async-done | bytes 1638416 | tf_op jit(solution)/shard_map/psum | solution.py:66
  396.1 2.7 copy.11
  (6 shorter events, 0.0 us)
Async XLA Ops:
  7.2 0.8 copy-start
  7.2 30.6 %copy-start.1 = (bf16[704,1280]{1,0:T(8,128)(2,1)S(1)}, bf16[704,1280]{1,0:T(8,128)(2,1)}, u32[]{:S(2)}) copy-start(bf16[704,1280]{1,0:T(8,128)(2,1)} %param.7) | copy-start | bytes 5406724
  7.2 108.3 %copy-start.3 = (f32[1280]{0:T(1024)S(1)}, f32[1280]{0:T(1024)}, u32[]{:S(2)}) copy-start(f32[1280]{0:T(1024)} %param.12) | copy-start | bytes 15364
  7.2 108.3 %copy-start.2 = (f32[1280]{0:T(1024)S(1)}, f32[1280]{0:T(1024)}, u32[]{:S(2)}) copy-start(f32[1280]{0:T(1024)} %param.13) | copy-start | bytes 15364
  7.2 108.3 %all-gather.2.cloned.1.call-start = ((), (), s32[]{:S(2)}) async-start(), calls=%async_computation.1 | async-start | bytes 7372800 | tf_op jit(solution)/shard_map/all_gather | solution.py:44
  7.9 342.7 %reduce-scatter.2.cloned.1.call-start = ((), (), s32[]{:S(2)}) async-start(), calls=%async_computation.2 | async-start | bytes 14745600 | tf_op jit(solution)/shard_map/reduce_scatter | solution.py:57
  126.9 1.9 copy-start.4
  137.5 258.6 %all-reduce.3.cloned.1.call-start = ((), (), s32[]{:S(2)}) async-start(), calls=%async_computation.3 | async-start | bytes 3276800 | tf_op jit(solution)/shard_map/psum | solution.py:66
Sparse Core Ops, SparseCore 0:
  10.2 105.2 all-gather.1
  137.6 212.9 reduce-scatter.1
  353.0 43.0 all-reduce.2
where the time goes:
time: 406 us; the launch traced here: 405 us
  waiting for transfers between devices  321 us (79%)
  matrix products  31 us (8%)
  blocking collectives  23.9 us (6%)
  between operations  15.2 us (4%)
  local copies, waits for them, and re-layouts  7.27 us (2%)
  other arithmetic  6.15 us (2%)
    reduce_scatter x1, waiting for transfers between devices, per_device(): lax.psum_scatter(grad_scale * lax.dot_general(hidden_grad, normed_rows, (...  202 us
    all_gather x1, waiting for transfers between devices, per_device(): w_piece = lax.all_gather(w_in, 'patch', axis=0, tiled=True)  77 us
    psum x1, waiting for transfers between devices, per_device(): grad_w_in = lax.psum(partial_value, 'dp')  41.7 us
    unnamed x1, blocking collectives  23.9 us
    dot_general x1, matrix products, per_device(): lax.dot_general(normed_rows, w_piece, (((1,), (1,)), ((), ())), preferred...  11.4 us
    dot_general x1, matrix products, per_device(): jnp.dot(slope_part, w_piece, preferred_element_type=jnp.float32)  10.9 us
    dot_general x1, matrix products, per_device(): lax.dot_general(hidden_grad, normed_rows, (((0,), (0,)), ((), ())), prefe...  8.68 us
  transfers between devices with their start and end apart: 3, of which 3 were waited for; matrix products, arithmetic and copies ran while one was open for 5% of the time, Pallas kernels for 0%

commit v1 on v0

v1 whole, which is shorter than its diff:
```python
import functools
import math

import jax
import jax.numpy as jnp
import numpy as np
from jax import lax
from jax.experimental import pallas as pl
from jax.experimental.pallas import tpu as pltpu
from jax.sharding import PartitionSpec as P

VIS_DEV = 352
AXES = ("dp", "patch")
F32, BF16 = jnp.float32, jnp.bfloat16
VMEM = pl.BlockSpec(memory_space=pltpu.VMEM)
SMEM = pl.BlockSpec(memory_space=pltpu.SMEM)
LIMIT = 56 * 1024 * 1024


def gelu_slope(pre_act):
    normal_cdf = 0.5 * (1.0 + lax.erf(pre_act * (1.0 / math.sqrt(2.0))))
    density = jnp.exp(-0.5 * pre_act * pre_act) * (1.0 / math.sqrt(2.0 * math.pi))
    return normal_cdf + pre_act * density


def standardise(block):
    as_float = block.astype(F32)
    mean_row = jnp.mean(as_float, axis=1, keepdims=True)
    centred = as_float - mean_row
    variance = jnp.mean(centred * centred, axis=1, keepdims=True)
    inverse = lax.rsqrt(variance + 1e-05)
    return centred * inverse, inverse


def norm_kernel(rows_ref, gamma_ref, beta_ref, out_ref):
    standard, _ = standardise(rows_ref[...])
    out_ref[...] = (standard * gamma_ref[...] + beta_ref[...]).astype(BF16)


def chunk_kernel(places, pieces, table_ref, counts_ref, n_ref, g_ref, b_ref, *refs):
    piece_refs, (keep_ref, send_ref, h_ref, w_ref), (sum_ref,) = refs[:pieces], refs[pieces : pieces + 4], refs[pieces + 4 :]
    for at, piece in enumerate(piece_refs):
        start = pl.multiple_of(table_ref[places["pieces"] + at], 16)
        w_ref[pl.ds(start, piece.shape[0]), :] = piece[...]
    per_dev, units = h_ref.shape
    count = counts_ref[0, table_ref[places["patch"]]]
    live = lax.broadcasted_iota(jnp.int32, (per_dev, 1), 0) < count
    for low in range(0, units, 256):
        cols = slice(low, min(low + 256, units))
        pre_act = lax.dot_general(n_ref[...], w_ref[cols, :], (((1,), (1,)), ((), ())), preferred_element_type=F32)
        slope = gelu_slope(pre_act + b_ref[:, cols].astype(F32))
        hidden = jnp.where(live, g_ref[:, cols].astype(F32) * slope, 0.0)
        h_ref[:, cols] = hidden.astype(BF16)
    width = n_ref.shape[1]
    block = keep_ref.shape[0] // 4
    for low in range(0, width, 256):
        cols = slice(low, min(low + 256, width))
        sum_ref[:, cols] = lax.dot_general(
            h_ref[...], n_ref[:, cols], (((0,), (0,)), ((), ())), preferred_element_type=F32
        )
    for at in range(8):
        start = pl.multiple_of(table_ref[places["blocks"] + at], 16)
        out = send_ref if at < 4 else keep_ref
        out[(at % 4) * block : (at % 4 + 1) * block, :] = sum_ref[pl.ds(start, block), :].astype(BF16)


def rows_kernel(places, chunks, table_ref, counts_ref, rows_ref, gamma_ref, *refs):
    h_refs, w_refs, out_ref = refs[:chunks], refs[chunks : 2 * chunks], refs[-1]
    tile = rows_ref.shape[0]
    normed_grad = jnp.dot(h_refs[0][...], w_refs[0][...], preferred_element_type=F32)
    for h, w in zip(h_refs[1:], w_refs[1:]):
        normed_grad += jnp.dot(h[...], w[...], preferred_element_type=F32)
    standard, inverse = standardise(rows_ref[...])
    scaled = normed_grad * gamma_ref[...]
    first = jnp.mean(scaled, axis=1, keepdims=True)
    second = jnp.mean(scaled * standard, axis=1, keepdims=True)
    grad = inverse * (scaled - first - standard * second)
    count = counts_ref[0, table_ref[places["patch"]]]
    row = lax.broadcasted_iota(jnp.int32, (tile, 1), 0) + pl.program_id(0) * tile
    out_ref[...] = jnp.where(row < count, grad, 0.0).astype(BF16)


def place_kernel(places, table_ref, *refs):
    quarter = refs[0].shape[0]
    for at, piece in enumerate(refs[:-1]):
        start = pl.multiple_of(table_ref[places["final"] + at], 16)
        refs[-1][pl.ds(start, quarter), :] = piece[...].astype(F32)


class Plan:
    def __init__(self, n_dp, n_patch, shard):
        self.nz, self.ny, self.nx = n_patch // 2, 2, 2
        self.n_patch, self.shard, self.quarter = n_patch, shard, shard // 4
        self.everyone = [
            (x, c, z, y) for x in range(2) for c in range(2) for z in range(self.nz) for y in range(2)
        ]

    def lin(self, x, c, z, y):
        return ((x * 2 + c) * self.nz + z) * 2 + y

    def perm(self, to):
        return [(self.lin(*d), self.lin(*to(*d))) for d in self.everyone]

    def across(self, x, c, z, y, flip_x, flip_y):
        return (x ^ flip_x, c, z, y ^ flip_y)

    def first(self, x, c, z, y):
        return (1 - x, c, z, y) if c == 0 else (x, c, z, 1 - y)

    def second(self, x, c, z, y):
        return (1 - x, c, z, y) if c == 1 else (x, c, z, 1 - y)

    def row(self, x, c, z, y):
        return y * self.shard + (x * 2 + c) * self.quarter

    def table(self):
        rows = []
        for d in self.everyone:
            x, c, z, y = d
            twin = (x, 1 - c, z, y)
            four = lambda e: [e, self.first(*e), self.second(*e), self.second(*self.first(*e))]
            order = lambda e: [four(e)[i] for i in (3, 1, 2, 0)]
            entry = [z * 2 + y]
            entry += [(z - s) % self.nz for s in range(self.nz)]
            entry += [self.row(*e) for e in four(d) + four(twin)]
            entry += [y * self.shard] + [
                self.row(qx, qc, z, 1 - y) for qx, qc in ((x, c), (1 - x, c), (x, 1 - c), (1 - x, 1 - c))
            ]
            entry += [self.row(*e) for e in order(twin) + order(d)]
            entry += [
                self.row(qx, qc, z, 0) for qx, qc in ((x, c), (1 - x, c), (x, 1 - c), (1 - x, 1 - c))
            ]
            rows.append(entry)
        return np.array(rows, np.int32)

    def places(self):
        base = 1 + self.nz
        return {"patch": 0, "chunk": 1, "far": base, "near": base + 8, "blocks": base + 13, "final": base + 21}


def call_chunk(places, step, table, counts, normed_rows, grad_hidden, bias, pieces, shard, near):
    per_dev, width = normed_rows.shape
    units = 2 * shard
    where = dict(places, pieces=places["near" if near else "far"])
    whole = lambda shape: pl.BlockSpec(shape, lambda i, t, c: (0,) * len(shape))
    return pl.pallas_call(
        functools.partial(chunk_kernel, where, len(pieces)),
        grid_spec=pltpu.PrefetchScalarGridSpec(
            num_scalar_prefetch=2,
            grid=(1,),
            in_specs=[
                whole((per_dev, width)),
                pl.BlockSpec((per_dev, units), lambda i, t, c: (0, t[places["chunk"] + step])),
                whole((1, units)),
            ]
            + [whole(p.shape) for p in pieces],
            out_specs=[
                whole((units // 2, width)),
                whole((units // 2, width)),
                whole((per_dev, units)),
                whole((units, width)),
            ],
            scratch_shapes=[pltpu.VMEM((units, width), F32)],
        ),
        out_shape=[
            jax.ShapeDtypeStruct((units // 2, width), BF16),
            jax.ShapeDtypeStruct((units // 2, width), BF16),
            jax.ShapeDtypeStruct((per_dev, units), BF16),
            jax.ShapeDtypeStruct((units, width), BF16),
        ],
        compiler_params=pltpu.CompilerParams(vmem_limit_bytes=LIMIT),
        cost_estimate=pl.CostEstimate(
            flops=4 * per_dev * units * width,
            bytes_accessed=2 * per_dev * (width + 2 * units) + 6 * units * width,
            transcendentals=per_dev * units,
        ),
        name="chunk_%d" % step,
    )(table, counts, normed_rows, grad_hidden, bias, *pieces)


def fast_device(plan, rows, grad_hidden, counts, w_in, b_in, gamma, beta):
    per_dev, width = rows.shape
    shard, quarter = plan.shard, plan.quarter
    n_patch = plan.n_patch
    dp_index, patch_index = lax.axis_index("dp"), lax.axis_index("patch")
    places = plan.places()
    table = lax.dynamic_index_in_dim(
        jnp.asarray(plan.table()), dp_index * n_patch + patch_index, 0, keepdims=False
    )
    gamma, beta = gamma.reshape(1, width), beta.reshape(1, width)
    swap = lambda to: functools.partial(lax.ppermute, axis_name=AXES, perm=plan.perm(to))
    core = swap(lambda x, c, z, y: (x, 1 - c, z, y))
    along_x = swap(lambda x, c, z, y: (1 - x, c, z, y))
    along_y = swap(lambda x, c, z, y: (x, c, z, 1 - y))
    first, second = swap(plan.first), swap(plan.second)
    up = lambda s: swap(lambda x, c, z, y: (x, c, (z + s) % plan.nz, y))

    mine = lax.dynamic_slice_in_dim(w_in, dp_index * quarter, quarter, 0)
    from_z = [None] + [up(s)(mine) for s in range(1, plan.nz)]
    beside = along_y(mine)
    diagonal = along_x(beside)
    pieces = [[w_in, beside, diagonal, core(beside), core(diagonal)]]
    bias_mine = b_in.reshape(1, shard)
    bias_other = along_y(bias_mine)
    low = patch_index % 2 == 0
    bias_here = jnp.concatenate(
        [jnp.where(low, bias_mine, bias_other), jnp.where(low, bias_other, bias_mine)], axis=1
    )
    bias = [bias_here] + [up(s)(bias_here) for s in range(1, plan.nz)]
    for s in range(1, plan.nz):
        a0 = from_z[s]
        a1 = first(a0)
        a2, a3 = second(a0), second(a1)
        pieces.append([a0, a1, a2, a3] + [core(a) for a in (a0, a1, a2, a3)])

    tile = per_dev // 4
    normed_rows = pl.pallas_call(
        norm_kernel,
        grid=(per_dev // tile,),
        in_specs=[
            pl.BlockSpec((tile, width), lambda i: (i, 0)),
            pl.BlockSpec((1, width), lambda i: (0, 0)),
            pl.BlockSpec((1, width), lambda i: (0, 0)),
        ],
        out_specs=pl.BlockSpec((tile, width), lambda i: (i, 0)),
        out_shape=jax.ShapeDtypeStruct((per_dev, width), BF16),
        compiler_params=pltpu.CompilerParams(vmem_limit_bytes=LIMIT),
        name="norm",
    )(rows, gamma, beta)

    hidden, weights, total = [], [], None
    scale = 1.0 / math.sqrt(VIS_DEV * n_patch * 4)
    for s in range(plan.nz):
        keep, send, h, w = call_chunk(
            places, s, table, counts, normed_rows, grad_hidden, bias[s], pieces[s], shard, s == 0
        )
        hidden.append(h)
        weights.append(w)
        own = lambda low, high: keep[low:high].astype(F32) + got[low:high].astype(F32)
        got = core(send)
        one = first(own(0, 2 * quarter).astype(BF16))
        two = second((own(2 * quarter, 3 * quarter) + one[:quarter].astype(F32)).astype(BF16))
        plane = own(3 * quarter, 4 * quarter) + one[quarter:].astype(F32) + two.astype(F32)
        if s:
            plane = up(-s)(plane.astype(BF16)).astype(F32)
        total = plane if total is None else total + plane
    done = (total * scale).astype(BF16)
    done_x = along_x(done)
    quarters = [done, done_x, core(done), core(done_x)]
    grad_w_in = pl.pallas_call(
        functools.partial(place_kernel, places),
        in_specs=[SMEM] + [VMEM] * 4,
        out_specs=VMEM,
        out_shape=jax.ShapeDtypeStruct((shard, width), F32),
        name="place",
    )(table, *quarters)

    whole = lambda shape: pl.BlockSpec(shape, lambda i, t, c: (0,) * len(shape))
    striped = lambda cols: pl.BlockSpec((tile, cols), lambda i, t, c: (i, 0))
    grad_rows = pl.pallas_call(
        functools.partial(rows_kernel, places, plan.nz),
        grid_spec=pltpu.PrefetchScalarGridSpec(
            num_scalar_prefetch=2,
            grid=(per_dev // tile,),
            in_specs=[striped(width), whole((1, width))]
            + [striped(h.shape[1]) for h in hidden]
            + [whole(w.shape) for w in weights],
            out_specs=striped(width),
        ),
        out_shape=jax.ShapeDtypeStruct((per_dev, width), BF16),
        compiler_params=pltpu.CompilerParams(vmem_limit_bytes=LIMIT),
        cost_estimate=pl.CostEstimate(
            flops=2 * per_dev * width * 2 * shard * plan.nz,
            bytes_accessed=4 * per_dev * width + 2 * (per_dev + width) * 2 * shard * plan.nz,
            transcendentals=0,
        ),
        name="grad_rows",
    )(table, counts, rows, gamma, *hidden, *weights)
    return grad_rows, grad_w_in


def any_device(rows, grad_hidden, counts, w_in, b_in, gamma, beta):
    patch_count, data_count = lax.axis_size("patch"), lax.axis_size("dp")
    live = (jnp.arange(rows.shape[0], dtype=jnp.int32) < jnp.take(counts[0], lax.axis_index("patch")))[:, None]
    standard, inverse = standardise(rows)
    normed_rows = (standard * gamma + beta).astype(BF16)
    w_all = lax.all_gather(w_in, "patch", axis=0, tiled=True)
    b_all = lax.all_gather(b_in, "patch", axis=0, tiled=True)
    pre_act = lax.dot_general(normed_rows, w_all, (((1,), (1,)), ((), ())), preferred_element_type=F32)
    slope = gelu_slope(pre_act + b_all.astype(F32))
    hidden = jnp.where(live, grad_hidden.astype(F32) * slope, 0.0).astype(BF16)
    scaled = jnp.dot(hidden, w_all, preferred_element_type=F32) * gamma
    first = jnp.mean(scaled, axis=1, keepdims=True)
    second = jnp.mean(scaled * standard, axis=1, keepdims=True)
    grad = inverse * (scaled - first - standard * second)
    grad_rows = jnp.where(live, grad, 0.0).astype(BF16)
    term = lax.dot_general(hidden, normed_rows, (((0,), (0,)), ((), ())), preferred_element_type=F32)
    scale = 1.0 / math.sqrt(VIS_DEV * patch_count * data_count)
    part = lax.psum_scatter(term * scale, "patch", scatter_dimension=0, tiled=True)
    return grad_rows, lax.psum(part, "dp")


def solution(mesh):
    n_dp, n_patch = mesh.shape["dp"], mesh.shape["patch"]

    def per_device(*args):
        shard = args[3].shape[0]
        if n_dp == 4 and n_patch % 2 == 0 and n_patch <= 8 and shard % 64 == 0 and args[0].shape[0] % 64 == 0:
            return fast_device(Plan(n_dp, n_patch, shard), *args)
        return any_device(*args)

    in_specs = (
        P(AXES, None), P(AXES, None), P("dp", None), P("patch", None), P("patch"), P(), P(),
    )
    return jax.shard_map(
        per_device, mesh=mesh, in_specs=in_specs, out_specs=(P(AXES, None), P("patch", None)), check_vma=False
    )
```

time: 406 us -> 169 us (0.42)
  waiting for transfers between devices: 321 us -> 55.7 us
  Pallas kernels: 0 us -> 55 us
  starting transfers between devices: 0.3 us -> 41.7 us
  matrix products: 31 us -> 0 us
  blocking collectives: 23.9 us -> 0 us
  between operations: 15.2 us -> 1.15 us
  other arithmetic: 6.15 us -> 2.02 us
    reduce_scatter x1 -> x0, waiting for transfers between devices: 202 us -> none  [per_device(): lax.psum_scatter(grad_scale * lax.dot_general(hidden_grad, normed_rows, (...]
    all_gather x1 -> x0, waiting for transfers between devices: 77 us -> none  [per_device(): w_piece = lax.all_gather(w_in, 'patch', axis=0, tiled=True)]
    ppermute x0 -> x50, waiting for transfers between devices: none -> 55.7 us  [the longest x4 21.2 us: fast_device(): one = first(own(0, 2 * quarter).astype(BF16))]
    pallas_call x0 -> x7, Pallas kernels: none -> 55 us  [the longest x4 35.5 us: call_chunk(): pl.pallas_call(functools.partial(chunk_kernel, where, len(pieces)), grid_...]
    ppermute x0 -> x50, starting transfers between devices: none -> 41.7 us  [the longest x6 8.05 us: fast_device(): a2, a3 = (second(a0), second(a1))]
    psum x1 -> x0, waiting for transfers between devices: 41.7 us -> none  [per_device(): grad_w_in = lax.psum(partial_value, 'dp')]
    dot_general x3 -> x0, matrix products: 31 us -> none  [the longest x1 11.4 us: per_device(): lax.dot_general(normed_rows, w_piece, (((1,), (1,)), ((), ())), preferred...]
    unnamed x1 -> x0, blocking collectives: 23.9 us -> none
  transfers between devices with their start and end apart: 3 -> 50, of which waited for: 3 -> 14; matrix products, arithmetic and copies ran while one was open for 5% -> 4% of each run, Pallas kernels for 0% -> 32%
where the time goes in v1:
time: 169 us; the launch traced here: 165 us
  waiting for transfers between devices  55.7 us (33%)
  Pallas kernels  55 us (33%)
  starting transfers between devices  41.7 us (25%)
  local copies, waits for them, and re-layouts  9.91 us (6%)
  other arithmetic  2.02 us (1%)
    pallas_call x4, Pallas kernels, call_chunk(): pl.pallas_call(functools.partial(chunk_kernel, where, len(pieces)), grid_...  35.5 us
    ppermute x4, waiting for transfers between devices, fast_device(): one = first(own(0, 2 * quarter).astype(BF16))  21.2 us
    pallas_call x1, Pallas kernels, fast_device(): pl.pallas_call(functools.partial(rows_kernel, places, plan.nz), grid_spec...  12.7 us
    ppermute x3, waiting for transfers between devices, fast_device(): plane = up(-s)(plane.astype(BF16)).astype(F32)  9.54 us
    ppermute x3, waiting for transfers between devices, fast_device(): bias = [bias_here] + [up(s)(bias_here) for s in range(1, plan.nz)]  8.89 us
    ppermute x6, starting transfers between devices, fast_device(): a2, a3 = (second(a0), second(a1))  8.05 us
    ppermute x3, starting transfers between devices, fast_device(): from_z = [None] + [up(s)(mine) for s in range(1, plan.nz)]  7.03 us
    ppermute x3, starting transfers between devices, fast_device(): a1 = first(a0)  6.62 us
  transfers between devices with their start and end apart: 50, of which 14 were waited for; matrix products, arithmetic and copies ran while one was open for 4% of the time, Pallas kernels for 32%

profile of v1, /device:TPU:0, one launch (start us, length us, event | category | flops | bytes accessed | tf_op | source)
XLA Modules:
  0.0 165.5 jit_solution(14994073137757222262)
XLA Ops:
  0.6 0.7 reshape.15
  1.3 3.0 %collective-permute-start = (bf16[1,320]{1,0:T(2,128)(2,1)S(1)}, bf16[1,320]{1,0:T(2,128)(2,1)S(1)}, u32[]{:S(2)}, u32[]{:S(2)}) collective-permute-start(bf16[1,320]{1,0:T(2,128)(2,1)S(1)} %reshape.15), channel_id=1, source_target_pairs={{0,1},{1,0},{2,3},{3,2},{4,5},{5,4},{6,7},{7,6},{8,9},{9,8},{10,11... | collective-permute-start | bytes 1928 | tf_op jit(solution)/shard_map/ppermute | solution.py:204
  4.3 0.9 constant_dynamic-slice_fusion
  5.2 3.7 %collective-permute-start.24 = (bf16[80,1280]{1,0:T(8,128)(2,1)S(1)}, bf16[80,1280]{1,0:T(8,128)(2,1)S(1)}, u32[]{:S(2)}, u32[]{:S(2)}) collective-permute-start(bf16[80,1280]{1,0:T(8,128)(2,1)S(1)} %constant_dynamic-slice_fusion), channel_id=1, source_target_pairs={{0,6},{1,7},{2,0},{3,1},{4,2},{5,3},{6,4},{7,5},{8,14},{9,15},{10,... | collective-permute-start | bytes 614408 | tf_op jit(solution)/shard_map/ppermute | solution.py:199
  8.9 0.7 broadcast_select_fusion.1
  9.7 1.1 collective-permute-start.23
  10.7 1.0 collective-permute-start.5
  11.7 2.9 %collective-permute-start.15 = (bf16[80,1280]{1,0:T(8,128)(2,1)S(1)}, bf16[80,1280]{1,0:T(8,128)(2,1)S(1)}, u32[]{:S(2)}, u32[]{:S(2)}) collective-permute-start(bf16[80,1280]{1,0:T(8,128)(2,1)S(1)} %constant_dynamic-slice_fusion), channel_id=1, source_target_pairs={{0,4},{1,5},{2,6},{3,7},{4,0},{5,1},{6,2},{7,3},{8,12},{9,13},{10,... | collective-permute-start | bytes 614408 | tf_op jit(solution)/shard_map/ppermute | solution.py:199
  14.6 0.5 collective-permute-start.6
  15.1 8.9 %collective-permute-done.14.b_ref = bf16[1,640]{1,0:T(2,128)(2,1)S(1)} collective-permute-done((bf16[1,640]{1,0:T(2,128)(2,1)S(1)}, bf16[1,640]{1,0:T(2,128)(2,1)S(1)}, u32[]{:S(2)}, u32[]{:S(2)}) %collective-permute-start.14) | collective-permute-done | bytes 1312 | tf_op jit(solution)/shard_map/ppermute | solution.py:209
  24.0 1.4 collective-permute-start.1
  25.5 0.7 collective-permute-start.26
  26.1 1.0 collective-permute-done.15.refs_0_
  27.1 1.5 collective-permute-start.25
  28.6 1.1 collective-permute-done.1.refs_1_
  29.8 2.2 %collective-permute-start.17 = (bf16[80,1280]{1,0:T(8,128)(2,1)S(1)}, bf16[80,1280]{1,0:T(8,128)(2,1)S(1)}, u32[]{:S(2)}, u32[]{:S(2)}) collective-permute-start(bf16[80,1280]{1,0:T(8,128)(2,1)S(1)} %collective-permute-done.15.refs_0_), channel_id=1, source_target_pairs={{0,1},{1,0},{2,3},{3,2},{4,5},{5,4},{6,7},{7,6},{8,24},{9,25},{10,... | collective-permute-start | bytes 614408 | tf_op jit(solution)/shard_map/ppermute | solution.py:213
  32.0 2.6 %collective-permute-start.16 = (bf16[80,1280]{1,0:T(8,128)(2,1)S(1)}, bf16[80,1280]{1,0:T(8,128)(2,1)S(1)}, u32[]{:S(2)}, u32[]{:S(2)}) collective-permute-start(bf16[80,1280]{1,0:T(8,128)(2,1)S(1)} %collective-permute-done.15.refs_0_), channel_id=1, source_target_pairs={{0,16},{1,17},{2,18},{3,19},{4,20},{5,21},{6,22},{7,23},{8,9},{9,8... | collective-permute-start | bytes 614408 | tf_op jit(solution)/shard_map/ppermute | solution.py:212
  34.5 2.0 %collective-permute-start.2 = (bf16[80,1280]{1,0:T(8,128)(2,1)S(1)}, bf16[80,1280]{1,0:T(8,128)(2,1)S(1)}, u32[]{:S(2)}, u32[]{:S(2)}) collective-permute-start(bf16[80,1280]{1,0:T(8,128)(2,1)S(1)} %collective-permute-done.1.refs_1_), channel_id=1, source_target_pairs={{0,16},{1,17},{2,18},{3,19},{4,20},{5,21},{6,22},{7,23},{8,24},{9,... | collective-permute-start | bytes 614408 | tf_op jit(solution)/shard_map/ppermute | solution.py:201
  36.6 2.4 %collective-permute-start.8 = (bf16[80,1280]{1,0:T(8,128)(2,1)S(1)}, bf16[80,1280]{1,0:T(8,128)(2,1)S(1)}, u32[]{:S(2)}, u32[]{:S(2)}) collective-permute-start(bf16[80,1280]{1,0:T(8,128)(2,1)S(1)} %collective-permute-done.6.refs_0_), channel_id=1, source_target_pairs={{0,1},{1,0},{2,3},{3,2},{4,5},{5,4},{6,7},{7,6},{8,24},{9,25},{10,... | collective-permute-start | bytes 614408 | tf_op jit(solution)/shard_map/ppermute | solution.py:213
  39.0 0.5 collective-permute-done.16.refs_1_
  39.5 0.7 collective-permute-start.27
  40.2 3.7 %collective-permute-done.2.refs_2_ = bf16[80,1280]{1,0:T(8,128)(2,1)S(1)} collective-permute-done((bf16[80,1280]{1,0:T(8,128)(2,1)S(1)}, bf16[80,1280]{1,0:T(8,128)(2,1)S(1)}, u32[]{:S(2)}, u32[]{:S(2)}) %collective-permute-start.2) | collective-permute-done | bytes 204832 | tf_op jit(solution)/shard_map/ppermute | solution.py:201
  43.9 1.3 reshape.13.gamma_ref
  45.2 1.3 reshape.14.beta_ref
  46.5 4.3 %norm.1.n_ref = bf16[704,1280]{1,0:T(8,128)(2,1)} custom-call(bf16[704,1280]{1,0:T(8,128)(2,1)} %rows_ref.3, f32[1,1280]{1,0:T(1,128)} %reshape.13.gamma_ref, f32[1,1280]{1,0:T(1,128)} %reshape.14.beta_ref), custom_call_target="tpu_custom_call" | custom-call | tf_op jit(solution)/shard_map/norm/pallas_call | solution.py:217
  50.9 1.2 dynamic-slice_bitcast_fusion.table_ref
  52.1 2.5 %collective-permute-start.7 = (bf16[80,1280]{1,0:T(8,128)(2,1)S(1)}, bf16[80,1280]{1,0:T(8,128)(2,1)S(1)}, u32[]{:S(2)}, u32[]{:S(2)}) collective-permute-start(bf16[80,1280]{1,0:T(8,128)(2,1)S(1)} %collective-permute-done.6.refs_0_), channel_id=1, source_target_pairs={{0,16},{1,17},{2,18},{3,19},{4,20},{5,21},{6,22},{7,23},{8,9},{9,8... | collective-permute-start | bytes 614408 | tf_op jit(solution)/shard_map/ppermute | solution.py:212
  54.8 0.5 collective-permute-start.30
  55.3 0.5 collective-permute-start.18
  55.9 0.7 copy-done.31
  56.5 8.8 %chunk_0.1 = (bf16[320,1280]{1,0:T(8,128)(2,1)}, bf16[320,1280]{1,0:T(8,128)(2,1)}, bf16[704,640]{1,0:T(8,128)(2,1)}, bf16[640,1280]{1,0:T(8,128)(2,1)}) custom-call(s32[30]{0:T(128)} %dynamic-slice_bitcast_fusion.table_ref, s32[1,8]{1,0:T(1,128)} %counts_ref.9, bf16[704,1280]{1,0:T(8,128)(2,1)} %norm.1.n_ref, bf16[704,2560]{1,0:T(8,128)(2,1)} %g_ref.7, ...), custom_call_target="tpu_custom_call" | custom-call | flops 2306867200 | bytes 8519680 | tf_op jit(solution)/shard_map/chunk_0/pallas_call | solution.py:146
  65.4 0.5 collective-permute-start.20
  66.1 1.6 collective-permute-start.9
  67.7 0.7 copy-done.33
  68.4 8.8 %chunk_3.1 = (bf16[320,1280]{1,0:T(8,128)(2,1)}, bf16[320,1280]{1,0:T(8,128)(2,1)}, bf16[704,640]{1,0:T(8,128)(2,1)}, bf16[640,1280]{1,0:T(8,128)(2,1)}) custom-call(s32[30]{0:T(128)} %dynamic-slice_bitcast_fusion.table_ref, s32[1,8]{1,0:T(1,128)} %counts_ref.9, bf16[704,1280]{1,0:T(8,128)(2,1)} %norm.1.n_ref, bf16[704,2560]{1,0:T(8,128)(2,1)} %g_ref.7, ...), custom_call_target="tpu_custom_call" | custom-call | flops 2306867200 | bytes 8519680 | tf_op jit(solution)/shard_map/chunk_3/pallas_call | solution.py:146
  77.3 0.5 collective-permute-start.12
  78.0 0.4 collective-permute-start.43
  78.4 0.3 copy-done.34
  78.7 8.9 %chunk_2.1 = (bf16[320,1280]{1,0:T(8,128)(2,1)}, bf16[320,1280]{1,0:T(8,128)(2,1)}, bf16[704,640]{1,0:T(8,128)(2,1)}, bf16[640,1280]{1,0:T(8,128)(2,1)}) custom-call(s32[30]{0:T(128)} %dynamic-slice_bitcast_fusion.table_ref, s32[1,8]{1,0:T(1,128)} %counts_ref.9, bf16[704,1280]{1,0:T(8,128)(2,1)} %norm.1.n_ref, bf16[704,2560]{1,0:T(8,128)(2,1)} %g_ref.7, ...), custom_call_target="tpu_custom_call" | custom-call | flops 2306867200 | bytes 8519680 | tf_op jit(solution)/shard_map/chunk_2/pallas_call | solution.py:146
  87.6 0.5 collective-permute-start.39
  88.3 0.5 copy-done.32
  88.8 0.7 copy-done.36
  89.5 9.1 %chunk_1.1 = (bf16[320,1280]{1,0:T(8,128)(2,1)}, bf16[320,1280]{1,0:T(8,128)(2,1)}, bf16[704,640]{1,0:T(8,128)(2,1)}, bf16[640,1280]{1,0:T(8,128)(2,1)}) custom-call(s32[30]{0:T(128)} %dynamic-slice_bitcast_fusion.table_ref, s32[1,8]{1,0:T(1,128)} %counts_ref.9, bf16[704,1280]{1,0:T(8,128)(2,1)} %norm.1.n_ref, bf16[704,2560]{1,0:T(8,128)(2,1)} %g_ref.7, ...), custom_call_target="tpu_custom_call" | custom-call | flops 2306867200 | bytes 8519680 | tf_op jit(solution)/shard_map/chunk_1/pallas_call | solution.py:146
  98.8 0.6 collective-permute-start.33
  99.5 1.5 collective-permute-start.44
  101.2 0.6 collective-permute-start.40
  101.9 1.5 collective-permute-start.36
  103.4 3.4 %collective-permute-done.33 = bf16[160,1280]{1,0:T(8,128)(2,1)S(1)} collective-permute-done((bf16[160,1280]{1,0:T(8,128)(2,1)S(1)}, bf16[160,1280]{1,0:T(8,128)(2,1)S(1)}, u32[]{:S(2)}, u32[]{:S(2)}) %collective-permute-start.33) | collective-permute-done | bytes 409632 | tf_op jit(solution)/shard_map/ppermute | solution.py:241
  106.9 0.6 collective-permute-start.34
  107.5 5.8 %collective-permute-done.44 = bf16[160,1280]{1,0:T(8,128)(2,1)S(1)} collective-permute-done((bf16[160,1280]{1,0:T(8,128)(2,1)S(1)}, bf16[160,1280]{1,0:T(8,128)(2,1)S(1)}, u32[]{:S(2)}, u32[]{:S(2)}) %collective-permute-start.44) | collective-permute-done | bytes 409632 | tf_op jit(solution)/shard_map/ppermute | solution.py:241
  113.3 0.6 collective-permute-start.45
  113.8 6.1 %collective-permute-done.40 = bf16[160,1280]{1,0:T(8,128)(2,1)S(1)} collective-permute-done((bf16[160,1280]{1,0:T(8,128)(2,1)S(1)}, bf16[160,1280]{1,0:T(8,128)(2,1)S(1)}, u32[]{:S(2)}, u32[]{:S(2)}) %collective-permute-start.40) | collective-permute-done | bytes 409632 | tf_op jit(solution)/shard_map/ppermute | solution.py:241
  120.1 0.6 collective-permute-start.41
  120.6 5.9 %collective-permute-done.36 = bf16[160,1280]{1,0:T(8,128)(2,1)S(1)} collective-permute-done((bf16[160,1280]{1,0:T(8,128)(2,1)S(1)}, bf16[160,1280]{1,0:T(8,128)(2,1)S(1)}, u32[]{:S(2)}, u32[]{:S(2)}) %collective-permute-start.36) | collective-permute-done | bytes 409632 | tf_op jit(solution)/shard_map/ppermute | solution.py:241
  126.6 0.6 collective-permute-start.37
  127.6 4.9 %collective-permute-done.37 = bf16[80,1280]{1,0:T(8,128)(2,1)S(1)} collective-permute-done((bf16[80,1280]{1,0:T(8,128)(2,1)S(1)}, bf16[80,1280]{1,0:T(8,128)(2,1)S(1)}, u32[]{:S(2)}, u32[]{:S(2)}) %collective-permute-start.37) | collective-permute-done | bytes 204832 | tf_op jit(solution)/shard_map/ppermute | solution.py:242
  132.7 4.6 %collective-permute-done.46 = bf16[80,1280]{1,0:T(8,128)(2,1)S(1)} collective-permute-done((bf16[80,1280]{1,0:T(8,128)(2,1)S(1)}, bf16[80,1280]{1,0:T(8,128)(2,1)S(1)}, u32[]{:S(2)}, u32[]{:S(2)}) %collective-permute-start.46) | collective-permute-done | bytes 204832 | tf_op jit(solution)/shard_map/ppermute | solution.py:245
  137.3 4.8 %collective-permute-done.42 = bf16[80,1280]{1,0:T(8,128)(2,1)S(1)} collective-permute-done((bf16[80,1280]{1,0:T(8,128)(2,1)S(1)}, bf16[80,1280]{1,0:T(8,128)(2,1)S(1)}, u32[]{:S(2)}, u32[]{:S(2)}) %collective-permute-start.42) | collective-permute-done | bytes 204832 | tf_op jit(solution)/shard_map/ppermute | solution.py:245
  142.4 1.7 %collective-permute-start.47 = (bf16[80,1280]{1,0:T(8,128)(2,1)S(1)}, bf16[80,1280]{1,0:T(8,128)(2,1)S(1)}, u32[]{:S(2)}, u32[]{:S(2)}) collective-permute-start(bf16[80,1280]{1,0:T(8,128)(2,1)S(1)} %multiply_convert_fusion.refs_0_), channel_id=1, source_target_pairs={{0,16},{1,17},{2,18},{3,19},{4,20},{5,21},{6,22},{7,23},{8,24},{9,... | collective-permute-start | bytes 614408 | tf_op jit(solution)/shard_map/ppermute | solution.py:248
  144.1 4.8 %collective-permute-done.47.refs_1_ = bf16[80,1280]{1,0:T(8,128)(2,1)S(1)} collective-permute-done((bf16[80,1280]{1,0:T(8,128)(2,1)S(1)}, bf16[80,1280]{1,0:T(8,128)(2,1)S(1)}, u32[]{:S(2)}, u32[]{:S(2)}) %collective-permute-start.47) | collective-permute-done | bytes 204832 | tf_op jit(solution)/shard_map/ppermute | solution.py:248
  148.9 12.7 %grad_rows.1 = bf16[704,1280]{1,0:T(8,128)(2,1)} custom-call(s32[30]{0:T(128)} %dynamic-slice_bitcast_fusion.table_ref, s32[1,8]{1,0:T(1,128)} %counts_ref.9, bf16[704,1280]{1,0:T(8,128)(2,1)} %rows_ref.3, f32[1,1280]{1,0:T(1,128)} %reshape.13.gamma_ref, bf16[704,640]{1,0:T(8,128)(2,1)} %get-tuple-element.18.refs_0_, ...), custom_call_target="tpu_custom_call" | custom-call | flops 4613734400 | bytes 13762560 | tf_op jit(solution)/shard_map/grad_rows/pallas_call | solution.py:260
  161.6 0.7 copy-done.6
  162.3 0.7 copy-done.7
  163.0 2.5 %place.1 = f32[320,1280]{1,0:T(8,128)} custom-call(s32[30]{0:T(128)} %dynamic-slice_bitcast_fusion.table_ref, bf16[80,1280]{1,0:T(8,128)(2,1)} %copy-done.4, bf16[80,1280]{1,0:T(8,128)(2,1)} %copy-done.5, bf16[80,1280]{1,0:T(8,128)(2,1)} %copy-done.6, bf16[80,1280]{1,0:T(8,128)(2,1)} %copy-done.7), custom_call_target="tpu_custom_call" | custom-call | tf_op jit(solution)/shard_map/place/pallas_call | solution.py:250
  (142 shorter events, 2.6 us)
Async XLA Ops:
  1.3 7.6 %collective-permute-start = (bf16[1,320]{1,0:T(2,128)(2,1)S(1)}, bf16[1,320]{1,0:T(2,128)(2,1)S(1)}, u32[]{:S(2)}, u32[]{:S(2)}) collective-permute-start(bf16[1,320]{1,0:T(2,128)(2,1)S(1)} %reshape.15), channel_id=1, source_target_pairs={{0,1},{1,0},{2,3},{3,2},{4,5},{5,4},{6,7},{7,6},{8,9},{9,8},{10,11... | collective-permute-start | bytes 1928 | tf_op jit(solution)/shard_map/ppermute | solution.py:204
  5.2 20.2 %collective-permute-start.24 = (bf16[80,1280]{1,0:T(8,128)(2,1)S(1)}, bf16[80,1280]{1,0:T(8,128)(2,1)S(1)}, u32[]{:S(2)}, u32[]{:S(2)}) collective-permute-start(bf16[80,1280]{1,0:T(8,128)(2,1)S(1)} %constant_dynamic-slice_fusion), channel_id=1, source_target_pairs={{0,6},{1,7},{2,0},{3,1},{4,2},{5,3},{6,4},{7,5},{8,14},{9,15},{10,... | collective-permute-start | bytes 614408 | tf_op jit(solution)/shard_map/ppermute | solution.py:199
  9.7 41.2 %copy-start.8 = (bf16[1,640]{1,0:T(2,128)(2,1)}, bf16[1,640]{1,0:T(2,128)(2,1)S(1)}, u32[]{:S(2)}) copy-start(bf16[1,640]{1,0:T(2,128)(2,1)S(1)} %pad_maximum_fusion.b_ref) | copy-start | bytes 3844
  9.7 5.0 %collective-permute-start.23 = (bf16[1,640]{1,0:T(2,128)(2,1)S(1)}, bf16[1,640]{1,0:T(2,128)(2,1)S(1)}, u32[]{:S(2)}, u32[]{:S(2)}) collective-permute-start(bf16[1,640]{1,0:T(2,128)(2,1)S(1)} %pad_maximum_fusion.b_ref), channel_id=1, source_target_pairs={{0,6},{1,7},{2,0},{3,1},{4,2},{5,3},{6,4},{7,5},{8,14},{9,15},{10,... | collective-permute-start | bytes 3848 | tf_op jit(solution)/shard_map/ppermute | solution.py:209
  10.7 13.3 %collective-permute-start.14 = (bf16[1,640]{1,0:T(2,128)(2,1)S(1)}, bf16[1,640]{1,0:T(2,128)(2,1)S(1)}, u32[]{:S(2)}, u32[]{:S(2)}) collective-permute-start(bf16[1,640]{1,0:T(2,128)(2,1)S(1)} %pad_maximum_fusion.b_ref), channel_id=1, source_target_pairs={{0,4},{1,5},{2,6},{3,7},{4,0},{5,1},{6,2},{7,3},{8,12},{9,13},{10,... | collective-permute-start | bytes 3848 | tf_op jit(solution)/shard_map/ppermute | solution.py:209
  10.7 14.7 %collective-permute-start.5 = (bf16[1,640]{1,0:T(2,128)(2,1)S(1)}, bf16[1,640]{1,0:T(2,128)(2,1)S(1)}, u32[]{:S(2)}, u32[]{:S(2)}) collective-permute-start(bf16[1,640]{1,0:T(2,128)(2,1)S(1)} %pad_maximum_fusion.b_ref), channel_id=1, source_target_pairs={{0,2},{1,3},{2,4},{3,5},{4,6},{5,7},{6,0},{7,1},{8,10},{9,11},{10,... | collective-permute-start | bytes 3848 | tf_op jit(solution)/shard_map/ppermute | solution.py:209
  11.7 15.4 %collective-permute-start.15 = (bf16[80,1280]{1,0:T(8,128)(2,1)S(1)}, bf16[80,1280]{1,0:T(8,128)(2,1)S(1)}, u32[]{:S(2)}, u32[]{:S(2)}) collective-permute-start(bf16[80,1280]{1,0:T(8,128)(2,1)S(1)} %constant_dynamic-slice_fusion), channel_id=1, source_target_pairs={{0,4},{1,5},{2,6},{3,7},{4,0},{5,1},{6,2},{7,3},{8,12},{9,13},{10,... | collective-permute-start | bytes 614408 | tf_op jit(solution)/shard_map/ppermute | solution.py:199
  14.6 36.2 %copy-start.39 = (bf16[1,640]{1,0:T(2,128)(2,1)}, bf16[1,640]{1,0:T(2,128)(2,1)S(1)}, u32[]{:S(2)}) copy-start(bf16[1,640]{1,0:T(2,128)(2,1)S(1)} %collective-permute-done.23.b_ref) | copy-start | bytes 3844
  14.6 14.0 %collective-permute-start.6 = (bf16[80,1280]{1,0:T(8,128)(2,1)S(1)}, bf16[80,1280]{1,0:T(8,128)(2,1)S(1)}, u32[]{:S(2)}, u32[]{:S(2)}) collective-permute-start(bf16[80,1280]{1,0:T(8,128)(2,1)S(1)} %constant_dynamic-slice_fusion), channel_id=1, source_target_pairs={{0,2},{1,3},{2,4},{3,5},{4,6},{5,7},{6,0},{7,1},{8,10},{9,11},{10,... | collective-permute-start | bytes 614408 | tf_op jit(solution)/shard_map/ppermute | solution.py:199
  24.0 26.8 %copy-start.38 = (bf16[1,640]{1,0:T(2,128)(2,1)}, bf16[1,640]{1,0:T(2,128)(2,1)S(1)}, u32[]{:S(2)}) copy-start(bf16[1,640]{1,0:T(2,128)(2,1)S(1)} %collective-permute-done.14.b_ref) | copy-start | bytes 3844
  24.0 5.8 %collective-permute-start.1 = (bf16[80,1280]{1,0:T(8,128)(2,1)S(1)}, bf16[80,1280]{1,0:T(8,128)(2,1)S(1)}, u32[]{:S(2)}, u32[]{:S(2)}) collective-permute-start(bf16[80,1280]{1,0:T(8,128)(2,1)S(1)} %constant_dynamic-slice_fusion), channel_id=1, source_target_pairs={{0,1},{1,0},{2,3},{3,2},{4,5},{5,4},{6,7},{7,6},{8,9},{9,8},{10,11... | collective-permute-start | bytes 614408 | tf_op jit(solution)/shard_map/ppermute | solution.py:200
  25.4 25.4 %copy-start.10 = (bf16[80,1280]{1,0:T(8,128)(2,1)}, bf16[80,1280]{1,0:T(8,128)(2,1)S(1)}, u32[]{:S(2)}) copy-start(bf16[80,1280]{1,0:T(8,128)(2,1)S(1)} %collective-permute-done.24.refs_0_) | copy-start | bytes 614404
  25.4 6.5 %collective-permute-start.28 = (bf16[80,1280]{1,0:T(8,128)(2,1)S(1)}, bf16[80,1280]{1,0:T(8,128)(2,1)S(1)}, u32[]{:S(2)}, u32[]{:S(2)}) collective-permute-start(bf16[80,1280]{1,0:T(8,128)(2,1)S(1)} %collective-permute-done.24.refs_0_), channel_id=1, source_target_pairs={{0,8},{1,9},{2,10},{3,11},{4,12},{5,13},{6,14},{7,15},{8,0},{9,1},... | collective-permute-start | bytes 614408 | tf_op jit(solution)/shard_map/ppermute | solution.py:214
  25.4 25.4 %copy-start.37 = (bf16[1,640]{1,0:T(2,128)(2,1)}, bf16[1,640]{1,0:T(2,128)(2,1)S(1)}, u32[]{:S(2)}) copy-start(bf16[1,640]{1,0:T(2,128)(2,1)S(1)} %collective-permute-done.5.b_ref) | copy-start | bytes 3844
  25.5 9.1 %collective-permute-start.26 = (bf16[80,1280]{1,0:T(8,128)(2,1)S(1)}, bf16[80,1280]{1,0:T(8,128)(2,1)S(1)}, u32[]{:S(2)}, u32[]{:S(2)}) collective-permute-start(bf16[80,1280]{1,0:T(8,128)(2,1)S(1)} %collective-permute-done.24.refs_0_), channel_id=1, source_target_pairs={{0,1},{1,0},{2,3},{3,2},{4,5},{5,4},{6,7},{7,6},{8,24},{9,25},{10,... | collective-permute-start | bytes 614408 | tf_op jit(solution)/shard_map/ppermute | solution.py:213
  27.1 23.7 %copy-start.11 = (bf16[80,1280]{1,0:T(8,128)(2,1)}, bf16[80,1280]{1,0:T(8,128)(2,1)S(1)}, u32[]{:S(2)}) copy-start(bf16[80,1280]{1,0:T(8,128)(2,1)S(1)} %collective-permute-done.15.refs_0_) | copy-start | bytes 614404
  27.1 9.4 %collective-permute-start.25 = (bf16[80,1280]{1,0:T(8,128)(2,1)S(1)}, bf16[80,1280]{1,0:T(8,128)(2,1)S(1)}, u32[]{:S(2)}, u32[]{:S(2)}) collective-permute-start(bf16[80,1280]{1,0:T(8,128)(2,1)S(1)} %collective-permute-done.24.refs_0_), channel_id=1, source_target_pairs={{0,16},{1,17},{2,18},{3,19},{4,20},{5,21},{6,22},{7,23},{8,9},{9,8... | collective-permute-start | bytes 614408 | tf_op jit(solution)/shard_map/ppermute | solution.py:212
  28.6 23.5 %copy-start.9 = (bf16[80,1280]{1,0:T(8,128)(2,1)}, bf16[80,1280]{1,0:T(8,128)(2,1)S(1)}, u32[]{:S(2)}) copy-start(bf16[80,1280]{1,0:T(8,128)(2,1)S(1)} %collective-permute-done.6.refs_0_) | copy-start | bytes 614404
  28.6 7.9 %collective-permute-start.19 = (bf16[80,1280]{1,0:T(8,128)(2,1)S(1)}, bf16[80,1280]{1,0:T(8,128)(2,1)S(1)}, u32[]{:S(2)}, u32[]{:S(2)}) collective-permute-start(bf16[80,1280]{1,0:T(8,128)(2,1)S(1)} %collective-permute-done.15.refs_0_), channel_id=1, source_target_pairs={{0,8},{1,9},{2,10},{3,11},{4,12},{5,13},{6,14},{7,15},{8,0},{9,1},... | collective-permute-start | bytes 614408 | tf_op jit(solution)/shard_map/ppermute | solution.py:214
  29.8 21.1 %copy-start.21 = (bf16[80,1280]{1,0:T(8,128)(2,1)}, bf16[80,1280]{1,0:T(8,128)(2,1)S(1)}, u32[]{:S(2)}) copy-start(bf16[80,1280]{1,0:T(8,128)(2,1)S(1)} %collective-permute-done.1.refs_1_) | copy-start | bytes 614404
  29.8 9.3 %collective-permute-start.17 = (bf16[80,1280]{1,0:T(8,128)(2,1)S(1)}, bf16[80,1280]{1,0:T(8,128)(2,1)S(1)}, u32[]{:S(2)}, u32[]{:S(2)}) collective-permute-start(bf16[80,1280]{1,0:T(8,128)(2,1)S(1)} %collective-permute-done.15.refs_0_), channel_id=1, source_target_pairs={{0,1},{1,0},{2,3},{3,2},{4,5},{5,4},{6,7},{7,6},{8,24},{9,25},{10,... | collective-permute-start | bytes 614408 | tf_op jit(solution)/shard_map/ppermute | solution.py:213
  32.0 18.9 %copy-start.17 = (bf16[80,1280]{1,0:T(8,128)(2,1)}, bf16[80,1280]{1,0:T(8,128)(2,1)S(1)}, u32[]{:S(2)}) copy-start(bf16[80,1280]{1,0:T(8,128)(2,1)S(1)} %collective-permute-done.28.refs_4_) | copy-start | bytes 614404
  32.0 7.6 %collective-permute-start.16 = (bf16[80,1280]{1,0:T(8,128)(2,1)S(1)}, bf16[80,1280]{1,0:T(8,128)(2,1)S(1)}, u32[]{:S(2)}, u32[]{:S(2)}) collective-permute-start(bf16[80,1280]{1,0:T(8,128)(2,1)S(1)} %collective-permute-done.15.refs_0_), channel_id=1, source_target_pairs={{0,16},{1,17},{2,18},{3,19},{4,20},{5,21},{6,22},{7,23},{8,9},{9,8... | collective-permute-start | bytes 614408 | tf_op jit(solution)/shard_map/ppermute | solution.py:212
  34.5 20.2 %copy-start.18 = (bf16[80,1280]{1,0:T(8,128)(2,1)}, bf16[80,1280]{1,0:T(8,128)(2,1)S(1)}, u32[]{:S(2)}) copy-start(bf16[80,1280]{1,0:T(8,128)(2,1)S(1)} %collective-permute-done.26.refs_2_) | copy-start | bytes 614404
  34.5 9.3 %collective-permute-start.2 = (bf16[80,1280]{1,0:T(8,128)(2,1)S(1)}, bf16[80,1280]{1,0:T(8,128)(2,1)S(1)}, u32[]{:S(2)}, u32[]{:S(2)}) collective-permute-start(bf16[80,1280]{1,0:T(8,128)(2,1)S(1)} %collective-permute-done.1.refs_1_), channel_id=1, source_target_pairs={{0,16},{1,17},{2,18},{3,19},{4,20},{5,21},{6,22},{7,23},{8,24},{9,... | collective-permute-start | bytes 614408 | tf_op jit(solution)/shard_map/ppermute | solution.py:201
  36.6 15.6 %collective-permute-start.10 = (bf16[80,1280]{1,0:T(8,128)(2,1)S(1)}, bf16[80,1280]{1,0:T(8,128)(2,1)S(1)}, u32[]{:S(2)}, u32[]{:S(2)}) collective-permute-start(bf16[80,1280]{1,0:T(8,128)(2,1)S(1)} %collective-permute-done.6.refs_0_), channel_id=1, source_target_pairs={{0,8},{1,9},{2,10},{3,11},{4,12},{5,13},{6,14},{7,15},{8,0},{9,1},... | collective-permute-start | bytes 614408 | tf_op jit(solution)/shard_map/ppermute | solution.py:214
  36.6 18.1 %collective-permute-start.8 = (bf16[80,1280]{1,0:T(8,128)(2,1)S(1)}, bf16[80,1280]{1,0:T(8,128)(2,1)S(1)}, u32[]{:S(2)}, u32[]{:S(2)}) collective-permute-start(bf16[80,1280]{1,0:T(8,128)(2,1)S(1)} %collective-permute-done.6.refs_0_), channel_id=1, source_target_pairs={{0,1},{1,0},{2,3},{3,2},{4,5},{5,4},{6,7},{7,6},{8,24},{9,25},{10,... | collective-permute-start | bytes 614408 | tf_op jit(solution)/shard_map/ppermute | solution.py:213
  39.0 27.0 %copy-start.14 = (bf16[80,1280]{1,0:T(8,128)(2,1)}, bf16[80,1280]{1,0:T(8,128)(2,1)S(1)}, u32[]{:S(2)}) copy-start(bf16[80,1280]{1,0:T(8,128)(2,1)S(1)} %collective-permute-done.17.refs_2_) | copy-start | bytes 614404
  39.0 15.8 %collective-permute-start.3 = (bf16[80,1280]{1,0:T(8,128)(2,1)S(1)}, bf16[80,1280]{1,0:T(8,128)(2,1)S(1)}, u32[]{:S(2)}, u32[]{:S(2)}) collective-permute-start(bf16[80,1280]{1,0:T(8,128)(2,1)S(1)} %collective-permute-done.1.refs_1_), channel_id=1, source_target_pairs={{0,8},{1,9},{2,10},{3,11},{4,12},{5,13},{6,14},{7,15},{8,0},{9,1},... | collective-permute-start | bytes 614408 | tf_op jit(solution)/shard_map/ppermute | solution.py:202
  39.5 25.9 %copy-start.16 = (bf16[80,1280]{1,0:T(8,128)(2,1)}, bf16[80,1280]{1,0:T(8,128)(2,1)S(1)}, u32[]{:S(2)}) copy-start(bf16[80,1280]{1,0:T(8,128)(2,1)S(1)} %collective-permute-done.16.refs_1_) | copy-start | bytes 614404
  39.5 15.8 %collective-permute-start.27 = (bf16[80,1280]{1,0:T(8,128)(2,1)S(1)}, bf16[80,1280]{1,0:T(8,128)(2,1)S(1)}, u32[]{:S(2)}, u32[]{:S(2)}) collective-permute-start(bf16[80,1280]{1,0:T(8,128)(2,1)S(1)} %collective-permute-done.25.refs_1_), channel_id=1, source_target_pairs={{0,1},{1,0},{2,3},{3,2},{4,5},{5,4},{6,7},{7,6},{8,24},{9,25},{10,... | collective-permute-start | bytes 614408 | tf_op jit(solution)/shard_map/ppermute | solution.py:213
  43.9 12.0 %collective-permute-start.4 = (bf16[80,1280]{1,0:T(8,128)(2,1)S(1)}, bf16[80,1280]{1,0:T(8,128)(2,1)S(1)}, u32[]{:S(2)}, u32[]{:S(2)}) collective-permute-start(bf16[80,1280]{1,0:T(8,128)(2,1)S(1)} %collective-permute-done.2.refs_2_), channel_id=1, source_target_pairs={{0,8},{1,9},{2,10},{3,11},{4,12},{5,13},{6,14},{7,15},{8,0},{9,1},... | collective-permute-start | bytes 614408 | tf_op jit(solution)/shard_map/ppermute | solution.py:202
  52.1 13.2 %collective-permute-start.7 = (bf16[80,1280]{1,0:T(8,128)(2,1)S(1)}, bf16[80,1280]{1,0:T(8,128)(2,1)S(1)}, u32[]{:S(2)}, u32[]{:S(2)}) collective-permute-start(bf16[80,1280]{1,0:T(8,128)(2,1)S(1)} %collective-permute-done.6.refs_0_), channel_id=1, source_target_pairs={{0,16},{1,17},{2,18},{3,19},{4,20},{5,21},{6,22},{7,23},{8,9},{9,8... | collective-permute-start | bytes 614408 | tf_op jit(solution)/shard_map/ppermute | solution.py:212
  54.7 22.6 %copy-start.15 = (bf16[80,1280]{1,0:T(8,128)(2,1)}, bf16[80,1280]{1,0:T(8,128)(2,1)S(1)}, u32[]{:S(2)}) copy-start(bf16[80,1280]{1,0:T(8,128)(2,1)S(1)} %collective-permute-done.8.refs_2_) | copy-start | bytes 614404
  54.7 11.3 %collective-permute-start.29 = (bf16[80,1280]{1,0:T(8,128)(2,1)S(1)}, bf16[80,1280]{1,0:T(8,128)(2,1)S(1)}, u32[]{:S(2)}, u32[]{:S(2)}) collective-permute-start(bf16[80,1280]{1,0:T(8,128)(2,1)S(1)} %collective-permute-done.25.refs_1_), channel_id=1, source_target_pairs={{0,8},{1,9},{2,10},{3,11},{4,12},{5,13},{6,14},{7,15},{8,0},{9,1},... | collective-permute-start | bytes 614408 | tf_op jit(solution)/shard_map/ppermute | solution.py:214
  54.8 10.6 %collective-permute-start.30 = (bf16[80,1280]{1,0:T(8,128)(2,1)S(1)}, bf16[80,1280]{1,0:T(8,128)(2,1)S(1)}, u32[]{:S(2)}, u32[]{:S(2)}) collective-permute-start(bf16[80,1280]{1,0:T(8,128)(2,1)S(1)} %collective-permute-done.26.refs_2_), channel_id=1, source_target_pairs={{0,8},{1,9},{2,10},{3,11},{4,12},{5,13},{6,14},{7,15},{8,0},{9,1},... | collective-permute-start | bytes 614408 | tf_op jit(solution)/shard_map/ppermute | solution.py:214
  55.3 10.8 %collective-permute-start.18 = (bf16[80,1280]{1,0:T(8,128)(2,1)S(1)}, bf16[80,1280]{1,0:T(8,128)(2,1)S(1)}, u32[]{:S(2)}, u32[]{:S(2)}) collective-permute-start(bf16[80,1280]{1,0:T(8,128)(2,1)S(1)} %collective-permute-done.16.refs_1_), channel_id=1, source_target_pairs={{0,1},{1,0},{2,3},{3,2},{4,5},{5,4},{6,7},{7,6},{8,24},{9,25},{10,... | collective-permute-start | bytes 614408 | tf_op jit(solution)/shard_map/ppermute | solution.py:213
  55.8 11.8 %collective-permute-start.31 = (bf16[80,1280]{1,0:T(8,128)(2,1)S(1)}, bf16[80,1280]{1,0:T(8,128)(2,1)S(1)}, u32[]{:S(2)}, u32[]{:S(2)}) collective-permute-start(bf16[80,1280]{1,0:T(8,128)(2,1)S(1)} %collective-permute-done.27.refs_3_), channel_id=1, source_target_pairs={{0,8},{1,9},{2,10},{3,11},{4,12},{5,13},{6,14},{7,15},{8,0},{9,1},... | collective-permute-start | bytes 614408 | tf_op jit(solution)/shard_map/ppermute | solution.py:214
  65.3 33.3 %collective-permute-start.32 = (bf16[320,1280]{1,0:T(8,128)(2,1)}, bf16[320,1280]{1,0:T(8,128)(2,1)S(1)}, u32[]{:S(2)}, u32[]{:S(2)}) collective-permute-start(bf16[320,1280]{1,0:T(8,128)(2,1)} %get-tuple-element.27), channel_id=1, source_target_pairs={{0,8},{1,9},{2,10},{3,11},{4,12},{5,13},{6,14},{7,15},{8,0},{9,1},... | collective-permute-start | bytes 2457608 | tf_op jit(solution)/shard_map/ppermute | solution.py:240
  65.4 11.9 %collective-permute-start.20 = (bf16[80,1280]{1,0:T(8,128)(2,1)S(1)}, bf16[80,1280]{1,0:T(8,128)(2,1)S(1)}, u32[]{:S(2)}, u32[]{:S(2)}) collective-permute-start(bf16[80,1280]{1,0:T(8,128)(2,1)S(1)} %collective-permute-done.16.refs_1_), channel_id=1, source_target_pairs={{0,8},{1,9},{2,10},{3,11},{4,12},{5,13},{6,14},{7,15},{8,0},{9,1},... | collective-permute-start | bytes 614408 | tf_op jit(solution)/shard_map/ppermute | solution.py:214
  66.0 11.2 %collective-permute-start.21 = (bf16[80,1280]{1,0:T(8,128)(2,1)S(1)}, bf16[80,1280]{1,0:T(8,128)(2,1)S(1)}, u32[]{:S(2)}, u32[]{:S(2)}) collective-permute-start(bf16[80,1280]{1,0:T(8,128)(2,1)S(1)} %collective-permute-done.17.refs_2_), channel_id=1, source_target_pairs={{0,8},{1,9},{2,10},{3,11},{4,12},{5,13},{6,14},{7,15},{8,0},{9,1},... | collective-permute-start | bytes 614408 | tf_op jit(solution)/shard_map/ppermute | solution.py:214
  66.1 11.8 %collective-permute-start.9 = (bf16[80,1280]{1,0:T(8,128)(2,1)S(1)}, bf16[80,1280]{1,0:T(8,128)(2,1)S(1)}, u32[]{:S(2)}, u32[]{:S(2)}) collective-permute-start(bf16[80,1280]{1,0:T(8,128)(2,1)S(1)} %collective-permute-done.7.refs_1_), channel_id=1, source_target_pairs={{0,1},{1,0},{2,3},{3,2},{4,5},{5,4},{6,7},{7,6},{8,24},{9,25},{10,... | collective-permute-start | bytes 614408 | tf_op jit(solution)/shard_map/ppermute | solution.py:213
  67.7 10.3 %collective-permute-start.22 = (bf16[80,1280]{1,0:T(8,128)(2,1)S(1)}, bf16[80,1280]{1,0:T(8,128)(2,1)S(1)}, u32[]{:S(2)}, u32[]{:S(2)}) collective-permute-start(bf16[80,1280]{1,0:T(8,128)(2,1)S(1)} %collective-permute-done.18.refs_3_), channel_id=1, source_target_pairs={{0,8},{1,9},{2,10},{3,11},{4,12},{5,13},{6,14},{7,15},{8,0},{9,1},... | collective-permute-start | bytes 614408 | tf_op jit(solution)/shard_map/ppermute | solution.py:214
  77.2 10.8 %collective-permute-start.11 = (bf16[80,1280]{1,0:T(8,128)(2,1)S(1)}, bf16[80,1280]{1,0:T(8,128)(2,1)S(1)}, u32[]{:S(2)}, u32[]{:S(2)}) collective-permute-start(bf16[80,1280]{1,0:T(8,128)(2,1)S(1)} %collective-permute-done.7.refs_1_), channel_id=1, source_target_pairs={{0,8},{1,9},{2,10},{3,11},{4,12},{5,13},{6,14},{7,15},{8,0},{9,1},... | collective-permute-start | bytes 614408 | tf_op jit(solution)/shard_map/ppermute | solution.py:214
  77.3 10.2 %collective-permute-start.12 = (bf16[80,1280]{1,0:T(8,128)(2,1)S(1)}, bf16[80,1280]{1,0:T(8,128)(2,1)S(1)}, u32[]{:S(2)}, u32[]{:S(2)}) collective-permute-start(bf16[80,1280]{1,0:T(8,128)(2,1)S(1)} %collective-permute-done.8.refs_2_), channel_id=1, source_target_pairs={{0,8},{1,9},{2,10},{3,11},{4,12},{5,13},{6,14},{7,15},{8,0},{9,1},... | collective-permute-start | bytes 614408 | tf_op jit(solution)/shard_map/ppermute | solution.py:214
  77.9 10.2 %collective-permute-start.13 = (bf16[80,1280]{1,0:T(8,128)(2,1)S(1)}, bf16[80,1280]{1,0:T(8,128)(2,1)S(1)}, u32[]{:S(2)}, u32[]{:S(2)}) collective-permute-start(bf16[80,1280]{1,0:T(8,128)(2,1)S(1)} %collective-permute-done.9.refs_3_), channel_id=1, source_target_pairs={{0,8},{1,9},{2,10},{3,11},{4,12},{5,13},{6,14},{7,15},{8,0},{9,1},... | collective-permute-start | bytes 614408 | tf_op jit(solution)/shard_map/ppermute | solution.py:214
  78.0 21.4 %collective-permute-start.43 = (bf16[320,1280]{1,0:T(8,128)(2,1)}, bf16[320,1280]{1,0:T(8,128)(2,1)S(1)}, u32[]{:S(2)}, u32[]{:S(2)}) collective-permute-start(bf16[320,1280]{1,0:T(8,128)(2,1)} %get-tuple-element.33), channel_id=1, source_target_pairs={{0,8},{1,9},{2,10},{3,11},{4,12},{5,13},{6,14},{7,15},{8,0},{9,1},... | collective-permute-start | bytes 2457608 | tf_op jit(solution)/shard_map/ppermute | solution.py:240
  87.6 13.5 %collective-permute-start.39 = (bf16[320,1280]{1,0:T(8,128)(2,1)}, bf16[320,1280]{1,0:T(8,128)(2,1)S(1)}, u32[]{:S(2)}, u32[]{:S(2)}) collective-permute-start(bf16[320,1280]{1,0:T(8,128)(2,1)} %get-tuple-element.31), channel_id=1, source_target_pairs={{0,8},{1,9},{2,10},{3,11},{4,12},{5,13},{6,14},{7,15},{8,0},{9,1},... | collective-permute-start | bytes 2457608 | tf_op jit(solution)/shard_map/ppermute | solution.py:240
  98.5 3.3 %collective-permute-start.35 = (bf16[320,1280]{1,0:T(8,128)(2,1)}, bf16[320,1280]{1,0:T(8,128)(2,1)S(1)}, u32[]{:S(2)}, u32[]{:S(2)}) collective-permute-start(bf16[320,1280]{1,0:T(8,128)(2,1)} %get-tuple-element.29), channel_id=1, source_target_pairs={{0,8},{1,9},{2,10},{3,11},{4,12},{5,13},{6,14},{7,15},{8,0},{9,1},... | collective-permute-start | bytes 2457608 | tf_op jit(solution)/shard_map/ppermute | solution.py:240
  98.8 8.0 %collective-permute-start.33 = (bf16[160,1280]{1,0:T(8,128)(2,1)S(1)}, bf16[160,1280]{1,0:T(8,128)(2,1)S(1)}, u32[]{:S(2)}, u32[]{:S(2)}) collective-permute-start(bf16[160,1280]{1,0:T(8,128)(2,1)S(1)} %add_convert_fusion.3), channel_id=1, source_target_pairs={{0,16},{1,17},{2,18},{3,19},{4,20},{5,21},{6,22},{7,23},{8,9},{9,8... | collective-permute-start | bytes 1228808 | tf_op jit(solution)/shard_map/ppermute | solution.py:241
  99.5 13.7 %collective-permute-start.44 = (bf16[160,1280]{1,0:T(8,128)(2,1)S(1)}, bf16[160,1280]{1,0:T(8,128)(2,1)S(1)}, u32[]{:S(2)}, u32[]{:S(2)}) collective-permute-start(bf16[160,1280]{1,0:T(8,128)(2,1)S(1)} %add_convert_fusion), channel_id=1, source_target_pairs={{0,16},{1,17},{2,18},{3,19},{4,20},{5,21},{6,22},{7,23},{8,9},{9,8... | collective-permute-start | bytes 1228808 | tf_op jit(solution)/shard_map/ppermute | solution.py:241
  101.2 18.8 %collective-permute-start.40 = (bf16[160,1280]{1,0:T(8,128)(2,1)S(1)}, bf16[160,1280]{1,0:T(8,128)(2,1)S(1)}, u32[]{:S(2)}, u32[]{:S(2)}) collective-permute-start(bf16[160,1280]{1,0:T(8,128)(2,1)S(1)} %add_convert_fusion.1), channel_id=1, source_target_pairs={{0,16},{1,17},{2,18},{3,19},{4,20},{5,21},{6,22},{7,23},{8,9},{9,8... | collective-permute-start | bytes 1228808 | tf_op jit(solution)/shard_map/ppermute | solution.py:241
  101.9 24.7 %collective-permute-start.36 = (bf16[160,1280]{1,0:T(8,128)(2,1)S(1)}, bf16[160,1280]{1,0:T(8,128)(2,1)S(1)}, u32[]{:S(2)}, u32[]{:S(2)}) collective-permute-start(bf16[160,1280]{1,0:T(8,128)(2,1)S(1)} %add_convert_fusion.2), channel_id=1, source_target_pairs={{0,16},{1,17},{2,18},{3,19},{4,20},{5,21},{6,22},{7,23},{8,9},{9,8... | collective-permute-start | bytes 1228808 | tf_op jit(solution)/shard_map/ppermute | solution.py:241
  106.9 25.8 %collective-permute-start.34 = (bf16[80,1280]{1,0:T(8,128)(2,1)S(1)}, bf16[80,1280]{1,0:T(8,128)(2,1)S(1)}, u32[]{:S(2)}, u32[]{:S(2)}) collective-permute-start(bf16[80,1280]{1,0:T(8,128)(2,1)S(1)} %add_convert_fusion.10), channel_id=1, source_target_pairs={{0,1},{1,0},{2,3},{3,2},{4,5},{5,4},{6,7},{7,6},{8,24},{9,25},{10,... | collective-permute-start | bytes 614408 | tf_op jit(solution)/shard_map/ppermute | solution.py:242
  113.3 13.9 %collective-permute-start.45 = (bf16[80,1280]{1,0:T(8,128)(2,1)S(1)}, bf16[80,1280]{1,0:T(8,128)(2,1)S(1)}, u32[]{:S(2)}, u32[]{:S(2)}) collective-permute-start(bf16[80,1280]{1,0:T(8,128)(2,1)S(1)} %add_convert_fusion.5), channel_id=1, source_target_pairs={{0,1},{1,0},{2,3},{3,2},{4,5},{5,4},{6,7},{7,6},{8,24},{9,25},{10,... | collective-permute-start | bytes 614408 | tf_op jit(solution)/shard_map/ppermute | solution.py:242
  120.1 7.4 %collective-permute-start.41 = (bf16[80,1280]{1,0:T(8,128)(2,1)S(1)}, bf16[80,1280]{1,0:T(8,128)(2,1)S(1)}, u32[]{:S(2)}, u32[]{:S(2)}) collective-permute-start(bf16[80,1280]{1,0:T(8,128)(2,1)S(1)} %add_convert_fusion.7), channel_id=1, source_target_pairs={{0,1},{1,0},{2,3},{3,2},{4,5},{5,4},{6,7},{7,6},{8,24},{9,25},{10,... | collective-permute-start | bytes 614408 | tf_op jit(solution)/shard_map/ppermute | solution.py:242
  126.6 5.8 %collective-permute-start.37 = (bf16[80,1280]{1,0:T(8,128)(2,1)S(1)}, bf16[80,1280]{1,0:T(8,128)(2,1)S(1)}, u32[]{:S(2)}, u32[]{:S(2)}) collective-permute-start(bf16[80,1280]{1,0:T(8,128)(2,1)S(1)} %add_convert_fusion.9), channel_id=1, source_target_pairs={{0,1},{1,0},{2,3},{3,2},{4,5},{5,4},{6,7},{7,6},{8,24},{9,25},{10,... | collective-permute-start | bytes 614408 | tf_op jit(solution)/shard_map/ppermute | solution.py:242
  127.3 9.9 %collective-permute-start.46 = (bf16[80,1280]{1,0:T(8,128)(2,1)S(1)}, bf16[80,1280]{1,0:T(8,128)(2,1)S(1)}, u32[]{:S(2)}, u32[]{:S(2)}) collective-permute-start(bf16[80,1280]{1,0:T(8,128)(2,1)S(1)} %add_convert_fusion.4), channel_id=1, source_target_pairs={{0,2},{1,3},{2,4},{3,5},{4,6},{5,7},{6,0},{7,1},{8,10},{9,11},{10,... | collective-permute-start | bytes 614408 | tf_op jit(solution)/shard_map/ppermute | solution.py:245
  127.5 14.6 %collective-permute-start.42 = (bf16[80,1280]{1,0:T(8,128)(2,1)S(1)}, bf16[80,1280]{1,0:T(8,128)(2,1)S(1)}, u32[]{:S(2)}, u32[]{:S(2)}) collective-permute-start(bf16[80,1280]{1,0:T(8,128)(2,1)S(1)} %add_convert_fusion.6), channel_id=1, source_target_pairs={{0,4},{1,5},{2,6},{3,7},{4,0},{5,1},{6,2},{7,3},{8,12},{9,13},{10,... | collective-permute-start | bytes 614408 | tf_op jit(solution)/shard_map/ppermute | solution.py:245
  132.6 9.6 %collective-permute-start.38 = (bf16[80,1280]{1,0:T(8,128)(2,1)S(1)}, bf16[80,1280]{1,0:T(8,128)(2,1)S(1)}, u32[]{:S(2)}, u32[]{:S(2)}) collective-permute-start(bf16[80,1280]{1,0:T(8,128)(2,1)S(1)} %add_convert_fusion.8), channel_id=1, source_target_pairs={{0,6},{1,7},{2,0},{3,1},{4,2},{5,3},{6,4},{7,5},{8,14},{9,15},{10,... | collective-permute-start | bytes 614408 | tf_op jit(solution)/shard_map/ppermute | solution.py:245
  142.4 19.2 %copy-start.4 = (bf16[80,1280]{1,0:T(8,128)(2,1)}, bf16[80,1280]{1,0:T(8,128)(2,1)S(1)}, u32[]{:S(2)}) copy-start(bf16[80,1280]{1,0:T(8,128)(2,1)S(1)} %multiply_convert_fusion.refs_0_) | copy-start | bytes 614404
  142.4 6.5 %collective-permute-start.47 = (bf16[80,1280]{1,0:T(8,128)(2,1)S(1)}, bf16[80,1280]{1,0:T(8,128)(2,1)S(1)}, u32[]{:S(2)}, u32[]{:S(2)}) collective-permute-start(bf16[80,1280]{1,0:T(8,128)(2,1)S(1)} %multiply_convert_fusion.refs_0_), channel_id=1, source_target_pairs={{0,16},{1,17},{2,18},{3,19},{4,20},{5,21},{6,22},{7,23},{8,24},{9,... | collective-permute-start | bytes 614408 | tf_op jit(solution)/shard_map/ppermute | solution.py:248
  144.1 17.5 %collective-permute-start.48 = (bf16[80,1280]{1,0:T(8,128)(2,1)S(1)}, bf16[80,1280]{1,0:T(8,128)(2,1)S(1)}, u32[]{:S(2)}, u32[]{:S(2)}) collective-permute-start(bf16[80,1280]{1,0:T(8,128)(2,1)S(1)} %multiply_convert_fusion.refs_0_), channel_id=1, source_target_pairs={{0,8},{1,9},{2,10},{3,11},{4,12},{5,13},{6,14},{7,15},{8,0},{9,1},... | collective-permute-start | bytes 614408 | tf_op jit(solution)/shard_map/ppermute | solution.py:249
  148.9 12.7 %collective-permute-start.49 = (bf16[80,1280]{1,0:T(8,128)(2,1)S(1)}, bf16[80,1280]{1,0:T(8,128)(2,1)S(1)}, u32[]{:S(2)}, u32[]{:S(2)}) collective-permute-start(bf16[80,1280]{1,0:T(8,128)(2,1)S(1)} %collective-permute-done.47.refs_1_), channel_id=1, source_target_pairs={{0,8},{1,9},{2,10},{3,11},{4,12},{5,13},{6,14},{7,15},{8,0},{9,1},... | collective-permute-start | bytes 614408 | tf_op jit(solution)/shard_map/ppermute | solution.py:249
  (26 other events, 149.2 us)

commit v2 on v1

--- a/solution.py
+++ b/solution.py
@@ -34,25 +34,34 @@
 
 def norm_kernel(rows_ref, gamma_ref, beta_ref, out_ref):
     standard, _ = standardise(rows_ref[...])
-    out_ref[...] = (standard * gamma_ref[...] + beta_ref[...]).astype(BF16)
-
-
-def chunk_kernel(places, pieces, table_ref, counts_ref, n_ref, g_ref, b_ref, *refs):
-    piece_refs, (keep_ref, send_ref, h_ref, w_ref), (sum_ref,) = refs[:pieces], refs[pieces : pieces + 4], refs[pieces + 4 :]
+    out_ref[...] = (standard * gamma_ref[...].reshape(1, -1) + beta_ref[...].reshape(1, -1)).astype(BF16)
+
+
+def chunk_kernel(places, pieces, waits, table_ref, counts_ref, n_ref, g_ref, b_ref, *refs):
+    piece_refs, (keep_ref, *send_refs, h_ref, w_ref), (sum_ref,) = (
+        refs[:pieces],
+        refs[pieces + waits : pieces + waits + 5],
+        refs[pieces + waits + 5 :],
+    )
+    block = keep_ref.shape[0] // 4
+    bias = b_ref[...].astype(F32)
     for at, piece in enumerate(piece_refs):
         start = pl.multiple_of(table_ref[places["pieces"] + at], 16)
-        w_ref[pl.ds(start, piece.shape[0]), :] = piece[...]
+        extra = piece.shape[0] % block
+        size = piece.shape[0] - extra
+        w_ref[pl.ds(start, size), :] = piece[:size, :]
+        if extra:
+            bias += piece[size:, : bias.shape[1]].astype(F32)[:1]
     per_dev, units = h_ref.shape
     count = counts_ref[0, table_ref[places["patch"]]]
     live = lax.broadcasted_iota(jnp.int32, (per_dev, 1), 0) < count
     for low in range(0, units, 256):
         cols = slice(low, min(low + 256, units))
         pre_act = lax.dot_general(n_ref[...], w_ref[cols, :], (((1,), (1,)), ((), ())), preferred_element_type=F32)
-        slope = gelu_slope(pre_act + b_ref[:, cols].astype(F32))
+        slope = gelu_slope(pre_act + bias[:, cols])
         hidden = jnp.where(live, g_ref[:, cols].astype(F32) * slope, 0.0)
         h_ref[:, cols] = hidden.astype(BF16)
     width = n_ref.shape[1]
-    block = keep_ref.shape[0] // 4
     for low in range(0, width, 256):
         cols = slice(low, min(low + 256, width))
         sum_ref[:, cols] = lax.dot_general(
@@ -60,23 +69,23 @@
         )
     for at in range(8):
         start = pl.multiple_of(table_ref[places["blocks"] + at], 16)
-        out = send_ref if at < 4 else keep_ref
-        out[(at % 4) * block : (at % 4 + 1) * block, :] = sum_ref[pl.ds(start, block), :].astype(BF16)
-
-
-def rows_kernel(places, chunks, table_ref, counts_ref, rows_ref, gamma_ref, *refs):
+        out, to = (send_refs[at // 2], at % 2) if at < 4 else (keep_ref, at % 4)
+        out[to * block : (to + 1) * block, :] = sum_ref[pl.ds(start, block), :].astype(BF16)
+
+
+def rows_kernel(places, chunks, first_tile, table_ref, counts_ref, rows_ref, gamma_ref, *refs):
     h_refs, w_refs, out_ref = refs[:chunks], refs[chunks : 2 * chunks], refs[-1]
     tile = rows_ref.shape[0]
     normed_grad = jnp.dot(h_refs[0][...], w_refs[0][...], preferred_element_type=F32)
     for h, w in zip(h_refs[1:], w_refs[1:]):
         normed_grad += jnp.dot(h[...], w[...], preferred_element_type=F32)
     standard, inverse = standardise(rows_ref[...])
-    scaled = normed_grad * gamma_ref[...]
+    scaled = normed_grad * gamma_ref[...].reshape(1, -1)
     first = jnp.mean(scaled, axis=1, keepdims=True)
     second = jnp.mean(scaled * standard, axis=1, keepdims=True)
     grad = inverse * (scaled - first - standard * second)
     count = counts_ref[0, table_ref[places["patch"]]]
-    row = lax.broadcasted_iota(jnp.int32, (tile, 1), 0) + pl.program_id(0) * tile
+    row = lax.broadcasted_iota(jnp.int32, (tile, 1), 0) + (pl.program_id(0) + first_tile) * tile
     out_ref[...] = jnp.where(row < count, grad, 0.0).astype(BF16)
 
 
@@ -138,13 +147,13 @@
         return {"patch": 0, "chunk": 1, "far": base, "near": base + 8, "blocks": base + 13, "final": base + 21}
 
 
-def call_chunk(places, step, table, counts, normed_rows, grad_hidden, bias, pieces, shard, near):
+def call_chunk(places, step, table, counts, normed_rows, grad_hidden, bias, pieces, shard, near, after):
     per_dev, width = normed_rows.shape
     units = 2 * shard
     where = dict(places, pieces=places["near" if near else "far"])
     whole = lambda shape: pl.BlockSpec(shape, lambda i, t, c: (0,) * len(shape))
     return pl.pallas_call(
-        functools.partial(chunk_kernel, where, len(pieces)),
+        functools.partial(chunk_kernel, where, len(pieces), len(after)),
         grid_spec=pltpu.PrefetchScalarGridSpec(
             num_scalar_prefetch=2,
             grid=(1,),
@@ -153,10 +162,12 @@
                 pl.BlockSpec((per_dev, units), lambda i, t, c: (0, t[places["chunk"] + step])),
                 whole((1, units)),
             ]
-            + [whole(p.shape) for p in pieces],
+            + [whole(p.shape) for p in pieces]
+            + [pl.BlockSpec(memory_space=pl.ANY)] * len(after),
             out_specs=[
                 whole((units // 2, width)),
-                whole((units // 2, width)),
+                whole((units // 4, width)),
+                whole((units // 4, width)),
                 whole((per_dev, units)),
                 whole((units, width)),
             ],
@@ -164,18 +175,19 @@
         ),
         out_shape=[
             jax.ShapeDtypeStruct((units // 2, width), BF16),
-            jax.ShapeDtypeStruct((units // 2, width), BF16),
+            jax.ShapeDtypeStruct((units // 4, width), BF16),
+            jax.ShapeDtypeStruct((units // 4, width), BF16),
             jax.ShapeDtypeStruct((per_dev, units), BF16),
             jax.ShapeDtypeStruct((units, width), BF16),
         ],
         compiler_params=pltpu.CompilerParams(vmem_limit_bytes=LIMIT),
         cost_estimate=pl.CostEstimate(
-            flops=4 * per_dev * units * width,
+            flops=80 * per_dev * units * width,
             bytes_accessed=2 * per_dev * (width + 2 * units) + 6 * units * width,
             transcendentals=per_dev * units,
         ),
         name="chunk_%d" % step,
-    )(table, counts, normed_rows, grad_hidden, bias, *pieces)
+    )(table, counts, normed_rows, grad_hidden, bias, *pieces, *after)
 
 
 def fast_device(plan, rows, grad_hidden, counts, w_in, b_in, gamma, beta):
@@ -187,63 +199,130 @@
     table = lax.dynamic_index_in_dim(
         jnp.asarray(plan.table()), dp_index * n_patch + patch_index, 0, keepdims=False
     )
-    gamma, beta = gamma.reshape(1, width), beta.reshape(1, width)
     swap = lambda to: functools.partial(lax.ppermute, axis_name=AXES, perm=plan.perm(to))
     core = swap(lambda x, c, z, y: (x, 1 - c, z, y))
     along_x = swap(lambda x, c, z, y: (1 - x, c, z, y))
     along_y = swap(lambda x, c, z, y: (x, c, z, 1 - y))
     first, second = swap(plan.first), swap(plan.second)
     up = lambda s: swap(lambda x, c, z, y: (x, c, (z + s) % plan.nz, y))
-
-    mine = lax.dynamic_slice_in_dim(w_in, dp_index * quarter, quarter, 0)
-    from_z = [None] + [up(s)(mine) for s in range(1, plan.nz)]
+    half = per_dev // 2
+    tile = half // 2
+
+    units = 2 * shard
+    bias = b_in.reshape(1, shard)
+    low = patch_index % 2 == 0
+    place = lambda row: jnp.where(
+        low, jnp.pad(row, ((0, 0), (0, width - shard))), jnp.pad(row, ((0, 0), (shard, width - units)))
+    )
+    in_quarter = lax.broadcasted_iota(jnp.int32, (1, shard), 1) // quarter == dp_index
+    bias_row = jnp.broadcast_to(place(jnp.where(in_quarter, bias, jnp.zeros((), BF16))), (8, width))
+    mine = jnp.concatenate([lax.dynamic_slice_in_dim(w_in, dp_index * quarter, quarter, 0), bias_row], axis=0)
+    bias_own = place(bias)[:, :units]
+
+    from_z = {s: up(s)(mine) for s in (1, plan.nz - 1)}
     beside = along_y(mine)
-    diagonal = along_x(beside)
-    pieces = [[w_in, beside, diagonal, core(beside), core(diagonal)]]
-    bias_mine = b_in.reshape(1, shard)
-    bias_other = along_y(bias_mine)
-    low = patch_index % 2 == 0
-    bias_here = jnp.concatenate(
-        [jnp.where(low, bias_mine, bias_other), jnp.where(low, bias_other, bias_mine)], axis=1
-    )
-    bias = [bias_here] + [up(s)(bias_here) for s in range(1, plan.nz)]
-    for s in range(1, plan.nz):
-        a0 = from_z[s]
-        a1 = first(a0)
-        a2, a3 = second(a0), second(a1)
-        pieces.append([a0, a1, a2, a3] + [core(a) for a in (a0, a1, a2, a3)])
-
-    tile = per_dev // 4
     normed_rows = pl.pallas_call(
         norm_kernel,
         grid=(per_dev // tile,),
         in_specs=[
             pl.BlockSpec((tile, width), lambda i: (i, 0)),
-            pl.BlockSpec((1, width), lambda i: (0, 0)),
-            pl.BlockSpec((1, width), lambda i: (0, 0)),
+            pl.BlockSpec((width,), lambda i: (0,)),
+            pl.BlockSpec((width,), lambda i: (0,)),
         ],
         out_specs=pl.BlockSpec((tile, width), lambda i: (i, 0)),
         out_shape=jax.ShapeDtypeStruct((per_dev, width), BF16),
         compiler_params=pltpu.CompilerParams(vmem_limit_bytes=LIMIT),
         name="norm",
     )(rows, gamma, beta)
-
-    hidden, weights, total = [], [], None
-    scale = 1.0 / math.sqrt(VIS_DEV * n_patch * 4)
-    for s in range(plan.nz):
-        keep, send, h, w = call_chunk(
-            places, s, table, counts, normed_rows, grad_hidden, bias[s], pieces[s], shard, s == 0
+    beside, normed_rows = lax.optimization_barrier((beside, normed_rows))
+    for s in range(2, plan.nz - 1):
+        from_z[s] = up(1)(from_z[s - 1])
+    diagonal = along_x(beside)
+    pieces = {0: [w_in, beside, diagonal, core(beside), core(diagonal)]}
+    order = [0, 1, plan.nz - 1] + list(range(2, plan.nz - 1)) if plan.nz > 2 else [0, 1]
+    for s in order[1:]:
+        a0 = from_z[s]
+        a1 = first(a0)
+        a2, a3 = second(a0), second(a1)
+        pieces[s] = [a0, a1, a2, a3] + [core(a) for a in (a0, a1, a2, a3)]
+
+    cut = lambda array, at, n=1: array[at * quarter : (at + n) * quarter].astype(F32)
+    tied = lambda array, gate: lax.optimization_barrier((array, *gate))[0]
+
+    def homeward(s, keep, send_first, send_second):
+        got_first, got_second = core(send_first), core(send_second)
+        gate = yield None
+        got_first = tied(got_first, gate)
+        t = (cut(keep, 0, 2) + got_first.astype(F32)).astype(BF16)
+        gate = yield t
+        one = tied(first(t), gate)
+        v = (cut(keep, 2) + cut(got_second, 0) + cut(one, 0)).astype(BF16)
+        gate = yield v
+        two = tied(second(v), gate)
+        plane = cut(keep, 3) + cut(got_second, 1) + cut(one, 1) + two.astype(F32)
+        plane = plane if s == 0 else plane.astype(BF16)
+        gate = yield plane
+        term = plane if s == 0 else tied(up(-s)(plane), gate or [])
+        while True:
+            yield term
+
+    def advance(gate=(), last=4):
+        gate = list(gate)
+        for at, m in enumerate(moving):
+            if steps[at] < last:
+                gate = [m.send(gate)]
+                steps[at] += 1
+        return gate
+
+    hidden, weights, moving, steps = [], [], [], []
+    empty = jnp.zeros((1, units), BF16)
+    after = [from_z[s] for s in order[1:]]
+    for s in order:
+        keep, send_first, send_second, h, w = call_chunk(
+            places, s, table, counts, normed_rows, grad_hidden, bias_own if s == 0 else empty, pieces[s], shard,
+            s == 0, after,
         )
         hidden.append(h)
         weights.append(w)
-        own = lambda low, high: keep[low:high].astype(F32) + got[low:high].astype(F32)
-        got = core(send)
-        one = first(own(0, 2 * quarter).astype(BF16))
-        two = second((own(2 * quarter, 3 * quarter) + one[:quarter].astype(F32)).astype(BF16))
-        plane = own(3 * quarter, 4 * quarter) + one[quarter:].astype(F32) + two.astype(F32)
-        if s:
-            plane = up(-s)(plane.astype(BF16)).astype(F32)
-        total = plane if total is None else total + plane
+        moving.append(homeward(s, keep, send_first, send_second))
+        next(moving[-1])
+        steps.append(0)
+        after = advance()
+
+    def call_rows(part, after, out):
+        whole = lambda shape: pl.BlockSpec(shape, lambda i, t, c: (0,) * len(shape))
+        striped = lambda cols: pl.BlockSpec((tile, cols), lambda i, t, c: (i + 2 * part, 0))
+        more = list(after) + list(out)
+        return pl.pallas_call(
+            functools.partial(rows_kernel, places, plan.nz, 2 * part),
+            grid_spec=pltpu.PrefetchScalarGridSpec(
+                num_scalar_prefetch=2,
+                grid=(2,),
+                in_specs=[striped(width), pl.BlockSpec((width,), lambda i, t, c: (0,))]
+                + [striped(h.shape[1]) for h in hidden]
+                + [whole(w.shape) for w in weights]
+                + [pl.BlockSpec(memory_space=pl.ANY)] * len(more),
+                out_specs=striped(width),
+            ),
+            out_shape=jax.ShapeDtypeStruct((per_dev, width), BF16),
+            input_output_aliases={3 + 2 * plan.nz + len(more): 0} if out else {},
+            compiler_params=pltpu.CompilerParams(vmem_limit_bytes=LIMIT),
+            cost_estimate=pl.CostEstimate(
+                flops=40 * half * width * units * plan.nz,
+                bytes_accessed=4 * half * width + 2 * (half + width) * units * plan.nz,
+                transcendentals=0,
+            ),
+            name="grad_rows_%d" % part,
+        )(table, counts, rows, gamma, *hidden, *weights, *more)
+
+    grad_rows = call_rows(0, after, [])
+    after = [grad_rows]
+    while min(steps) < 3:
+        after = advance(after, 3)
+    grad_rows = call_rows(1, after, [grad_rows])
+    scale = 1.0 / math.sqrt(VIS_DEV * n_patch * 4)
+    total = sum(next(m).astype(F32) for m in moving)
+    total, grad_rows = lax.optimization_barrier((total, grad_rows))
     done = (total * scale).astype(BF16)
     done_x = along_x(done)
     quarters = [done, done_x, core(done), core(done_x)]
@@ -254,28 +333,6 @@
         out_shape=jax.ShapeDtypeStruct((shard, width), F32),
         name="place",
     )(table, *quarters)
-
-    whole = lambda shape: pl.BlockSpec(shape, lambda i, t, c: (0,) * len(shape))
-    striped = lambda cols: pl.BlockSpec((tile, cols), lambda i, t, c: (i, 0))
-    grad_rows = pl.pallas_call(
-        functools.partial(rows_kernel, places, plan.nz),
-        grid_spec=pltpu.PrefetchScalarGridSpec(
-            num_scalar_prefetch=2,
-            grid=(per_dev // tile,),
-            in_specs=[striped(width), whole((1, width))]
-            + [striped(h.shape[1]) for h in hidden]
-            + [whole(w.shape) for w in weights],
-            out_specs=striped(width),
-        ),
-        out_shape=jax.ShapeDtypeStruct((per_dev, width), BF16),
-        compiler_params=pltpu.CompilerParams(vmem_limit_bytes=LIMIT),
-        cost_estimate=pl.CostEstimate(
-            flops=2 * per_dev * width * 2 * shard * plan.nz,
-            bytes_accessed=4 * per_dev * width + 2 * (per_dev + width) * 2 * shard * plan.nz,
-            transcendentals=0,
-        ),
-        name="grad_rows",
-    )(table, counts, rows, gamma, *hidden, *weights)
     return grad_rows, grad_w_in
 
 

time: 169 us -> 147 us (0.87); the launches traced: 165 us -> 147 us
  waiting for transfers between devices: 55.7 us -> 39.9 us
  starting transfers between devices: 41.7 us -> 34 us
  Pallas kernels: 55 us -> 59.1 us
  other arithmetic: 2.02 us -> 5.53 us
  local copies, waits for them, and re-layouts: 9.91 us -> 7.02 us
    ppermute x36, waiting for transfers between devices: 45.6 us -> 21.1 us  [the longest x3 7.25 us: homeward(): term = plane if s == 0 else tied(up(-s)(plane), gate or [])]
    ppermute x6, waiting for transfers between devices: 0.02 us -> 8.44 us  [fast_device(): a2, a3 = (second(a0), second(a1))]
    pallas_call x5 -> x6, Pallas kernels: 48.2 us -> 52.2 us  [the longest x4 34.6 us: call_chunk(): pl.pallas_call(functools.partial(chunk_kernel, where, len(pieces), len(af...]
    ppermute x3, starting transfers between devices: 6.62 us -> 2.67 us  [fast_device(): a1 = first(a0)]
    reshape x3 -> x1, local copies, waits for them, and re-layouts: 3.3 us -> 0.01 us  [fast_device(): bias = b_in.reshape(1, shard)]
    convert_element_type x11, other arithmetic: 1.05 us -> 3.84 us  [the longest x4 3.16 us: homeward(): t = (cut(keep, 0, 2) + got_first.astype(F32)).astype(BF16)]
    ppermute x6, starting transfers between devices: 8.05 us -> 5.69 us  [fast_device(): a2, a3 = (second(a0), second(a1))]
    ppermute x1, waiting for transfers between devices: 3.67 us -> 1.73 us  [fast_device(): diagonal = along_x(beside)]
  transfers between devices with their start and end apart: 50 -> 50, of which waited for: 14 -> 12; matrix products, arithmetic and copies ran while one was open for 4% -> 4% of each run, Pallas kernels for 32% -> 39%
where the time goes in v2:
time: 147 us
  Pallas kernels  59.1 us (40%)
  waiting for transfers between devices  39.9 us (27%)
  starting transfers between devices  34 us (23%)
  local copies, waits for them, and re-layouts  7.02 us (5%)
  other arithmetic  5.53 us (4%)
    pallas_call x4, Pallas kernels, call_chunk(): pl.pallas_call(functools.partial(chunk_kernel, where, len(pieces), len(af...  34.6 us
    pallas_call x2, Pallas kernels, call_rows(): pl.pallas_call(functools.partial(rows_kernel, places, plan.nz, 2 * part),...  17.6 us
    ppermute x6, waiting for transfers between devices, fast_device(): a2, a3 = (second(a0), second(a1))  8.44 us
    ppermute x3, waiting for transfers between devices, homeward(): term = plane if s == 0 else tied(up(-s)(plane), gate or [])  7.25 us
    ppermute x4, waiting for transfers between devices, homeward(): one = tied(first(t), gate)  6.67 us
    ppermute x1, waiting for transfers between devices, fast_device(): done_x = along_x(done)  5.74 us
    ppermute x6, starting transfers between devices, fast_device(): a2, a3 = (second(a0), second(a1))  5.69 us
    ppermute x4, starting transfers between devices, homeward(): one = tied(first(t), gate)  5.02 us
  transfers between devices with their start and end apart: 50, of which 12 were waited for; matrix products, arithmetic and copies ran while one was open for 4% of the time, Pallas kernels for 39%

profile of v2, /device:TPU:0, one launch (start us, length us, event | category | flops | bytes accessed | tf_op | source)
XLA Modules:
  0.0 146.8 jit_solution(14068021245465729759)
XLA Ops:
  0.6 0.7 fusion.2
  1.4 0.9 constant_dynamic-slice_fusion
  2.4 3.0 %collective-permute-start = (bf16[88,1280]{1,0:T(8,128)(2,1)S(1)}, bf16[88,1280]{1,0:T(8,128)(2,1)S(1)}, u32[]{:S(2)}, u32[]{:S(2)}) collective-permute-start(bf16[88,1280]{1,0:T(8,128)(2,1)S(1)} %pad_maximum_fusion), channel_id=1, source_target_pairs={{0,1},{1,0},{2,3},{3,2},{4,5},{5,4},{6,7},{7,6},{8,9},{9,8},{10,11... | collective-permute-start | bytes 675848 | tf_op jit(solution)/shard_map/ppermute | solution.py:223
  5.5 1.6 %collective-permute-start.4 = (bf16[88,1280]{1,0:T(8,128)(2,1)S(1)}, bf16[88,1280]{1,0:T(8,128)(2,1)S(1)}, u32[]{:S(2)}, u32[]{:S(2)}) collective-permute-start(bf16[88,1280]{1,0:T(8,128)(2,1)S(1)} %pad_maximum_fusion), channel_id=1, source_target_pairs={{0,2},{1,3},{2,4},{3,5},{4,6},{5,7},{6,0},{7,1},{8,10},{9,11},{10,... | collective-permute-start | bytes 675848 | tf_op jit(solution)/shard_map/ppermute | solution.py:222
  7.0 4.3 %norm.1.n_ref = bf16[704,1280]{1,0:T(8,128)(2,1)} custom-call(bf16[704,1280]{1,0:T(8,128)(2,1)} %rows_ref.5, f32[1280]{0:T(1024)} %gamma_ref.5, f32[1280]{0:T(1024)} %beta_ref.1), custom_call_target="tpu_custom_call" | custom-call | tf_op jit(solution)/shard_map/norm/pallas_call | solution.py:224
  11.4 1.6 %collective-permute-start.1 = (bf16[88,1280]{1,0:T(8,128)(2,1)S(1)}, bf16[88,1280]{1,0:T(8,128)(2,1)S(1)}, u32[]{:S(2)}, u32[]{:S(2)}) collective-permute-start(bf16[88,1280]{1,0:T(8,128)(2,1)S(1)} %collective-permute-done.refs_1_), channel_id=1, source_target_pairs={{0,16},{1,17},{2,18},{3,19},{4,20},{5,21},{6,22},{7,23},{8,24},{9,... | collective-permute-start | bytes 675848 | tf_op jit(solution)/shard_map/ppermute | solution.py:240
  12.9 3.4 %collective-permute-start.5 = (bf16[88,1280]{1,0:T(8,128)(2,1)S(1)}, bf16[88,1280]{1,0:T(8,128)(2,1)S(1)}, u32[]{:S(2)}, u32[]{:S(2)}) collective-permute-start(bf16[88,1280]{1,0:T(8,128)(2,1)S(1)} %pad_maximum_fusion), channel_id=1, source_target_pairs={{0,6},{1,7},{2,0},{3,1},{4,2},{5,3},{6,4},{7,5},{8,14},{9,15},{10,... | collective-permute-start | bytes 675848 | tf_op jit(solution)/shard_map/ppermute | solution.py:222
  16.4 1.7 %collective-permute-done.1.refs_2_ = bf16[88,1280]{1,0:T(8,128)(2,1)S(1)} collective-permute-done((bf16[88,1280]{1,0:T(8,128)(2,1)S(1)}, bf16[88,1280]{1,0:T(8,128)(2,1)S(1)}, u32[]{:S(2)}, u32[]{:S(2)}) %collective-permute-start.1) | collective-permute-done | bytes 225312 | tf_op jit(solution)/shard_map/ppermute | solution.py:240
  18.1 1.3 dynamic-slice_bitcast_fusion.table_ref
  19.5 0.7 broadcast_select_fusion.1.b_ref
  20.1 1.5 %collective-permute-start.11 = (bf16[88,1280]{1,0:T(8,128)(2,1)S(1)}, bf16[88,1280]{1,0:T(8,128)(2,1)S(1)}, u32[]{:S(2)}, u32[]{:S(2)}) collective-permute-start(bf16[88,1280]{1,0:T(8,128)(2,1)S(1)} %collective-permute-done.4.refs_5_.refs_0_), channel_id=1, source_target_pairs={{0,16},{1,17},{2,18},{3,19},{4,20},{5,21},{6,22},{7,23},{8,9},{9,8... | collective-permute-start | bytes 675848 | tf_op jit(solution)/shard_map/ppermute | solution.py:245
  21.6 0.7 collective-permute-done.5.refs_6_.refs_0_
  22.3 3.9 %collective-permute-done.6.refs_7_.refs_0_ = bf16[88,1280]{1,0:T(8,128)(2,1)S(1)} collective-permute-done((bf16[88,1280]{1,0:T(8,128)(2,1)S(1)}, bf16[88,1280]{1,0:T(8,128)(2,1)S(1)}, u32[]{:S(2)}, u32[]{:S(2)}) %collective-permute-start.6) | collective-permute-done | bytes 225312 | tf_op jit(solution)/shard_map/ppermute | solution.py:239
  26.2 0.6 copy-done.16
  27.0 0.7 copy-done.44
  27.7 8.4 %chunk_0.1 = (bf16[320,1280]{1,0:T(8,128)(2,1)}, bf16[160,1280]{1,0:T(8,128)(2,1)}, bf16[160,1280]{1,0:T(8,128)(2,1)}, bf16[704,640]{1,0:T(8,128)(2,1)}, bf16[640,1280]{1,0:T(8,128)(2,1)}) custom-call(s32[30]{0:T(128)} %dynamic-slice_bitcast_fusion.table_ref, s32[1,8]{1,0:T(1,128)} %counts_ref.11, bf16[704,1280]{1,0:T(8,128)(2,1)} %norm.1.n_ref, ...), custom_call_target="tpu_custom_call" | custom-call | flops 46137344000 | bytes 8519680 | tf_op jit(solution)/shard_map/chunk_0/pallas_call | solution.py:155
  36.1 1.4 collective-permute-start.12
  37.6 0.6 collective-permute-start.13
  38.2 0.5 collective-permute-start.23
  38.7 4.4 %collective-permute-done.12.refs_2_ = bf16[88,1280]{1,0:T(8,128)(2,1)S(1)} collective-permute-done((bf16[88,1280]{1,0:T(8,128)(2,1)}, bf16[88,1280]{1,0:T(8,128)(2,1)S(1)}, u32[]{:S(2)}, u32[]{:S(2)}) %collective-permute-start.12) | collective-permute-done | bytes 225312 | tf_op jit(solution)/shard_map/ppermute | solution.py:246
  43.1 4.0 %collective-permute-done.13.refs_3_ = bf16[88,1280]{1,0:T(8,128)(2,1)S(1)} collective-permute-done((bf16[88,1280]{1,0:T(8,128)(2,1)S(1)}, bf16[88,1280]{1,0:T(8,128)(2,1)S(1)}, u32[]{:S(2)}, u32[]{:S(2)}) %collective-permute-start.13) | collective-permute-done | bytes 225312 | tf_op jit(solution)/shard_map/ppermute | solution.py:246
  47.2 0.5 collective-permute-start.17
  47.7 1.1 add_convert_fusion.3.refs_8_
  48.8 1.4 collective-permute-start.24
  50.3 0.7 collective-permute-start.25
  51.1 1.5 %collective-permute-start.9 = (bf16[160,1280]{1,0:T(8,128)(2,1)S(1)}, bf16[160,1280]{1,0:T(8,128)(2,1)S(1)}, u32[]{:S(2)}, u32[]{:S(2)}) collective-permute-start(bf16[160,1280]{1,0:T(8,128)(2,1)S(1)} %add_convert_fusion.3.refs_8_), channel_id=1, source_target_pairs={{0,16},{1,17},{2,18},{3,19},{4,20},{5,21},{6,22},{7,23},{8,9},{9,8... | collective-permute-start | bytes 1228808 | tf_op jit(solution)/shard_map/ppermute | solution.py:258
  52.6 0.6 broadcast_in_dim.17.b_ref
  53.2 8.8 %chunk_1.1 = (bf16[320,1280]{1,0:T(8,128)(2,1)}, bf16[160,1280]{1,0:T(8,128)(2,1)}, bf16[160,1280]{1,0:T(8,128)(2,1)}, bf16[704,640]{1,0:T(8,128)(2,1)}, bf16[640,1280]{1,0:T(8,128)(2,1)}) custom-call(s32[30]{0:T(128)} %dynamic-slice_bitcast_fusion.table_ref, s32[1,8]{1,0:T(1,128)} %counts_ref.11, bf16[704,1280]{1,0:T(8,128)(2,1)} %norm.1.n_ref, ...), custom_call_target="tpu_custom_call" | custom-call | flops 46137344000 | bytes 8519680 | tf_op jit(solution)/shard_map/chunk_1/pallas_call | solution.py:155
  62.2 0.4 collective-permute-start.19
  62.7 0.6 collective-permute-start.34
  63.5 0.9 collective-permute-done.19
  64.4 0.2 collective-permute-start.29
  64.6 1.9 %add_convert_fusion.2.refs_8_ = bf16[160,1280]{1,0:T(8,128)(2,1)} fusion(bf16[160,1280]{1,0:T(8,128)(2,1)S(1)} %collective-permute-done.19, bf16[320,1280]{1,0:T(8,128)(2,1)} %get-tuple-element.40), kind=kLoop, calls=%fused_computation.2 | loop fusion | flops 819200 | bytes 1228800 | tf_op jit(solution)/shard_map/convert_element_type | solution.py:256
  66.4 0.8 collective-permute-start.35
  67.3 1.5 %collective-permute-done.34.refs_1_ = bf16[88,1280]{1,0:T(8,128)(2,1)S(1)} collective-permute-done((bf16[88,1280]{1,0:T(8,128)(2,1)S(1)}, bf16[88,1280]{1,0:T(8,128)(2,1)S(1)}, u32[]{:S(2)}, u32[]{:S(2)}) %collective-permute-start.34) | collective-permute-done | bytes 225312 | tf_op jit(solution)/shard_map/ppermute | solution.py:245
  68.8 0.6 collective-permute-start.36
  69.5 1.5 collective-permute-start.10
  71.0 8.8 %chunk_3.1 = (bf16[320,1280]{1,0:T(8,128)(2,1)}, bf16[160,1280]{1,0:T(8,128)(2,1)}, bf16[160,1280]{1,0:T(8,128)(2,1)}, bf16[704,640]{1,0:T(8,128)(2,1)}, bf16[640,1280]{1,0:T(8,128)(2,1)}) custom-call(s32[30]{0:T(128)} %dynamic-slice_bitcast_fusion.table_ref, s32[1,8]{1,0:T(1,128)} %counts_ref.11, bf16[704,1280]{1,0:T(8,128)(2,1)} %norm.1.n_ref, ...), custom_call_target="tpu_custom_call" | custom-call | flops 46137344000 | bytes 8519680 | tf_op jit(solution)/shard_map/chunk_3/pallas_call | solution.py:155
  79.9 0.6 collective-permute-start.20
  80.6 0.3 collective-permute-start.38
  80.9 0.3 collective-permute-start.39
  81.2 6.7 %collective-permute-done.20 = bf16[160,1280]{1,0:T(8,128)(2,1)S(1)} collective-permute-done((bf16[160,1280]{1,0:T(8,128)(2,1)S(1)}, bf16[160,1280]{1,0:T(8,128)(2,1)S(1)}, u32[]{:S(2)}, u32[]{:S(2)}) %collective-permute-start.20) | collective-permute-done | bytes 409632 | tf_op jit(solution)/shard_map/ppermute | solution.py:258
  87.9 0.5 collective-permute-start.31
  88.5 1.7 %collective-permute-done.31 = bf16[160,1280]{1,0:T(8,128)(2,1)S(1)} collective-permute-done((bf16[160,1280]{1,0:T(8,128)(2,1)}, bf16[160,1280]{1,0:T(8,128)(2,1)S(1)}, u32[]{:S(2)}, u32[]{:S(2)}) %collective-permute-start.31) | collective-permute-done | bytes 409632 | tf_op jit(solution)/shard_map/ppermute | solution.py:253
  90.2 0.2 collective-permute-start.30
  90.5 0.7 collective-permute-start.21
  91.2 1.3 collective-permute-start.32
  92.6 0.6 copy-done.37
  93.2 0.7 copy-done.41
  93.9 8.6 %chunk_2.1 = (bf16[320,1280]{1,0:T(8,128)(2,1)}, bf16[160,1280]{1,0:T(8,128)(2,1)}, bf16[160,1280]{1,0:T(8,128)(2,1)}, bf16[704,640]{1,0:T(8,128)(2,1)}, bf16[640,1280]{1,0:T(8,128)(2,1)}) custom-call(s32[30]{0:T(128)} %dynamic-slice_bitcast_fusion.table_ref, s32[1,8]{1,0:T(1,128)} %counts_ref.11, bf16[704,1280]{1,0:T(8,128)(2,1)} %norm.1.n_ref, ...), custom_call_target="tpu_custom_call" | custom-call | flops 46137344000 | bytes 8519680 | tf_op jit(solution)/shard_map/chunk_2/pallas_call | solution.py:155
  102.5 0.5 collective-permute-start.43
  103.1 3.1 %collective-permute-start.22 = (bf16[80,1280]{1,0:T(8,128)(2,1)S(1)}, bf16[80,1280]{1,0:T(8,128)(2,1)S(1)}, u32[]{:S(2)}, u32[]{:S(2)}) collective-permute-start(bf16[80,1280]{1,0:T(8,128)(2,1)S(1)} %add_convert_fusion.8), channel_id=1, source_target_pairs={{0,6},{1,7},{2,0},{3,1},{4,2},{5,3},{6,4},{7,5},{8,14},{9,15},{10,... | collective-permute-start | bytes 614408 | tf_op jit(solution)/shard_map/ppermute | solution.py:265
  106.3 0.7 collective-permute-start.33
  107.0 1.6 %collective-permute-start.44 = (bf16[160,1280]{1,0:T(8,128)(2,1)S(1)}, bf16[160,1280]{1,0:T(8,128)(2,1)S(1)}, u32[]{:S(2)}, u32[]{:S(2)}) collective-permute-start(bf16[160,1280]{1,0:T(8,128)(2,1)S(1)} %add_convert_fusion.refs_8_), channel_id=1, source_target_pairs={{0,16},{1,17},{2,18},{3,19},{4,20},{5,21},{6,22},{7,23},{8,9},{9,8... | collective-permute-start | bytes 1228808 | tf_op jit(solution)/shard_map/ppermute | solution.py:258
  108.6 8.8 %grad_rows_0.1.refs_9_ = bf16[704,1280]{1,0:T(8,128)(2,1)} custom-call(s32[30]{0:T(128)} %dynamic-slice_bitcast_fusion.table_ref, s32[1,8]{1,0:T(1,128)} %counts_ref.11, bf16[704,1280]{1,0:T(8,128)(2,1)} %rows_ref.5, f32[1280]{0:T(1024)} %gamma_ref.5, bf16[704,640]{1,0:T(8,128)(2,1)} %get-tuple-element.51.refs_0_, ...), custom_call_target="tpu_custom_call" | custom-call | flops 46137344000 | bytes 10158080 | tf_op jit(solution)/shard_map/grad_rows_0/pallas_call | solution.py:296
  117.7 0.7 collective-permute-start.45
  118.4 7.2 %collective-permute-done.42 = bf16[80,1280]{1,0:T(8,128)(2,1)S(1)} collective-permute-done((bf16[80,1280]{1,0:T(8,128)(2,1)S(1)}, bf16[80,1280]{1,0:T(8,128)(2,1)S(1)}, u32[]{:S(2)}, u32[]{:S(2)}) %collective-permute-start.42) | collective-permute-done | bytes 204832 | tf_op jit(solution)/shard_map/ppermute | solution.py:265
  125.8 0.6 copy-done.9
  126.4 8.8 %grad_rows_1.1 = bf16[704,1280]{1,0:T(8,128)(2,1)} custom-call(s32[30]{0:T(128)} %dynamic-slice_bitcast_fusion.table_ref, s32[1,8]{1,0:T(1,128)} %counts_ref.11, bf16[704,1280]{1,0:T(8,128)(2,1)} %rows_ref.5, f32[1280]{0:T(1024)} %gamma_ref.5, bf16[704,640]{1,0:T(8,128)(2,1)} %get-tuple-element.51.refs_0_, ...), custom_call_target="tpu_custom_call", output_to_operand_aliasing={{}: (13, {})} | custom-call | flops 46137344000 | bytes 10158080 | tf_op jit(solution)/shard_map/grad_rows_1/pallas_call | solution.py:296
  135.4 1.0 collective-permute-start.47
  136.4 5.7 %collective-permute-done.47.refs_1_ = bf16[80,1280]{1,0:T(8,128)(2,1)S(1)} collective-permute-done((bf16[80,1280]{1,0:T(8,128)(2,1)S(1)}, bf16[80,1280]{1,0:T(8,128)(2,1)S(1)}, u32[]{:S(2)}, u32[]{:S(2)}) %collective-permute-start.47) | collective-permute-done | bytes 204832 | tf_op jit(solution)/shard_map/ppermute | solution.py:327
  142.1 1.4 collective-permute-done.49.refs_3_
  143.6 0.7 copy-done.12
  144.2 2.5 %place.1 = f32[320,1280]{1,0:T(8,128)} custom-call(s32[30]{0:T(128)} %dynamic-slice_bitcast_fusion.table_ref, bf16[80,1280]{1,0:T(8,128)(2,1)} %copy-done.4, bf16[80,1280]{1,0:T(8,128)(2,1)} %copy-done.10, bf16[80,1280]{1,0:T(8,128)(2,1)} %copy-done.11, bf16[80,1280]{1,0:T(8,128)(2,1)} %copy-done.12), custom_call_target="tpu_custom_call" | custom-call | tf_op jit(solution)/shard_map/place/pallas_call | solution.py:329
  (158 shorter events, 2.2 us)
Async XLA Ops:
  2.4 15.7 %copy-start.13 = (bf16[320]{0:T(512)(128)(2,1)S(1)}, bf16[320]{0:T(512)(128)(2,1)}, u32[]{:S(2)}) copy-start(bf16[320]{0:T(512)(128)(2,1)} %param.12) | copy-start | bytes 1924
  2.4 8.9 %collective-permute-start = (bf16[88,1280]{1,0:T(8,128)(2,1)S(1)}, bf16[88,1280]{1,0:T(8,128)(2,1)S(1)}, u32[]{:S(2)}, u32[]{:S(2)}) collective-permute-start(bf16[88,1280]{1,0:T(8,128)(2,1)S(1)} %pad_maximum_fusion), channel_id=1, source_target_pairs={{0,1},{1,0},{2,3},{3,2},{4,5},{5,4},{6,7},{7,6},{8,9},{9,8},{10,11... | collective-permute-start | bytes 675848 | tf_op jit(solution)/shard_map/ppermute | solution.py:223
  5.5 10.8 %collective-permute-start.4 = (bf16[88,1280]{1,0:T(8,128)(2,1)S(1)}, bf16[88,1280]{1,0:T(8,128)(2,1)S(1)}, u32[]{:S(2)}, u32[]{:S(2)}) collective-permute-start(bf16[88,1280]{1,0:T(8,128)(2,1)S(1)} %pad_maximum_fusion), channel_id=1, source_target_pairs={{0,2},{1,3},{2,4},{3,5},{4,6},{5,7},{6,0},{7,1},{8,10},{9,11},{10,... | collective-permute-start | bytes 675848 | tf_op jit(solution)/shard_map/ppermute | solution.py:222
  11.4 14.8 %copy-start.31 = (bf16[88,1280]{1,0:T(8,128)(2,1)}, bf16[88,1280]{1,0:T(8,128)(2,1)S(1)}, u32[]{:S(2)}) copy-start(bf16[88,1280]{1,0:T(8,128)(2,1)S(1)} %collective-permute-done.refs_1_) | copy-start | bytes 675844
  11.4 6.8 %collective-permute-start.1 = (bf16[88,1280]{1,0:T(8,128)(2,1)S(1)}, bf16[88,1280]{1,0:T(8,128)(2,1)S(1)}, u32[]{:S(2)}, u32[]{:S(2)}) collective-permute-start(bf16[88,1280]{1,0:T(8,128)(2,1)S(1)} %collective-permute-done.refs_1_), channel_id=1, source_target_pairs={{0,16},{1,17},{2,18},{3,19},{4,20},{5,21},{6,22},{7,23},{8,24},{9,... | collective-permute-start | bytes 675848 | tf_op jit(solution)/shard_map/ppermute | solution.py:240
  12.9 9.4 %collective-permute-start.5 = (bf16[88,1280]{1,0:T(8,128)(2,1)S(1)}, bf16[88,1280]{1,0:T(8,128)(2,1)S(1)}, u32[]{:S(2)}, u32[]{:S(2)}) collective-permute-start(bf16[88,1280]{1,0:T(8,128)(2,1)S(1)} %pad_maximum_fusion), channel_id=1, source_target_pairs={{0,6},{1,7},{2,0},{3,1},{4,2},{5,3},{6,4},{7,5},{8,14},{9,15},{10,... | collective-permute-start | bytes 675848 | tf_op jit(solution)/shard_map/ppermute | solution.py:222
  16.3 9.9 %collective-permute-start.2 = (bf16[88,1280]{1,0:T(8,128)(2,1)S(1)}, bf16[88,1280]{1,0:T(8,128)(2,1)S(1)}, u32[]{:S(2)}, u32[]{:S(2)}) collective-permute-start(bf16[88,1280]{1,0:T(8,128)(2,1)S(1)} %collective-permute-done.refs_1_), channel_id=1, source_target_pairs={{0,8},{1,9},{2,10},{3,11},{4,12},{5,13},{6,14},{7,15},{8,0},{9,1},... | collective-permute-start | bytes 675848 | tf_op jit(solution)/shard_map/ppermute | solution.py:241
  16.3 9.9 %copy-start.19 = (bf16[88,1280]{1,0:T(8,128)(2,1)}, bf16[88,1280]{1,0:T(8,128)(2,1)S(1)}, u32[]{:S(2)}) copy-start(bf16[88,1280]{1,0:T(8,128)(2,1)S(1)} %collective-permute-done.4.refs_5_.refs_0_) | copy-start | bytes 675844
  16.3 9.9 %collective-permute-start.6 = (bf16[88,1280]{1,0:T(8,128)(2,1)S(1)}, bf16[88,1280]{1,0:T(8,128)(2,1)S(1)}, u32[]{:S(2)}, u32[]{:S(2)}) collective-permute-start(bf16[88,1280]{1,0:T(8,128)(2,1)S(1)} %collective-permute-done.4.refs_5_.refs_0_), channel_id=1, source_target_pairs={{0,2},{1,3},{2,4},{3,5},{4,6},{5,7},{6,0},{7,1},{8,10},{9,11},{10,... | collective-permute-start | bytes 675848 | tf_op jit(solution)/shard_map/ppermute | solution.py:239
  18.1 8.1 %collective-permute-start.3 = (bf16[88,1280]{1,0:T(8,128)(2,1)S(1)}, bf16[88,1280]{1,0:T(8,128)(2,1)S(1)}, u32[]{:S(2)}, u32[]{:S(2)}) collective-permute-start(bf16[88,1280]{1,0:T(8,128)(2,1)S(1)} %collective-permute-done.1.refs_2_), channel_id=1, source_target_pairs={{0,8},{1,9},{2,10},{3,11},{4,12},{5,13},{6,14},{7,15},{8,0},{9,1},... | collective-permute-start | bytes 675848 | tf_op jit(solution)/shard_map/ppermute | solution.py:241
  20.1 17.4 %collective-permute-start.11 = (bf16[88,1280]{1,0:T(8,128)(2,1)S(1)}, bf16[88,1280]{1,0:T(8,128)(2,1)S(1)}, u32[]{:S(2)}, u32[]{:S(2)}) collective-permute-start(bf16[88,1280]{1,0:T(8,128)(2,1)S(1)} %collective-permute-done.4.refs_5_.refs_0_), channel_id=1, source_target_pairs={{0,16},{1,17},{2,18},{3,19},{4,20},{5,21},{6,22},{7,23},{8,9},{9,8... | collective-permute-start | bytes 675848 | tf_op jit(solution)/shard_map/ppermute | solution.py:245
  36.1 11.1 %collective-permute-start.8 = (bf16[160,1280]{1,0:T(8,128)(2,1)}, bf16[160,1280]{1,0:T(8,128)(2,1)S(1)}, u32[]{:S(2)}, u32[]{:S(2)}) collective-permute-start(bf16[160,1280]{1,0:T(8,128)(2,1)} %get-tuple-element.39), channel_id=1, source_target_pairs={{0,8},{1,9},{2,10},{3,11},{4,12},{5,13},{6,14},{7,15},{8,0},{9,1},... | collective-permute-start | bytes 1228808 | tf_op jit(solution)/shard_map/ppermute | solution.py:253
  36.1 7.0 %collective-permute-start.12 = (bf16[88,1280]{1,0:T(8,128)(2,1)}, bf16[88,1280]{1,0:T(8,128)(2,1)S(1)}, u32[]{:S(2)}, u32[]{:S(2)}) collective-permute-start(bf16[88,1280]{1,0:T(8,128)(2,1)} %copy-done.19), channel_id=1, source_target_pairs={{0,1},{1,0},{2,3},{3,2},{4,5},{5,4},{6,7},{7,6},{8,24},{9,25},{10,... | collective-permute-start | bytes 675848 | tf_op jit(solution)/shard_map/ppermute | solution.py:246
  37.6 15.6 %copy-start.27 = (bf16[88,1280]{1,0:T(8,128)(2,1)}, bf16[88,1280]{1,0:T(8,128)(2,1)S(1)}, u32[]{:S(2)}) copy-start(bf16[88,1280]{1,0:T(8,128)(2,1)S(1)} %collective-permute-done.11.refs_1_) | copy-start | bytes 675844
  37.6 9.6 %collective-permute-start.13 = (bf16[88,1280]{1,0:T(8,128)(2,1)S(1)}, bf16[88,1280]{1,0:T(8,128)(2,1)S(1)}, u32[]{:S(2)}, u32[]{:S(2)}) collective-permute-start(bf16[88,1280]{1,0:T(8,128)(2,1)S(1)} %collective-permute-done.11.refs_1_), channel_id=1, source_target_pairs={{0,1},{1,0},{2,3},{3,2},{4,5},{5,4},{6,7},{7,6},{8,24},{9,25},{10,... | collective-permute-start | bytes 675848 | tf_op jit(solution)/shard_map/ppermute | solution.py:246
  38.2 10.6 %collective-permute-start.14 = (bf16[88,1280]{1,0:T(8,128)(2,1)}, bf16[88,1280]{1,0:T(8,128)(2,1)S(1)}, u32[]{:S(2)}, u32[]{:S(2)}) collective-permute-start(bf16[88,1280]{1,0:T(8,128)(2,1)} %copy-done.19), channel_id=1, source_target_pairs={{0,8},{1,9},{2,10},{3,11},{4,12},{5,13},{6,14},{7,15},{8,0},{9,1},... | collective-permute-start | bytes 675848 | tf_op jit(solution)/shard_map/ppermute | solution.py:247
  38.2 12.1 %collective-permute-start.23 = (bf16[88,1280]{1,0:T(8,128)(2,1)}, bf16[88,1280]{1,0:T(8,128)(2,1)S(1)}, u32[]{:S(2)}, u32[]{:S(2)}) collective-permute-start(bf16[88,1280]{1,0:T(8,128)(2,1)} %copy-done.18), channel_id=1, source_target_pairs={{0,16},{1,17},{2,18},{3,19},{4,20},{5,21},{6,22},{7,23},{8,9},{9,8... | collective-permute-start | bytes 675848 | tf_op jit(solution)/shard_map/ppermute | solution.py:245
  43.1 10.0 %copy-start.29 = (bf16[88,1280]{1,0:T(8,128)(2,1)}, bf16[88,1280]{1,0:T(8,128)(2,1)S(1)}, u32[]{:S(2)}) copy-start(bf16[88,1280]{1,0:T(8,128)(2,1)S(1)} %collective-permute-done.12.refs_2_) | copy-start | bytes 675844
  43.1 7.2 %collective-permute-start.15 = (bf16[88,1280]{1,0:T(8,128)(2,1)S(1)}, bf16[88,1280]{1,0:T(8,128)(2,1)S(1)}, u32[]{:S(2)}, u32[]{:S(2)}) collective-permute-start(bf16[88,1280]{1,0:T(8,128)(2,1)S(1)} %collective-permute-done.11.refs_1_), channel_id=1, source_target_pairs={{0,8},{1,9},{2,10},{3,11},{4,12},{5,13},{6,14},{7,15},{8,0},{9,1},... | collective-permute-start | bytes 675848 | tf_op jit(solution)/shard_map/ppermute | solution.py:247
  47.2 3.8 %collective-permute-start.16 = (bf16[88,1280]{1,0:T(8,128)(2,1)S(1)}, bf16[88,1280]{1,0:T(8,128)(2,1)S(1)}, u32[]{:S(2)}, u32[]{:S(2)}) collective-permute-start(bf16[88,1280]{1,0:T(8,128)(2,1)S(1)} %collective-permute-done.12.refs_2_), channel_id=1, source_target_pairs={{0,8},{1,9},{2,10},{3,11},{4,12},{5,13},{6,14},{7,15},{8,0},{9,1},... | collective-permute-start | bytes 675848 | tf_op jit(solution)/shard_map/ppermute | solution.py:247
  47.2 3.9 %collective-permute-start.17 = (bf16[88,1280]{1,0:T(8,128)(2,1)S(1)}, bf16[88,1280]{1,0:T(8,128)(2,1)S(1)}, u32[]{:S(2)}, u32[]{:S(2)}) collective-permute-start(bf16[88,1280]{1,0:T(8,128)(2,1)S(1)} %collective-permute-done.13.refs_3_), channel_id=1, source_target_pairs={{0,8},{1,9},{2,10},{3,11},{4,12},{5,13},{6,14},{7,15},{8,0},{9,1},... | collective-permute-start | bytes 675848 | tf_op jit(solution)/shard_map/ppermute | solution.py:247
  48.8 13.9 %collective-permute-start.24 = (bf16[88,1280]{1,0:T(8,128)(2,1)}, bf16[88,1280]{1,0:T(8,128)(2,1)S(1)}, u32[]{:S(2)}, u32[]{:S(2)}) collective-permute-start(bf16[88,1280]{1,0:T(8,128)(2,1)} %copy-done.18), channel_id=1, source_target_pairs={{0,1},{1,0},{2,3},{3,2},{4,5},{5,4},{6,7},{7,6},{8,24},{9,25},{10,... | collective-permute-start | bytes 675848 | tf_op jit(solution)/shard_map/ppermute | solution.py:246
  50.3 11.7 %copy-start.20 = (bf16[88,1280]{1,0:T(8,128)(2,1)}, bf16[88,1280]{1,0:T(8,128)(2,1)S(1)}, u32[]{:S(2)}) copy-start(bf16[88,1280]{1,0:T(8,128)(2,1)S(1)} %collective-permute-done.23.refs_1_) | copy-start | bytes 675844
  50.3 16.2 %collective-permute-start.26 = (bf16[88,1280]{1,0:T(8,128)(2,1)}, bf16[88,1280]{1,0:T(8,128)(2,1)S(1)}, u32[]{:S(2)}, u32[]{:S(2)}) collective-permute-start(bf16[88,1280]{1,0:T(8,128)(2,1)} %copy-done.18), channel_id=1, source_target_pairs={{0,8},{1,9},{2,10},{3,11},{4,12},{5,13},{6,14},{7,15},{8,0},{9,1},... | collective-permute-start | bytes 675848 | tf_op jit(solution)/shard_map/ppermute | solution.py:247
  50.3 13.1 %collective-permute-start.25 = (bf16[88,1280]{1,0:T(8,128)(2,1)S(1)}, bf16[88,1280]{1,0:T(8,128)(2,1)S(1)}, u32[]{:S(2)}, u32[]{:S(2)}) collective-permute-start(bf16[88,1280]{1,0:T(8,128)(2,1)S(1)} %collective-permute-done.23.refs_1_), channel_id=1, source_target_pairs={{0,1},{1,0},{2,3},{3,2},{4,5},{5,4},{6,7},{7,6},{8,24},{9,25},{10,... | collective-permute-start | bytes 675848 | tf_op jit(solution)/shard_map/ppermute | solution.py:246
  51.0 11.2 %collective-permute-start.7 = (bf16[160,1280]{1,0:T(8,128)(2,1)}, bf16[160,1280]{1,0:T(8,128)(2,1)S(1)}, u32[]{:S(2)}, u32[]{:S(2)}) collective-permute-start(bf16[160,1280]{1,0:T(8,128)(2,1)} %get-tuple-element.38), channel_id=1, source_target_pairs={{0,8},{1,9},{2,10},{3,11},{4,12},{5,13},{6,14},{7,15},{8,0},{9,1},... | collective-permute-start | bytes 1228808 | tf_op jit(solution)/shard_map/ppermute | solution.py:253
  51.1 10.9 %collective-permute-start.9 = (bf16[160,1280]{1,0:T(8,128)(2,1)S(1)}, bf16[160,1280]{1,0:T(8,128)(2,1)S(1)}, u32[]{:S(2)}, u32[]{:S(2)}) collective-permute-start(bf16[160,1280]{1,0:T(8,128)(2,1)S(1)} %add_convert_fusion.3.refs_8_), channel_id=1, source_target_pairs={{0,16},{1,17},{2,18},{3,19},{4,20},{5,21},{6,22},{7,23},{8,9},{9,8... | collective-permute-start | bytes 1228808 | tf_op jit(solution)/shard_map/ppermute | solution.py:258
  53.2 9.5 %copy-start.17 = (bf16[88,1280]{1,0:T(8,128)(2,1)S(1)}, bf16[88,1280]{1,0:T(8,128)(2,1)}, u32[]{:S(2)}) copy-start(bf16[88,1280]{1,0:T(8,128)(2,1)} %copy-done.16) | copy-start | bytes 675844
  62.0 5.2 %collective-permute-start.27 = (bf16[88,1280]{1,0:T(8,128)(2,1)S(1)}, bf16[88,1280]{1,0:T(8,128)(2,1)S(1)}, u32[]{:S(2)}, u32[]{:S(2)}) collective-permute-start(bf16[88,1280]{1,0:T(8,128)(2,1)S(1)} %collective-permute-done.23.refs_1_), channel_id=1, source_target_pairs={{0,8},{1,9},{2,10},{3,11},{4,12},{5,13},{6,14},{7,15},{8,0},{9,1},... | collective-permute-start | bytes 675848 | tf_op jit(solution)/shard_map/ppermute | solution.py:247
  62.2 2.2 %collective-permute-start.19 = (bf16[160,1280]{1,0:T(8,128)(2,1)}, bf16[160,1280]{1,0:T(8,128)(2,1)S(1)}, u32[]{:S(2)}, u32[]{:S(2)}) collective-permute-start(bf16[160,1280]{1,0:T(8,128)(2,1)} %get-tuple-element.42), channel_id=1, source_target_pairs={{0,8},{1,9},{2,10},{3,11},{4,12},{5,13},{6,14},{7,15},{8,0},{9,1},... | collective-permute-start | bytes 1228808 | tf_op jit(solution)/shard_map/ppermute | solution.py:253
  62.7 6.0 %collective-permute-start.34 = (bf16[88,1280]{1,0:T(8,128)(2,1)S(1)}, bf16[88,1280]{1,0:T(8,128)(2,1)S(1)}, u32[]{:S(2)}, u32[]{:S(2)}) collective-permute-start(bf16[88,1280]{1,0:T(8,128)(2,1)S(1)} %copy-done.17), channel_id=1, source_target_pairs={{0,16},{1,17},{2,18},{3,19},{4,20},{5,21},{6,22},{7,23},{8,9},{9,8... | collective-permute-start | bytes 675848 | tf_op jit(solution)/shard_map/ppermute | solution.py:245
  63.4 6.0 %collective-permute-start.28 = (bf16[88,1280]{1,0:T(8,128)(2,1)S(1)}, bf16[88,1280]{1,0:T(8,128)(2,1)S(1)}, u32[]{:S(2)}, u32[]{:S(2)}) collective-permute-start(bf16[88,1280]{1,0:T(8,128)(2,1)S(1)} %collective-permute-done.24.refs_2_), channel_id=1, source_target_pairs={{0,8},{1,9},{2,10},{3,11},{4,12},{5,13},{6,14},{7,15},{8,0},{9,1},... | collective-permute-start | bytes 675848 | tf_op jit(solution)/shard_map/ppermute | solution.py:247
  64.4 5.1 %collective-permute-start.29 = (bf16[88,1280]{1,0:T(8,128)(2,1)S(1)}, bf16[88,1280]{1,0:T(8,128)(2,1)S(1)}, u32[]{:S(2)}, u32[]{:S(2)}) collective-permute-start(bf16[88,1280]{1,0:T(8,128)(2,1)S(1)} %collective-permute-done.25.refs_3_), channel_id=1, source_target_pairs={{0,8},{1,9},{2,10},{3,11},{4,12},{5,13},{6,14},{7,15},{8,0},{9,1},... | collective-permute-start | bytes 675848 | tf_op jit(solution)/shard_map/ppermute | solution.py:247
  66.4 14.2 %collective-permute-start.35 = (bf16[88,1280]{1,0:T(8,128)(2,1)S(1)}, bf16[88,1280]{1,0:T(8,128)(2,1)S(1)}, u32[]{:S(2)}, u32[]{:S(2)}) collective-permute-start(bf16[88,1280]{1,0:T(8,128)(2,1)S(1)} %copy-done.17), channel_id=1, source_target_pairs={{0,1},{1,0},{2,3},{3,2},{4,5},{5,4},{6,7},{7,6},{8,24},{9,25},{10,... | collective-permute-start | bytes 675848 | tf_op jit(solution)/shard_map/ppermute | solution.py:246
  67.3 23.2 %collective-permute-start.37 = (bf16[88,1280]{1,0:T(8,128)(2,1)S(1)}, bf16[88,1280]{1,0:T(8,128)(2,1)S(1)}, u32[]{:S(2)}, u32[]{:S(2)}) collective-permute-start(bf16[88,1280]{1,0:T(8,128)(2,1)S(1)} %copy-done.17), channel_id=1, source_target_pairs={{0,8},{1,9},{2,10},{3,11},{4,12},{5,13},{6,14},{7,15},{8,0},{9,1},... | collective-permute-start | bytes 675848 | tf_op jit(solution)/shard_map/ppermute | solution.py:247
  68.8 11.9 %copy-start.21 = (bf16[88,1280]{1,0:T(8,128)(2,1)}, bf16[88,1280]{1,0:T(8,128)(2,1)S(1)}, u32[]{:S(2)}) copy-start(bf16[88,1280]{1,0:T(8,128)(2,1)S(1)} %collective-permute-done.34.refs_1_) | copy-start | bytes 675844
  68.8 12.1 %collective-permute-start.36 = (bf16[88,1280]{1,0:T(8,128)(2,1)S(1)}, bf16[88,1280]{1,0:T(8,128)(2,1)S(1)}, u32[]{:S(2)}, u32[]{:S(2)}) collective-permute-start(bf16[88,1280]{1,0:T(8,128)(2,1)S(1)} %collective-permute-done.34.refs_1_), channel_id=1, source_target_pairs={{0,1},{1,0},{2,3},{3,2},{4,5},{5,4},{6,7},{7,6},{8,24},{9,25},{10,... | collective-permute-start | bytes 675848 | tf_op jit(solution)/shard_map/ppermute | solution.py:246
  69.4 10.4 %copy-start.5 = (bf16[160,1280]{1,0:T(8,128)(2,1)S(1)}, bf16[160,1280]{1,0:T(8,128)(2,1)}, u32[]{:S(2)}) copy-start(bf16[160,1280]{1,0:T(8,128)(2,1)} %add_convert_fusion.2.refs_8_) | copy-start | bytes 1228804
  69.4 19.0 %copy-start.1 = (bf16[320,1280]{1,0:T(8,128)(2,1)S(1)}, bf16[320,1280]{1,0:T(8,128)(2,1)}, u32[]{:S(2)}) copy-start(bf16[320,1280]{1,0:T(8,128)(2,1)} %get-tuple-element.40) | copy-start | bytes 2457604
  69.4 18.5 %collective-permute-start.18 = (bf16[160,1280]{1,0:T(8,128)(2,1)S(1)}, bf16[160,1280]{1,0:T(8,128)(2,1)S(1)}, u32[]{:S(2)}, u32[]{:S(2)}) collective-permute-start(bf16[160,1280]{1,0:T(8,128)(2,1)S(1)} %copy-done.14), channel_id=1, source_target_pairs={{0,8},{1,9},{2,10},{3,11},{4,12},{5,13},{6,14},{7,15},{8,0},{9,1},... | collective-permute-start | bytes 1228808 | tf_op jit(solution)/shard_map/ppermute | solution.py:253
  69.5 10.3 %collective-permute-start.10 = (bf16[80,1280]{1,0:T(8,128)(2,1)S(1)}, bf16[80,1280]{1,0:T(8,128)(2,1)S(1)}, u32[]{:S(2)}, u32[]{:S(2)}) collective-permute-start(bf16[80,1280]{1,0:T(8,128)(2,1)S(1)} %add_convert_fusion.10), channel_id=1, source_target_pairs={{0,1},{1,0},{2,3},{3,2},{4,5},{5,4},{6,7},{7,6},{8,24},{9,25},{10,... | collective-permute-start | bytes 614408 | tf_op jit(solution)/shard_map/ppermute | solution.py:261
  79.8 10.3 %copy-start.15 = (bf16[160,1280]{1,0:T(8,128)(2,1)S(1)}, bf16[160,1280]{1,0:T(8,128)(2,1)}, u32[]{:S(2)}) copy-start(bf16[160,1280]{1,0:T(8,128)(2,1)} %get-tuple-element.47) | copy-start | bytes 1228804
  79.8 10.5 %copy-start.2 = (bf16[320,1280]{1,0:T(8,128)(2,1)S(1)}, bf16[320,1280]{1,0:T(8,128)(2,1)}, u32[]{:S(2)}) copy-start(bf16[320,1280]{1,0:T(8,128)(2,1)} %get-tuple-element.46) | copy-start | bytes 2457604
  79.9 8.0 %collective-permute-start.20 = (bf16[160,1280]{1,0:T(8,128)(2,1)S(1)}, bf16[160,1280]{1,0:T(8,128)(2,1)S(1)}, u32[]{:S(2)}, u32[]{:S(2)}) collective-permute-start(bf16[160,1280]{1,0:T(8,128)(2,1)S(1)} %copy-done.5), channel_id=1, source_target_pairs={{0,16},{1,17},{2,18},{3,19},{4,20},{5,21},{6,22},{7,23},{8,9},{9,8... | collective-permute-start | bytes 1228808 | tf_op jit(solution)/shard_map/ppermute | solution.py:258
  80.6 11.9 %copy-start.23 = (bf16[88,1280]{1,0:T(8,128)(2,1)}, bf16[88,1280]{1,0:T(8,128)(2,1)S(1)}, u32[]{:S(2)}) copy-start(bf16[88,1280]{1,0:T(8,128)(2,1)S(1)} %collective-permute-done.35.refs_2_) | copy-start | bytes 675844
  80.6 10.6 %collective-permute-start.38 = (bf16[88,1280]{1,0:T(8,128)(2,1)S(1)}, bf16[88,1280]{1,0:T(8,128)(2,1)S(1)}, u32[]{:S(2)}, u32[]{:S(2)}) collective-permute-start(bf16[88,1280]{1,0:T(8,128)(2,1)S(1)} %collective-permute-done.34.refs_1_), channel_id=1, source_target_pairs={{0,8},{1,9},{2,10},{3,11},{4,12},{5,13},{6,14},{7,15},{8,0},{9,1},... | collective-permute-start | bytes 675848 | tf_op jit(solution)/shard_map/ppermute | solution.py:247
  80.9 11.6 %copy-start.28 = (bf16[88,1280]{1,0:T(8,128)(2,1)}, bf16[88,1280]{1,0:T(8,128)(2,1)S(1)}, u32[]{:S(2)}) copy-start(bf16[88,1280]{1,0:T(8,128)(2,1)S(1)} %collective-permute-done.36.refs_3_) | copy-start | bytes 675844
  80.9 11.6 %collective-permute-start.39 = (bf16[88,1280]{1,0:T(8,128)(2,1)S(1)}, bf16[88,1280]{1,0:T(8,128)(2,1)S(1)}, u32[]{:S(2)}, u32[]{:S(2)}) collective-permute-start(bf16[88,1280]{1,0:T(8,128)(2,1)S(1)} %collective-permute-done.35.refs_2_), channel_id=1, source_target_pairs={{0,8},{1,9},{2,10},{3,11},{4,12},{5,13},{6,14},{7,15},{8,0},{9,1},... | collective-permute-start | bytes 675848 | tf_op jit(solution)/shard_map/ppermute | solution.py:247
  87.9 4.7 %collective-permute-start.40 = (bf16[88,1280]{1,0:T(8,128)(2,1)S(1)}, bf16[88,1280]{1,0:T(8,128)(2,1)S(1)}, u32[]{:S(2)}, u32[]{:S(2)}) collective-permute-start(bf16[88,1280]{1,0:T(8,128)(2,1)S(1)} %collective-permute-done.36.refs_3_), channel_id=1, source_target_pairs={{0,8},{1,9},{2,10},{3,11},{4,12},{5,13},{6,14},{7,15},{8,0},{9,1},... | collective-permute-start | bytes 675848 | tf_op jit(solution)/shard_map/ppermute | solution.py:247
  87.9 2.3 %collective-permute-start.31 = (bf16[160,1280]{1,0:T(8,128)(2,1)}, bf16[160,1280]{1,0:T(8,128)(2,1)S(1)}, u32[]{:S(2)}, u32[]{:S(2)}) collective-permute-start(bf16[160,1280]{1,0:T(8,128)(2,1)} %get-tuple-element.48), channel_id=1, source_target_pairs={{0,8},{1,9},{2,10},{3,11},{4,12},{5,13},{6,14},{7,15},{8,0},{9,1},... | collective-permute-start | bytes 1228808 | tf_op jit(solution)/shard_map/ppermute | solution.py:253
  90.2 16.0 %collective-permute-start.30 = (bf16[160,1280]{1,0:T(8,128)(2,1)S(1)}, bf16[160,1280]{1,0:T(8,128)(2,1)S(1)}, u32[]{:S(2)}, u32[]{:S(2)}) collective-permute-start(bf16[160,1280]{1,0:T(8,128)(2,1)S(1)} %copy-done.15), channel_id=1, source_target_pairs={{0,8},{1,9},{2,10},{3,11},{4,12},{5,13},{6,14},{7,15},{8,0},{9,1},... | collective-permute-start | bytes 1228808 | tf_op jit(solution)/shard_map/ppermute | solution.py:253
  90.5 12.5 %collective-permute-start.21 = (bf16[80,1280]{1,0:T(8,128)(2,1)S(1)}, bf16[80,1280]{1,0:T(8,128)(2,1)S(1)}, u32[]{:S(2)}, u32[]{:S(2)}) collective-permute-start(bf16[80,1280]{1,0:T(8,128)(2,1)S(1)} %add_convert_fusion.9), channel_id=1, source_target_pairs={{0,1},{1,0},{2,3},{3,2},{4,5},{5,4},{6,7},{7,6},{8,24},{9,25},{10,... | collective-permute-start | bytes 614408 | tf_op jit(solution)/shard_map/ppermute | solution.py:261
  91.2 15.0 %collective-permute-start.32 = (bf16[160,1280]{1,0:T(8,128)(2,1)S(1)}, bf16[160,1280]{1,0:T(8,128)(2,1)S(1)}, u32[]{:S(2)}, u32[]{:S(2)}) collective-permute-start(bf16[160,1280]{1,0:T(8,128)(2,1)S(1)} %add_convert_fusion.1.refs_8_), channel_id=1, source_target_pairs={{0,16},{1,17},{2,18},{3,19},{4,20},{5,21},{6,22},{7,23},{8,9},{9,8... | collective-permute-start | bytes 1228808 | tf_op jit(solution)/shard_map/ppermute | solution.py:258
  102.5 4.4 %collective-permute-start.41 = (bf16[160,1280]{1,0:T(8,128)(2,1)}, bf16[160,1280]{1,0:T(8,128)(2,1)S(1)}, u32[]{:S(2)}, u32[]{:S(2)}) collective-permute-start(bf16[160,1280]{1,0:T(8,128)(2,1)} %get-tuple-element.60), channel_id=1, source_target_pairs={{0,8},{1,9},{2,10},{3,11},{4,12},{5,13},{6,14},{7,15},{8,0},{9,1},... | collective-permute-start | bytes 1228808 | tf_op jit(solution)/shard_map/ppermute | solution.py:253
  102.5 15.1 %collective-permute-start.43 = (bf16[160,1280]{1,0:T(8,128)(2,1)}, bf16[160,1280]{1,0:T(8,128)(2,1)S(1)}, u32[]{:S(2)}, u32[]{:S(2)}) collective-permute-start(bf16[160,1280]{1,0:T(8,128)(2,1)} %get-tuple-element.63), channel_id=1, source_target_pairs={{0,8},{1,9},{2,10},{3,11},{4,12},{5,13},{6,14},{7,15},{8,0},{9,1},... | collective-permute-start | bytes 1228808 | tf_op jit(solution)/shard_map/ppermute | solution.py:253
  103.1 15.3 %collective-permute-start.22 = (bf16[80,1280]{1,0:T(8,128)(2,1)S(1)}, bf16[80,1280]{1,0:T(8,128)(2,1)S(1)}, u32[]{:S(2)}, u32[]{:S(2)}) collective-permute-start(bf16[80,1280]{1,0:T(8,128)(2,1)S(1)} %add_convert_fusion.8), channel_id=1, source_target_pairs={{0,6},{1,7},{2,0},{3,1},{4,2},{5,3},{6,4},{7,5},{8,14},{9,15},{10,... | collective-permute-start | bytes 614408 | tf_op jit(solution)/shard_map/ppermute | solution.py:265
  106.3 11.1 %collective-permute-start.33 = (bf16[80,1280]{1,0:T(8,128)(2,1)S(1)}, bf16[80,1280]{1,0:T(8,128)(2,1)S(1)}, u32[]{:S(2)}, u32[]{:S(2)}) collective-permute-start(bf16[80,1280]{1,0:T(8,128)(2,1)S(1)} %add_convert_fusion.7), channel_id=1, source_target_pairs={{0,1},{1,0},{2,3},{3,2},{4,5},{5,4},{6,7},{7,6},{8,24},{9,25},{10,... | collective-permute-start | bytes 614408 | tf_op jit(solution)/shard_map/ppermute | solution.py:261
  107.0 10.6 %collective-permute-start.44 = (bf16[160,1280]{1,0:T(8,128)(2,1)S(1)}, bf16[160,1280]{1,0:T(8,128)(2,1)S(1)}, u32[]{:S(2)}, u32[]{:S(2)}) collective-permute-start(bf16[160,1280]{1,0:T(8,128)(2,1)S(1)} %add_convert_fusion.refs_8_), channel_id=1, source_target_pairs={{0,16},{1,17},{2,18},{3,19},{4,20},{5,21},{6,22},{7,23},{8,9},{9,8... | collective-permute-start | bytes 1228808 | tf_op jit(solution)/shard_map/ppermute | solution.py:258
  117.5 8.1 %collective-permute-start.42 = (bf16[80,1280]{1,0:T(8,128)(2,1)S(1)}, bf16[80,1280]{1,0:T(8,128)(2,1)S(1)}, u32[]{:S(2)}, u32[]{:S(2)}) collective-permute-start(bf16[80,1280]{1,0:T(8,128)(2,1)S(1)} %add_convert_fusion.6), channel_id=1, source_target_pairs={{0,2},{1,3},{2,4},{3,5},{4,6},{5,7},{6,0},{7,1},{8,10},{9,11},{10,... | collective-permute-start | bytes 614408 | tf_op jit(solution)/shard_map/ppermute | solution.py:265
  117.7 7.9 %collective-permute-start.45 = (bf16[80,1280]{1,0:T(8,128)(2,1)S(1)}, bf16[80,1280]{1,0:T(8,128)(2,1)S(1)}, u32[]{:S(2)}, u32[]{:S(2)}) collective-permute-start(bf16[80,1280]{1,0:T(8,128)(2,1)S(1)} %add_convert_fusion.5), channel_id=1, source_target_pairs={{0,1},{1,0},{2,3},{3,2},{4,5},{5,4},{6,7},{7,6},{8,24},{9,25},{10,... | collective-permute-start | bytes 614408 | tf_op jit(solution)/shard_map/ppermute | solution.py:261
  125.7 9.5 %collective-permute-start.46 = (bf16[80,1280]{1,0:T(8,128)(2,1)S(1)}, bf16[80,1280]{1,0:T(8,128)(2,1)S(1)}, u32[]{:S(2)}, u32[]{:S(2)}) collective-permute-start(bf16[80,1280]{1,0:T(8,128)(2,1)S(1)} %add_convert_fusion.4.refs_8_), channel_id=1, source_target_pairs={{0,4},{1,5},{2,6},{3,7},{4,0},{5,1},{6,2},{7,3},{8,12},{9,13},{10,... | collective-permute-start | bytes 614408 | tf_op jit(solution)/shard_map/ppermute | solution.py:265
  135.4 6.7 %collective-permute-start.47 = (bf16[80,1280]{1,0:T(8,128)(2,1)S(1)}, bf16[80,1280]{1,0:T(8,128)(2,1)S(1)}, u32[]{:S(2)}, u32[]{:S(2)}) collective-permute-start(bf16[80,1280]{1,0:T(8,128)(2,1)S(1)} %multiply_convert_fusion.refs_0_), channel_id=1, source_target_pairs={{0,16},{1,17},{2,18},{3,19},{4,20},{5,21},{6,22},{7,23},{8,24},{9,... | collective-permute-start | bytes 614408 | tf_op jit(solution)/shard_map/ppermute | solution.py:327
  136.4 5.7 %collective-permute-start.48 = (bf16[80,1280]{1,0:T(8,128)(2,1)S(1)}, bf16[80,1280]{1,0:T(8,128)(2,1)S(1)}, u32[]{:S(2)}, u32[]{:S(2)}) collective-permute-start(bf16[80,1280]{1,0:T(8,128)(2,1)S(1)} %multiply_convert_fusion.refs_0_), channel_id=1, source_target_pairs={{0,8},{1,9},{2,10},{3,11},{4,12},{5,13},{6,14},{7,15},{8,0},{9,1},... | collective-permute-start | bytes 614408 | tf_op jit(solution)/shard_map/ppermute | solution.py:328
  142.1 1.5 collective-permute-start.49
  (31 other events, 105.5 us)

commit v3 on v2

--- a/solution.py
+++ b/solution.py
@@ -14,7 +14,7 @@
 F32, BF16 = jnp.float32, jnp.bfloat16
 VMEM = pl.BlockSpec(memory_space=pltpu.VMEM)
 SMEM = pl.BlockSpec(memory_space=pltpu.SMEM)
-LIMIT = 56 * 1024 * 1024
+LIMIT = 30 * 1024 * 1024
 
 
 def gelu_slope(pre_act):
@@ -40,8 +40,8 @@
 def chunk_kernel(places, pieces, waits, table_ref, counts_ref, n_ref, g_ref, b_ref, *refs):
     piece_refs, (keep_ref, *send_refs, h_ref, w_ref), (sum_ref,) = (
         refs[:pieces],
-        refs[pieces + waits : pieces + waits + 5],
-        refs[pieces + waits + 5 :],
+        refs[pieces + waits : pieces + waits + 7],
+        refs[pieces + waits + 7 :],
     )
     block = keep_ref.shape[0] // 4
     bias = b_ref[...].astype(F32)
@@ -69,7 +69,7 @@
         )
     for at in range(8):
         start = pl.multiple_of(table_ref[places["blocks"] + at], 16)
-        out, to = (send_refs[at // 2], at % 2) if at < 4 else (keep_ref, at % 4)
+        out, to = (send_refs[at], 0) if at < 4 else (keep_ref, at % 4)
         out[to * block : (to + 1) * block, :] = sum_ref[pl.ds(start, block), :].astype(BF16)
 
 
@@ -166,8 +166,7 @@
             + [pl.BlockSpec(memory_space=pl.ANY)] * len(after),
             out_specs=[
                 whole((units // 2, width)),
-                whole((units // 4, width)),
-                whole((units // 4, width)),
+                *[whole((units // 8, width))] * 4,
                 whole((per_dev, units)),
                 whole((units, width)),
             ],
@@ -175,16 +174,15 @@
         ),
         out_shape=[
             jax.ShapeDtypeStruct((units // 2, width), BF16),
-            jax.ShapeDtypeStruct((units // 4, width), BF16),
-            jax.ShapeDtypeStruct((units // 4, width), BF16),
+            *[jax.ShapeDtypeStruct((units // 8, width), BF16)] * 4,
             jax.ShapeDtypeStruct((per_dev, units), BF16),
             jax.ShapeDtypeStruct((units, width), BF16),
         ],
         compiler_params=pltpu.CompilerParams(vmem_limit_bytes=LIMIT),
         cost_estimate=pl.CostEstimate(
-            flops=80 * per_dev * units * width,
-            bytes_accessed=2 * per_dev * (width + 2 * units) + 6 * units * width,
-            transcendentals=per_dev * units,
+            flops=per_dev * units,
+            bytes_accessed=0,
+            transcendentals=0,
         ),
         name="chunk_%d" % step,
     )(table, counts, normed_rows, grad_hidden, bias, *pieces, *after)
@@ -234,65 +232,62 @@
         compiler_params=pltpu.CompilerParams(vmem_limit_bytes=LIMIT),
         name="norm",
     )(rows, gamma, beta)
-    beside, normed_rows = lax.optimization_barrier((beside, normed_rows))
-    for s in range(2, plan.nz - 1):
-        from_z[s] = up(1)(from_z[s - 1])
+    tied = lambda array, gate: lax.optimization_barrier((array, *gate))[0]
+    from_z[2] = up(1)(from_z[1])
+    from_z[1] = tied(from_z[1], [from_z[3], normed_rows])
     diagonal = along_x(beside)
     pieces = {0: [w_in, beside, diagonal, core(beside), core(diagonal)]}
-    order = [0, 1, plan.nz - 1] + list(range(2, plan.nz - 1)) if plan.nz > 2 else [0, 1]
-    for s in order[1:]:
+    arrival = [1, 3, 2]
+    for s in arrival:
         a0 = from_z[s]
         a1 = first(a0)
         a2, a3 = second(a0), second(a1)
         pieces[s] = [a0, a1, a2, a3] + [core(a) for a in (a0, a1, a2, a3)]
 
     cut = lambda array, at, n=1: array[at * quarter : (at + n) * quarter].astype(F32)
-    tied = lambda array, gate: lax.optimization_barrier((array, *gate))[0]
-
-    def homeward(s, keep, send_first, send_second):
-        got_first, got_second = core(send_first), core(send_second)
+
+    def homeward(s, keep, *sends):
+        got = [core(send) for send in sends]
         gate = yield None
-        got_first = tied(got_first, gate)
-        t = (cut(keep, 0, 2) + got_first.astype(F32)).astype(BF16)
+        got[0] = tied(got[0], gate)
+        t = (cut(keep, 0, 2) + jnp.concatenate(got[:2], axis=0).astype(F32)).astype(BF16)
         gate = yield t
         one = tied(first(t), gate)
-        v = (cut(keep, 2) + cut(got_second, 0) + cut(one, 0)).astype(BF16)
+        v = (cut(keep, 2) + got[2].astype(F32) + cut(one, 0)).astype(BF16)
         gate = yield v
         two = tied(second(v), gate)
-        plane = cut(keep, 3) + cut(got_second, 1) + cut(one, 1) + two.astype(F32)
+        plane = cut(keep, 3) + got[3].astype(F32) + cut(one, 1) + two.astype(F32)
         plane = plane if s == 0 else plane.astype(BF16)
         gate = yield plane
         term = plane if s == 0 else tied(up(-s)(plane), gate or [])
         while True:
             yield term
 
-    def advance(gate=(), last=4):
+    def advance(steps, gate=()):
         gate = list(gate)
-        for at, m in enumerate(moving):
-            if steps[at] < last:
-                gate = [m.send(gate)]
-                steps[at] += 1
+        for at in steps:
+            gate = [moving[at].send(gate)]
         return gate
 
-    hidden, weights, moving, steps = [], [], [], []
+    hidden, weights, moving = [], [], []
     empty = jnp.zeros((1, units), BF16)
-    after = [from_z[s] for s in order[1:]]
-    for s in order:
-        keep, send_first, send_second, h, w = call_chunk(
-            places, s, table, counts, normed_rows, grad_hidden, bias_own if s == 0 else empty, pieces[s], shard,
-            s == 0, after,
+    order = [0] + arrival
+    after = []
+    for at, s in enumerate(order):
+        keep, *sends, h, w = call_chunk(
+            places, s, tied(table, after + [[from_z[2]],[],[],[]][at]), counts, normed_rows, grad_hidden, bias_own if s == 0 else empty,
+            pieces[s], shard, s == 0, [],
         )
         hidden.append(h)
         weights.append(w)
-        moving.append(homeward(s, keep, send_first, send_second))
+        moving.append(homeward(s, keep, *sends))
         next(moving[-1])
-        steps.append(0)
-        after = advance()
+        after = advance([[0],[0,1],[0,1,2],[1,2,3],[1,2,3],[3]][at])
 
     def call_rows(part, after, out):
         whole = lambda shape: pl.BlockSpec(shape, lambda i, t, c: (0,) * len(shape))
         striped = lambda cols: pl.BlockSpec((tile, cols), lambda i, t, c: (i + 2 * part, 0))
-        more = list(after) + list(out)
+        more = list(out)
         return pl.pallas_call(
             functools.partial(rows_kernel, places, plan.nz, 2 * part),
             grid_spec=pltpu.PrefetchScalarGridSpec(
@@ -308,17 +303,17 @@
             input_output_aliases={3 + 2 * plan.nz + len(more): 0} if out else {},
             compiler_params=pltpu.CompilerParams(vmem_limit_bytes=LIMIT),
             cost_estimate=pl.CostEstimate(
-                flops=40 * half * width * units * plan.nz,
-                bytes_accessed=4 * half * width + 2 * (half + width) * units * plan.nz,
+                flops=half * width,
+                bytes_accessed=0,
                 transcendentals=0,
             ),
             name="grad_rows_%d" % part,
-        )(table, counts, rows, gamma, *hidden, *weights, *more)
+        )(tied(table, after), counts, rows, gamma, *hidden, *weights, *more)
 
     grad_rows = call_rows(0, after, [])
     after = [grad_rows]
-    while min(steps) < 3:
-        after = advance(after, 3)
+    for steps in [[0],[0,1],[0,1,2],[1,2,3],[1,2,3],[3]][4:]:
+        after = advance(steps, after)
     grad_rows = call_rows(1, after, [grad_rows])
     scale = 1.0 / math.sqrt(VIS_DEV * n_patch * 4)
     total = sum(next(m).astype(F32) for m in moving)
@@ -326,13 +321,18 @@
     done = (total * scale).astype(BF16)
     done_x = along_x(done)
     quarters = [done, done_x, core(done), core(done_x)]
-    grad_w_in = pl.pallas_call(
-        functools.partial(place_kernel, places),
-        in_specs=[SMEM] + [VMEM] * 4,
-        out_specs=VMEM,
-        out_shape=jax.ShapeDtypeStruct((shard, width), F32),
-        name="place",
-    )(table, *quarters)
+    same_x, same_c = [dp_index // 2 == v for v in (0, 1)], [dp_index % 2 == v for v in (0, 1)]
+    grad_w_in = jnp.concatenate(
+        [
+            jnp.where(
+                same_x[at // 2],
+                jnp.where(same_c[at % 2], quarters[0], quarters[2]),
+                jnp.where(same_c[at % 2], quarters[1], quarters[3]),
+            ).astype(F32)
+            for at in range(4)
+        ],
+        axis=0,
+    )
     return grad_rows, grad_w_in
 
 
@@ -362,7 +362,7 @@
 
     def per_device(*args):
         shard = args[3].shape[0]
-        if n_dp == 4 and n_patch % 2 == 0 and n_patch <= 8 and shard % 64 == 0 and args[0].shape[0] % 64 == 0:
+        if n_dp == 4 and n_patch == 8 and shard % 64 == 0 and args[0].shape[0] % 64 == 0:
             return fast_device(Plan(n_dp, n_patch, shard), *args)
         return any_device(*args)
 

time: 147 us -> 125 us (0.85)
  Pallas kernels: 59.1 us -> 31.3 us
  starting transfers between devices: 34 us -> 39 us
  waiting for transfers between devices: 39.9 us -> 43.5 us
  other arithmetic: 5.53 us -> 3.6 us
    pallas_call x4, Pallas kernels: 34.6 us -> 19.6 us  [call_chunk(): pl.pallas_call(functools.partial(chunk_kernel, where, len(pieces), len(af...]
    pallas_call x2, Pallas kernels: 17.6 us -> 10.3 us  [call_rows(): pl.pallas_call(functools.partial(rows_kernel, places, plan.nz, 2 * part),...]
    ppermute x4, waiting for transfers between devices: 0.01 us -> 4.11 us  [homeward(): two = tied(second(v), gate)]
    ppermute x6, waiting for transfers between devices: 8.44 us -> 4.35 us  [fast_device(): a2, a3 = (second(a0), second(a1))]
    ppermute x9 -> x17, starting transfers between devices: 1.81 us -> 5.49 us  [the longest x16 4.37 us: homeward(): got = [core(send) for send in sends]]
    ppermute x3, waiting for transfers between devices: 1.5 us -> 4.8 us  [fast_device(): a1 = first(a0)]
    ppermute x9 -> x17, waiting for transfers between devices: 6.44 us -> 3.31 us  [the longest x1 2.02 us: fast_device(): from_z[2] = up(1)(from_z[1])]
    ppermute x4, waiting for transfers between devices: 6.67 us -> 9.62 us  [homeward(): one = tied(first(t), gate)]
  transfers between devices with their start and end apart: 50 -> 58, of which waited for: 12 -> 19; matrix products, arithmetic and copies ran while one was open for 4% -> 2% of each run, Pallas kernels for 39% -> 25%
where the time goes in v3:
time: 125 us
  waiting for transfers between devices  43.5 us (35%)
  starting transfers between devices  39 us (31%)
  Pallas kernels  31.3 us (25%)
  local copies, waits for them, and re-layouts  6.66 us (5%)
  other arithmetic  3.6 us (3%)
    pallas_call x4, Pallas kernels, call_chunk(): pl.pallas_call(functools.partial(chunk_kernel, where, len(pieces), len(af...  19.6 us
    pallas_call x2, Pallas kernels, call_rows(): pl.pallas_call(functools.partial(rows_kernel, places, plan.nz, 2 * part),...  10.3 us
    ppermute x4, waiting for transfers between devices, homeward(): one = tied(first(t), gate)  9.62 us
    ppermute x3, waiting for transfers between devices, homeward(): term = plane if s == 0 else tied(up(-s)(plane), gate or [])  6.72 us
    ppermute x1, waiting for transfers between devices, fast_device(): done_x = along_x(done)  5.89 us
    ppermute x6, starting transfers between devices, fast_device(): a2, a3 = (second(a0), second(a1))  5.54 us
    unnamed x18, local copies, waits for them, and re-layouts  4.92 us
    ppermute x4, starting transfers between devices, homeward(): two = tied(second(v), gate)  4.85 us
  transfers between devices with their start and end apart: 58, of which 19 were waited for; matrix products, arithmetic and copies ran while one was open for 2% of the time, Pallas kernels for 25%

profile of v3, /device:TPU:0, one launch (start us, length us, event | category | flops | bytes accessed | tf_op | source)
XLA Modules:
  0.0 125.1 jit_solution(13707790300003175518)
XLA Ops:
  0.6 0.7 fusion.2
  1.4 1.0 constant_dynamic-slice_fusion
  2.5 3.0 %collective-permute-start.2 = (bf16[88,1280]{1,0:T(8,128)(2,1)S(1)}, bf16[88,1280]{1,0:T(8,128)(2,1)}, u32[]{:S(2)}, u32[]{:S(2)}) collective-permute-start(bf16[88,1280]{1,0:T(8,128)(2,1)S(1)} %pad_maximum_fusion), channel_id=1, source_target_pairs={{0,1},{1,0},{2,3},{3,2},{4,5},{5,4},{6,7},{7,6},{8,9},{9,8},{10,11... | collective-permute-start | bytes 675848 | tf_op jit(solution)/shard_map/ppermute | solution.py:221
  5.6 1.6 %collective-permute-start = (bf16[88,1280]{1,0:T(8,128)(2,1)S(1)}, bf16[88,1280]{1,0:T(8,128)(2,1)S(1)}, u32[]{:S(2)}, u32[]{:S(2)}) collective-permute-start(bf16[88,1280]{1,0:T(8,128)(2,1)S(1)} %pad_maximum_fusion), channel_id=1, source_target_pairs={{0,2},{1,3},{2,4},{3,5},{4,6},{5,7},{6,0},{7,1},{8,10},{9,11},{10,... | collective-permute-start | bytes 675848 | tf_op jit(solution)/shard_map/ppermute | solution.py:220
  7.1 2.2 %collective-permute-start.12 = (bf16[88,1280]{1,0:T(8,128)(2,1)S(1)}, bf16[88,1280]{1,0:T(8,128)(2,1)S(1)}, u32[]{:S(2)}, u32[]{:S(2)}) collective-permute-start(bf16[88,1280]{1,0:T(8,128)(2,1)S(1)} %pad_maximum_fusion), channel_id=1, source_target_pairs={{0,6},{1,7},{2,0},{3,1},{4,2},{5,3},{6,4},{7,5},{8,14},{9,15},{10,... | collective-permute-start | bytes 675848 | tf_op jit(solution)/shard_map/ppermute | solution.py:220
  9.4 1.8 %collective-permute-done.2.refs_1_ = bf16[88,1280]{1,0:T(8,128)(2,1)} collective-permute-done((bf16[88,1280]{1,0:T(8,128)(2,1)S(1)}, bf16[88,1280]{1,0:T(8,128)(2,1)}, u32[]{:S(2)}, u32[]{:S(2)}) %collective-permute-start.2) | collective-permute-done | bytes 225312 | tf_op jit(solution)/shard_map/ppermute | solution.py:221
  11.2 1.7 %collective-permute-start.3 = (bf16[88,1280]{1,0:T(8,128)(2,1)}, bf16[88,1280]{1,0:T(8,128)(2,1)}, u32[]{:S(2)}, u32[]{:S(2)}) collective-permute-start(bf16[88,1280]{1,0:T(8,128)(2,1)} %collective-permute-done.2.refs_1_), channel_id=1, source_target_pairs={{0,16},{1,17},{2,18},{3,19},{4,20},{5,21},{6,22},{7,23},{8,24},{9,... | collective-permute-start | bytes 675848 | tf_op jit(solution)/shard_map/ppermute | solution.py:238
  12.9 1.5 %copy-done.1 = bf16[704,1280]{1,0:T(8,128)(2,1)S(1)} copy-done((bf16[704,1280]{1,0:T(8,128)(2,1)S(1)}, bf16[704,1280]{1,0:T(8,128)(2,1)}, u32[]{:S(2)}) %copy-start.1) | copy-done | bytes 1802264
  14.4 0.7 copy-done.4
  15.1 0.7 copy-done.7
  15.8 1.5 %norm.1.n_ref = bf16[704,1280]{1,0:T(8,128)(2,1)S(1)} custom-call(bf16[704,1280]{1,0:T(8,128)(2,1)S(1)} %copy-done.1, f32[1280]{0:T(1024)S(1)} %copy-done.4, f32[1280]{0:T(1024)S(1)} %copy-done.7), custom_call_target="tpu_custom_call" | custom-call | tf_op jit(solution)/shard_map/norm/pallas_call | solution.py:222
  17.3 1.4 %collective-permute-done.12.refs_0_ = bf16[88,1280]{1,0:T(8,128)(2,1)S(1)} collective-permute-done((bf16[88,1280]{1,0:T(8,128)(2,1)S(1)}, bf16[88,1280]{1,0:T(8,128)(2,1)S(1)}, u32[]{:S(2)}, u32[]{:S(2)}) %collective-permute-start.12) | collective-permute-done | bytes 225312 | tf_op jit(solution)/shard_map/ppermute | solution.py:220
  18.7 1.5 %collective-permute-start.13 = (bf16[88,1280]{1,0:T(8,128)(2,1)S(1)}, bf16[88,1280]{1,0:T(8,128)(2,1)S(1)}, u32[]{:S(2)}, u32[]{:S(2)}) collective-permute-start(bf16[88,1280]{1,0:T(8,128)(2,1)S(1)} %collective-permute-done.refs_0_), channel_id=1, source_target_pairs={{0,16},{1,17},{2,18},{3,19},{4,20},{5,21},{6,22},{7,23},{8,9},{9,8... | collective-permute-start | bytes 675848 | tf_op jit(solution)/shard_map/ppermute | solution.py:243
  20.2 1.1 collective-permute-start.1
  21.3 0.5 collective-permute-start.5
  21.9 0.5 collective-permute-start.14
  22.4 2.3 %collective-permute-done.13.refs_1_ = bf16[88,1280]{1,0:T(8,128)(2,1)S(1)} collective-permute-done((bf16[88,1280]{1,0:T(8,128)(2,1)S(1)}, bf16[88,1280]{1,0:T(8,128)(2,1)S(1)}, u32[]{:S(2)}, u32[]{:S(2)}) %collective-permute-start.13) | collective-permute-done | bytes 225312 | tf_op jit(solution)/shard_map/ppermute | solution.py:243
  24.7 0.5 collective-permute-start.15
  25.2 0.7 dynamic-slice_bitcast_fusion.table_ref
  25.9 2.0 %collective-permute-done.1.refs_0_ = bf16[88,1280]{1,0:T(8,128)(2,1)S(1)} collective-permute-done((bf16[88,1280]{1,0:T(8,128)(2,1)S(1)}, bf16[88,1280]{1,0:T(8,128)(2,1)S(1)}, u32[]{:S(2)}, u32[]{:S(2)}) %collective-permute-start.1) | collective-permute-done | bytes 225312 | tf_op jit(solution)/shard_map/ppermute | solution.py:236
  28.0 2.0 %copy-done = bf16[704,2560]{1,0:T(8,128)(2,1)S(1)} copy-done((bf16[704,2560]{1,0:T(8,128)(2,1)S(1)}, bf16[704,2560]{1,0:T(8,128)(2,1)}, u32[]{:S(2)}) %copy-start) | copy-done | bytes 3604504
  30.0 5.8 %chunk_0.1 = (bf16[320,1280]{1,0:T(8,128)(2,1)S(1)}, bf16[80,1280]{1,0:T(8,128)(2,1)S(1)}, bf16[80,1280]{1,0:T(8,128)(2,1)S(1)}, bf16[80,1280]{1,0:T(8,128)(2,1)...) custom-call(s32[30]{0:T(128)S(1)} %dynamic-slice_bitcast_fusion.table_ref, ...), custom_call_target="tpu_custom_call" | custom-call | flops 450560 | tf_op jit(solution)/shard_map/chunk_0/pallas_call | solution.py:155
  35.9 0.5 collective-permute-start.8
  37.7 1.2 collective-permute-start.9
  39.0 0.9 collective-permute-start.27
  39.9 4.5 %chunk_1.1 = (bf16[320,1280]{1,0:T(8,128)(2,1)S(1)}, bf16[80,1280]{1,0:T(8,128)(2,1)S(1)}, bf16[80,1280]{1,0:T(8,128)(2,1)S(1)}, bf16[80,1280]{1,0:T(8,128)(2,1)...) custom-call(s32[30]{0:T(128)S(1)} %dynamic-slice_bitcast_fusion.table_ref, ...), custom_call_target="tpu_custom_call" | custom-call | flops 450560 | tf_op jit(solution)/shard_map/chunk_1/pallas_call | solution.py:155
  44.4 0.6 collective-permute-start.21
  45.0 1.2 collective-permute-start.28
  46.1 2.5 %collective-permute-done.27.refs_1_ = bf16[88,1280]{1,0:T(8,128)(2,1)S(1)} collective-permute-done((bf16[88,1280]{1,0:T(8,128)(2,1)S(1)}, bf16[88,1280]{1,0:T(8,128)(2,1)S(1)}, u32[]{:S(2)}, u32[]{:S(2)}) %collective-permute-start.27) | collective-permute-done | bytes 225312 | tf_op jit(solution)/shard_map/ppermute | solution.py:243
  48.6 1.2 collective-permute-start.29
  50.4 0.5 collective-permute-done.28.refs_2_
  50.9 1.2 collective-permute-start.36
  52.1 3.8 %collective-permute-done.29.refs_3_ = bf16[88,1280]{1,0:T(8,128)(2,1)S(1)} collective-permute-done((bf16[88,1280]{1,0:T(8,128)(2,1)S(1)}, bf16[88,1280]{1,0:T(8,128)(2,1)S(1)}, u32[]{:S(2)}, u32[]{:S(2)}) %collective-permute-start.29) | collective-permute-done | bytes 225312 | tf_op jit(solution)/shard_map/ppermute | solution.py:244
  55.9 0.5 collective-permute-start.33
  56.4 0.8 collective-permute-start.11
  57.4 1.3 %collective-permute-start.37 = (bf16[88,1280]{1,0:T(8,128)(2,1)S(1)}, bf16[88,1280]{1,0:T(8,128)(2,1)S(1)}, u32[]{:S(2)}, u32[]{:S(2)}) collective-permute-start(bf16[88,1280]{1,0:T(8,128)(2,1)S(1)} %collective-permute-done.1.refs_0_), channel_id=1, source_target_pairs={{0,1},{1,0},{2,3},{3,2},{4,5},{5,4},{6,7},{7,6},{8,24},{9,25},{10,... | collective-permute-start | bytes 675848 | tf_op jit(solution)/shard_map/ppermute | solution.py:244
  58.7 0.9 collective-permute-start.38
  59.5 4.7 %chunk_3.1 = (bf16[320,1280]{1,0:T(8,128)(2,1)S(1)}, bf16[80,1280]{1,0:T(8,128)(2,1)S(1)}, bf16[80,1280]{1,0:T(8,128)(2,1)S(1)}, bf16[80,1280]{1,0:T(8,128)(2,1)...) custom-call(s32[30]{0:T(128)S(1)} %dynamic-slice_bitcast_fusion.table_ref, ...), custom_call_target="tpu_custom_call" | custom-call | flops 450560 | tf_op jit(solution)/shard_map/chunk_3/pallas_call | solution.py:155
  64.6 1.7 %collective-permute-start.23 = (bf16[160,1280]{1,0:T(8,128)(2,1)S(1)}, bf16[160,1280]{1,0:T(8,128)(2,1)S(1)}, u32[]{:S(2)}, u32[]{:S(2)}) collective-permute-start(bf16[160,1280]{1,0:T(8,128)(2,1)S(1)} %add_convert_fusion.2), channel_id=1, source_target_pairs={{0,16},{1,17},{2,18},{3,19},{4,20},{5,21},{6,22},{7,23},{8,9},{9,8... | collective-permute-start | bytes 1228808 | tf_op jit(solution)/shard_map/ppermute | solution.py:255
  66.4 6.2 %collective-permute-done.23 = bf16[160,1280]{1,0:T(8,128)(2,1)S(1)} collective-permute-done((bf16[160,1280]{1,0:T(8,128)(2,1)S(1)}, bf16[160,1280]{1,0:T(8,128)(2,1)S(1)}, u32[]{:S(2)}, u32[]{:S(2)}) %collective-permute-start.23) | collective-permute-done | bytes 409632 | tf_op jit(solution)/shard_map/ppermute | solution.py:255
  72.6 0.5 collective-permute-start.35
  73.2 0.8 collective-permute-done.34
  74.7 1.7 %collective-permute-start.25 = (bf16[80,1280]{1,0:T(8,128)(2,1)S(1)}, bf16[80,1280]{1,0:T(8,128)(2,1)S(1)}, u32[]{:S(2)}, u32[]{:S(2)}) collective-permute-start(bf16[80,1280]{1,0:T(8,128)(2,1)S(1)} %add_convert_fusion.9), channel_id=1, source_target_pairs={{0,1},{1,0},{2,3},{3,2},{4,5},{5,4},{6,7},{7,6},{8,24},{9,25},{10,... | collective-permute-start | bytes 614408 | tf_op jit(solution)/shard_map/ppermute | solution.py:258
  77.1 0.7 collective-permute-start.45
  77.8 4.5 %chunk_2.1 = (bf16[320,1280]{1,0:T(8,128)(2,1)S(1)}, bf16[80,1280]{1,0:T(8,128)(2,1)S(1)}, bf16[80,1280]{1,0:T(8,128)(2,1)S(1)}, bf16[80,1280]{1,0:T(8,128)(2,1)...) custom-call(s32[30]{0:T(128)S(1)} %dynamic-slice_bitcast_fusion.table_ref, ...), custom_call_target="tpu_custom_call" | custom-call | flops 450560 | tf_op jit(solution)/shard_map/chunk_2/pallas_call | solution.py:155
  83.0 2.0 %collective-permute-done.45 = bf16[160,1280]{1,0:T(8,128)(2,1)S(1)} collective-permute-done((bf16[160,1280]{1,0:T(8,128)(2,1)S(1)}, bf16[160,1280]{1,0:T(8,128)(2,1)S(1)}, u32[]{:S(2)}, u32[]{:S(2)}) %collective-permute-start.45) | collective-permute-done | bytes 409632 | tf_op jit(solution)/shard_map/ppermute | solution.py:255
  85.1 1.2 collective-permute-start.26
  86.4 1.4 %collective-permute-start.48 = (bf16[80,1280]{1,0:T(8,128)(2,1)S(1)}, bf16[80,1280]{1,0:T(8,128)(2,1)S(1)}, u32[]{:S(2)}, u32[]{:S(2)}) collective-permute-start(bf16[80,1280]{1,0:T(8,128)(2,1)S(1)} %add_convert_fusion.7), channel_id=1, source_target_pairs={{0,1},{1,0},{2,3},{3,2},{4,5},{5,4},{6,7},{7,6},{8,24},{9,25},{10,... | collective-permute-start | bytes 614408 | tf_op jit(solution)/shard_map/ppermute | solution.py:258
  87.9 0.8 collective-permute-start.51
  88.7 5.1 %grad_rows_0.1.refs_8_ = bf16[704,1280]{1,0:T(8,128)(2,1)} custom-call(s32[30]{0:T(128)S(1)} %dynamic-slice_bitcast_fusion.table_ref, s32[1,8]{1,0:T(1,128)S(1)} %copy-done.6, bf16[704,1280]{1,0:T(8,128)(2,1)S(1)} %copy-done.2, f32[1280]{0:T(1024)S(1)} %copy-done.5, bf16[704,640]{1,0:T(8,128)(2,1)S(1)} %get-tuple-element.76.refs_0_, ...), custom_call_target="tpu_custom_call" | custom-call | flops 450560 | tf_op jit(solution)/shard_map/grad_rows_0/pallas_call | solution.py:291
  93.8 0.6 collective-permute-done.48
  94.5 1.4 %collective-permute-done.51 = bf16[160,1280]{1,0:T(8,128)(2,1)S(1)} collective-permute-done((bf16[160,1280]{1,0:T(8,128)(2,1)S(1)}, bf16[160,1280]{1,0:T(8,128)(2,1)S(1)}, u32[]{:S(2)}, u32[]{:S(2)}) %collective-permute-start.51) | collective-permute-done | bytes 409632 | tf_op jit(solution)/shard_map/ppermute | solution.py:255
  96.0 0.9 collective-permute-start.53
  96.9 0.6 collective-permute-start.50
  97.5 0.8 collective-permute-start.49
  98.3 3.5 %collective-permute-done.53 = bf16[80,1280]{1,0:T(8,128)(2,1)S(1)} collective-permute-done((bf16[80,1280]{1,0:T(8,128)(2,1)S(1)}, bf16[80,1280]{1,0:T(8,128)(2,1)S(1)}, u32[]{:S(2)}, u32[]{:S(2)}) %collective-permute-start.53) | collective-permute-done | bytes 204832 | tf_op jit(solution)/shard_map/ppermute | solution.py:258
  102.0 1.2 collective-permute-start.54
  103.1 4.0 %collective-permute-done.49 = bf16[80,1280]{1,0:T(8,128)(2,1)S(1)} collective-permute-done((bf16[80,1280]{1,0:T(8,128)(2,1)S(1)}, bf16[80,1280]{1,0:T(8,128)(2,1)S(1)}, u32[]{:S(2)}, u32[]{:S(2)}) %collective-permute-start.49) | collective-permute-done | bytes 204832 | tf_op jit(solution)/shard_map/ppermute | solution.py:262
  107.2 5.2 %grad_rows_1.1 = bf16[704,1280]{1,0:T(8,128)(2,1)} custom-call(s32[30]{0:T(128)S(1)} %dynamic-slice_bitcast_fusion.table_ref, s32[1,8]{1,0:T(1,128)S(1)} %copy-done.6, bf16[704,1280]{1,0:T(8,128)(2,1)S(1)} %copy-done.2, f32[1280]{0:T(1024)S(1)} %copy-done.5, bf16[704,640]{1,0:T(8,128)(2,1)S(1)} %get-tuple-element.76.refs_0_, ...), custom_call_target="tpu_custom_call", output_to_operand_aliasing={{}: (12, {})} | custom-call | flops 450560 | tf_op jit(solution)/shard_map/grad_rows_1/pallas_call | solution.py:291
  112.4 2.7 %collective-permute-done.54 = bf16[80,1280]{1,0:T(8,128)(2,1)S(1)} collective-permute-done((bf16[80,1280]{1,0:T(8,128)(2,1)S(1)}, bf16[80,1280]{1,0:T(8,128)(2,1)S(1)}, u32[]{:S(2)}, u32[]{:S(2)}) %collective-permute-start.54) | collective-permute-done | bytes 204832 | tf_op jit(solution)/shard_map/ppermute | solution.py:262
  115.2 1.2 collective-permute-start.56
  116.4 5.9 %collective-permute-done.56 = bf16[80,1280]{1,0:T(8,128)(2,1)S(1)} collective-permute-done((bf16[80,1280]{1,0:T(8,128)(2,1)S(1)}, bf16[80,1280]{1,0:T(8,128)(2,1)S(1)}, u32[]{:S(2)}, u32[]{:S(2)}) %collective-permute-start.56) | collective-permute-done | bytes 204832 | tf_op jit(solution)/shard_map/ppermute | solution.py:322
  122.3 1.4 %collective-permute-done.57 = bf16[80,1280]{1,0:T(8,128)(2,1)S(1)} collective-permute-done((bf16[80,1280]{1,0:T(8,128)(2,1)S(1)}, bf16[80,1280]{1,0:T(8,128)(2,1)S(1)}, u32[]{:S(2)}, u32[]{:S(2)}) %collective-permute-start.57) | collective-permute-done | bytes 204832 | tf_op jit(solution)/shard_map/ppermute | solution.py:323
  123.8 1.3 %maximum_convert_fusion = f32[320,1280]{1,0:T(8,128)} fusion(bf16[80,1280]{1,0:T(8,128)(2,1)S(1)} %get-tuple-element.95, bf16[80,1280]{1,0:T(8,128)(2,1)S(1)} %get-tuple-element.96, bf16[80,1280]{1,0:T(8,128)(2,1)S(1)} %get-tuple-element.97, bf16[80,1280]{1,0:T(8,128)(2,1)S(1)} %get-tuple-element.94), kind=kLoop, calls=%fused_computation | loop fusion | flops 3276800 | bytes 2457600 | tf_op jit(solution)/shard_map/concatenate | solution.py:325
  (103 shorter events, 5.8 us)
Async XLA Ops:
  1.4 26.5 %copy-start.3 = (bf16[320,1280]{1,0:T(8,128)(2,1)S(1)}, bf16[320,1280]{1,0:T(8,128)(2,1)}, u32[]{:S(2)}) copy-start(bf16[320,1280]{1,0:T(8,128)(2,1)} %refs_0_.1) | copy-start | bytes 2457604
  2.5 19.3 %copy-start.8 = (bf16[320]{0:T(512)(128)(2,1)S(1)}, bf16[320]{0:T(512)(128)(2,1)}, u32[]{:S(2)}) copy-start(bf16[320]{0:T(512)(128)(2,1)} %param.12) | copy-start | bytes 1924
  2.5 25.5 %copy-start.6 = (s32[1,8]{1,0:T(1,128)S(1)}, s32[1,8]{1,0:T(1,128)}, u32[]{:S(2)}) copy-start(s32[1,8]{1,0:T(1,128)} %counts_ref.11) | copy-start | bytes 100
  2.5 8.7 %collective-permute-start.2 = (bf16[88,1280]{1,0:T(8,128)(2,1)S(1)}, bf16[88,1280]{1,0:T(8,128)(2,1)}, u32[]{:S(2)}, u32[]{:S(2)}) collective-permute-start(bf16[88,1280]{1,0:T(8,128)(2,1)S(1)} %pad_maximum_fusion), channel_id=1, source_target_pairs={{0,1},{1,0},{2,3},{3,2},{4,5},{5,4},{6,7},{7,6},{8,9},{9,8},{10,11... | collective-permute-start | bytes 675848 | tf_op jit(solution)/shard_map/ppermute | solution.py:221
  5.6 11.7 %collective-permute-start = (bf16[88,1280]{1,0:T(8,128)(2,1)S(1)}, bf16[88,1280]{1,0:T(8,128)(2,1)S(1)}, u32[]{:S(2)}, u32[]{:S(2)}) collective-permute-start(bf16[88,1280]{1,0:T(8,128)(2,1)S(1)} %pad_maximum_fusion), channel_id=1, source_target_pairs={{0,2},{1,3},{2,4},{3,5},{4,6},{5,7},{6,0},{7,1},{8,10},{9,11},{10,... | collective-permute-start | bytes 675848 | tf_op jit(solution)/shard_map/ppermute | solution.py:220
  7.1 11.5 %collective-permute-start.12 = (bf16[88,1280]{1,0:T(8,128)(2,1)S(1)}, bf16[88,1280]{1,0:T(8,128)(2,1)S(1)}, u32[]{:S(2)}, u32[]{:S(2)}) collective-permute-start(bf16[88,1280]{1,0:T(8,128)(2,1)S(1)} %pad_maximum_fusion), channel_id=1, source_target_pairs={{0,6},{1,7},{2,0},{3,1},{4,2},{5,3},{6,4},{7,5},{8,14},{9,15},{10,... | collective-permute-start | bytes 675848 | tf_op jit(solution)/shard_map/ppermute | solution.py:220
  11.2 10.1 %collective-permute-start.3 = (bf16[88,1280]{1,0:T(8,128)(2,1)}, bf16[88,1280]{1,0:T(8,128)(2,1)}, u32[]{:S(2)}, u32[]{:S(2)}) collective-permute-start(bf16[88,1280]{1,0:T(8,128)(2,1)} %collective-permute-done.2.refs_1_), channel_id=1, source_target_pairs={{0,16},{1,17},{2,18},{3,19},{4,20},{5,21},{6,22},{7,23},{8,24},{9,... | collective-permute-start | bytes 675848 | tf_op jit(solution)/shard_map/ppermute | solution.py:238
  18.7 6.0 %collective-permute-start.13 = (bf16[88,1280]{1,0:T(8,128)(2,1)S(1)}, bf16[88,1280]{1,0:T(8,128)(2,1)S(1)}, u32[]{:S(2)}, u32[]{:S(2)}) collective-permute-start(bf16[88,1280]{1,0:T(8,128)(2,1)S(1)} %collective-permute-done.refs_0_), channel_id=1, source_target_pairs={{0,16},{1,17},{2,18},{3,19},{4,20},{5,21},{6,22},{7,23},{8,9},{9,8... | collective-permute-start | bytes 675848 | tf_op jit(solution)/shard_map/ppermute | solution.py:243
  20.2 7.8 %collective-permute-start.1 = (bf16[88,1280]{1,0:T(8,128)(2,1)S(1)}, bf16[88,1280]{1,0:T(8,128)(2,1)S(1)}, u32[]{:S(2)}, u32[]{:S(2)}) collective-permute-start(bf16[88,1280]{1,0:T(8,128)(2,1)S(1)} %collective-permute-done.refs_0_), channel_id=1, source_target_pairs={{0,2},{1,3},{2,4},{3,5},{4,6},{5,7},{6,0},{7,1},{8,10},{9,11},{10,... | collective-permute-start | bytes 675848 | tf_op jit(solution)/shard_map/ppermute | solution.py:236
  21.3 6.7 %collective-permute-start.4 = (bf16[88,1280]{1,0:T(8,128)(2,1)}, bf16[88,1280]{1,0:T(8,128)(2,1)}, u32[]{:S(2)}, u32[]{:S(2)}) collective-permute-start(bf16[88,1280]{1,0:T(8,128)(2,1)} %collective-permute-done.2.refs_1_), channel_id=1, source_target_pairs={{0,8},{1,9},{2,10},{3,11},{4,12},{5,13},{6,14},{7,15},{8,0},{9,1},... | collective-permute-start | bytes 675848 | tf_op jit(solution)/shard_map/ppermute | solution.py:239
  21.3 6.6 %collective-permute-start.5 = (bf16[88,1280]{1,0:T(8,128)(2,1)}, bf16[88,1280]{1,0:T(8,128)(2,1)}, u32[]{:S(2)}, u32[]{:S(2)}) collective-permute-start(bf16[88,1280]{1,0:T(8,128)(2,1)} %collective-permute-done.3.refs_2_), channel_id=1, source_target_pairs={{0,8},{1,9},{2,10},{3,11},{4,12},{5,13},{6,14},{7,15},{8,0},{9,1},... | collective-permute-start | bytes 675848 | tf_op jit(solution)/shard_map/ppermute | solution.py:239
  21.9 14.6 %collective-permute-start.14 = (bf16[88,1280]{1,0:T(8,128)(2,1)S(1)}, bf16[88,1280]{1,0:T(8,128)(2,1)S(1)}, u32[]{:S(2)}, u32[]{:S(2)}) collective-permute-start(bf16[88,1280]{1,0:T(8,128)(2,1)S(1)} %collective-permute-done.refs_0_), channel_id=1, source_target_pairs={{0,1},{1,0},{2,3},{3,2},{4,5},{5,4},{6,7},{7,6},{8,24},{9,25},{10,... | collective-permute-start | bytes 675848 | tf_op jit(solution)/shard_map/ppermute | solution.py:244
  24.7 12.2 %collective-permute-start.15 = (bf16[88,1280]{1,0:T(8,128)(2,1)S(1)}, bf16[88,1280]{1,0:T(8,128)(2,1)S(1)}, u32[]{:S(2)}, u32[]{:S(2)}) collective-permute-start(bf16[88,1280]{1,0:T(8,128)(2,1)S(1)} %collective-permute-done.13.refs_1_), channel_id=1, source_target_pairs={{0,1},{1,0},{2,3},{3,2},{4,5},{5,4},{6,7},{7,6},{8,24},{9,25},{10,... | collective-permute-start | bytes 675848 | tf_op jit(solution)/shard_map/ppermute | solution.py:244
  28.0 2.0 %copy-start = (bf16[704,2560]{1,0:T(8,128)(2,1)S(1)}, bf16[704,2560]{1,0:T(8,128)(2,1)}, u32[]{:S(2)}) copy-start(bf16[704,2560]{1,0:T(8,128)(2,1)} %g_ref.7) | copy-start | bytes 10813444
  35.8 1.5 %collective-permute-start.7 = (bf16[80,1280]{1,0:T(8,128)(2,1)S(1)}, bf16[80,1280]{1,0:T(8,128)(2,1)S(1)}, u32[]{:S(2)}, u32[]{:S(2)}) collective-permute-start(bf16[80,1280]{1,0:T(8,128)(2,1)S(1)} %get-tuple-element.51), channel_id=1, source_target_pairs={{0,8},{1,9},{2,10},{3,11},{4,12},{5,13},{6,14},{7,15},{8,0},{9,1},... | collective-permute-start | bytes 614408 | tf_op jit(solution)/shard_map/ppermute | solution.py:250
  35.9 1.7 %collective-permute-start.8 = (bf16[80,1280]{1,0:T(8,128)(2,1)S(1)}, bf16[80,1280]{1,0:T(8,128)(2,1)S(1)}, u32[]{:S(2)}, u32[]{:S(2)}) collective-permute-start(bf16[80,1280]{1,0:T(8,128)(2,1)S(1)} %get-tuple-element.52), channel_id=1, source_target_pairs={{0,8},{1,9},{2,10},{3,11},{4,12},{5,13},{6,14},{7,15},{8,0},{9,1},... | collective-permute-start | bytes 614408 | tf_op jit(solution)/shard_map/ppermute | solution.py:250
  36.4 2.6 %collective-permute-start.16 = (bf16[88,1280]{1,0:T(8,128)(2,1)S(1)}, bf16[88,1280]{1,0:T(8,128)(2,1)S(1)}, u32[]{:S(2)}, u32[]{:S(2)}) collective-permute-start(bf16[88,1280]{1,0:T(8,128)(2,1)S(1)} %collective-permute-done.refs_0_), channel_id=1, source_target_pairs={{0,8},{1,9},{2,10},{3,11},{4,12},{5,13},{6,14},{7,15},{8,0},{9,1},... | collective-permute-start | bytes 675848 | tf_op jit(solution)/shard_map/ppermute | solution.py:245
  36.5 3.4 %collective-permute-start.17 = (bf16[88,1280]{1,0:T(8,128)(2,1)S(1)}, bf16[88,1280]{1,0:T(8,128)(2,1)S(1)}, u32[]{:S(2)}, u32[]{:S(2)}) collective-permute-start(bf16[88,1280]{1,0:T(8,128)(2,1)S(1)} %collective-permute-done.13.refs_1_), channel_id=1, source_target_pairs={{0,8},{1,9},{2,10},{3,11},{4,12},{5,13},{6,14},{7,15},{8,0},{9,1},... | collective-permute-start | bytes 675848 | tf_op jit(solution)/shard_map/ppermute | solution.py:245
  36.9 2.9 %collective-permute-start.18 = (bf16[88,1280]{1,0:T(8,128)(2,1)S(1)}, bf16[88,1280]{1,0:T(8,128)(2,1)S(1)}, u32[]{:S(2)}, u32[]{:S(2)}) collective-permute-start(bf16[88,1280]{1,0:T(8,128)(2,1)S(1)} %collective-permute-done.14.refs_2_), channel_id=1, source_target_pairs={{0,8},{1,9},{2,10},{3,11},{4,12},{5,13},{6,14},{7,15},{8,0},{9,1},... | collective-permute-start | bytes 675848 | tf_op jit(solution)/shard_map/ppermute | solution.py:245
  37.3 2.5 %collective-permute-start.19 = (bf16[88,1280]{1,0:T(8,128)(2,1)S(1)}, bf16[88,1280]{1,0:T(8,128)(2,1)S(1)}, u32[]{:S(2)}, u32[]{:S(2)}) collective-permute-start(bf16[88,1280]{1,0:T(8,128)(2,1)S(1)} %collective-permute-done.15.refs_3_), channel_id=1, source_target_pairs={{0,8},{1,9},{2,10},{3,11},{4,12},{5,13},{6,14},{7,15},{8,0},{9,1},... | collective-permute-start | bytes 675848 | tf_op jit(solution)/shard_map/ppermute | solution.py:245
  37.7 10.9 %collective-permute-start.9 = (bf16[160,1280]{1,0:T(8,128)(2,1)S(1)}, bf16[160,1280]{1,0:T(8,128)(2,1)S(1)}, u32[]{:S(2)}, u32[]{:S(2)}) collective-permute-start(bf16[160,1280]{1,0:T(8,128)(2,1)S(1)} %add_convert_fusion.3), channel_id=1, source_target_pairs={{0,16},{1,17},{2,18},{3,19},{4,20},{5,21},{6,22},{7,23},{8,9},{9,8... | collective-permute-start | bytes 1228808 | tf_op jit(solution)/shard_map/ppermute | solution.py:255
  39.0 9.7 %collective-permute-start.27 = (bf16[88,1280]{1,0:T(8,128)(2,1)S(1)}, bf16[88,1280]{1,0:T(8,128)(2,1)S(1)}, u32[]{:S(2)}, u32[]{:S(2)}) collective-permute-start(bf16[88,1280]{1,0:T(8,128)(2,1)S(1)} %collective-permute-done.12.refs_0_), channel_id=1, source_target_pairs={{0,16},{1,17},{2,18},{3,19},{4,20},{5,21},{6,22},{7,23},{8,9},{9,8... | collective-permute-start | bytes 675848 | tf_op jit(solution)/shard_map/ppermute | solution.py:243
  39.8 10.0 %collective-permute-start.10 = (bf16[80,1280]{1,0:T(8,128)(2,1)S(1)}, bf16[80,1280]{1,0:T(8,128)(2,1)S(1)}, u32[]{:S(2)}, u32[]{:S(2)}) collective-permute-start(bf16[80,1280]{1,0:T(8,128)(2,1)S(1)} %get-tuple-element.53), channel_id=1, source_target_pairs={{0,8},{1,9},{2,10},{3,11},{4,12},{5,13},{6,14},{7,15},{8,0},{9,1},... | collective-permute-start | bytes 614408 | tf_op jit(solution)/shard_map/ppermute | solution.py:250
  44.4 5.6 %collective-permute-start.21 = (bf16[80,1280]{1,0:T(8,128)(2,1)S(1)}, bf16[80,1280]{1,0:T(8,128)(2,1)S(1)}, u32[]{:S(2)}, u32[]{:S(2)}) collective-permute-start(bf16[80,1280]{1,0:T(8,128)(2,1)S(1)} %get-tuple-element.58), channel_id=1, source_target_pairs={{0,8},{1,9},{2,10},{3,11},{4,12},{5,13},{6,14},{7,15},{8,0},{9,1},... | collective-permute-start | bytes 614408 | tf_op jit(solution)/shard_map/ppermute | solution.py:250
  45.0 6.0 %collective-permute-start.28 = (bf16[88,1280]{1,0:T(8,128)(2,1)S(1)}, bf16[88,1280]{1,0:T(8,128)(2,1)S(1)}, u32[]{:S(2)}, u32[]{:S(2)}) collective-permute-start(bf16[88,1280]{1,0:T(8,128)(2,1)S(1)} %collective-permute-done.12.refs_0_), channel_id=1, source_target_pairs={{0,1},{1,0},{2,3},{3,2},{4,5},{5,4},{6,7},{7,6},{8,24},{9,25},{10,... | collective-permute-start | bytes 675848 | tf_op jit(solution)/shard_map/ppermute | solution.py:244
  48.6 3.5 %collective-permute-start.30 = (bf16[88,1280]{1,0:T(8,128)(2,1)S(1)}, bf16[88,1280]{1,0:T(8,128)(2,1)S(1)}, u32[]{:S(2)}, u32[]{:S(2)}) collective-permute-start(bf16[88,1280]{1,0:T(8,128)(2,1)S(1)} %collective-permute-done.12.refs_0_), channel_id=1, source_target_pairs={{0,8},{1,9},{2,10},{3,11},{4,12},{5,13},{6,14},{7,15},{8,0},{9,1},... | collective-permute-start | bytes 675848 | tf_op jit(solution)/shard_map/ppermute | solution.py:245
  48.6 7.3 %collective-permute-start.29 = (bf16[88,1280]{1,0:T(8,128)(2,1)S(1)}, bf16[88,1280]{1,0:T(8,128)(2,1)S(1)}, u32[]{:S(2)}, u32[]{:S(2)}) collective-permute-start(bf16[88,1280]{1,0:T(8,128)(2,1)S(1)} %collective-permute-done.27.refs_1_), channel_id=1, source_target_pairs={{0,1},{1,0},{2,3},{3,2},{4,5},{5,4},{6,7},{7,6},{8,24},{9,25},{10,... | collective-permute-start | bytes 675848 | tf_op jit(solution)/shard_map/ppermute | solution.py:244
  49.8 6.1 %collective-permute-start.31 = (bf16[88,1280]{1,0:T(8,128)(2,1)S(1)}, bf16[88,1280]{1,0:T(8,128)(2,1)S(1)}, u32[]{:S(2)}, u32[]{:S(2)}) collective-permute-start(bf16[88,1280]{1,0:T(8,128)(2,1)S(1)} %collective-permute-done.27.refs_1_), channel_id=1, source_target_pairs={{0,8},{1,9},{2,10},{3,11},{4,12},{5,13},{6,14},{7,15},{8,0},{9,1},... | collective-permute-start | bytes 675848 | tf_op jit(solution)/shard_map/ppermute | solution.py:245
  50.0 6.4 %collective-permute-start.22 = (bf16[80,1280]{1,0:T(8,128)(2,1)S(1)}, bf16[80,1280]{1,0:T(8,128)(2,1)S(1)}, u32[]{:S(2)}, u32[]{:S(2)}) collective-permute-start(bf16[80,1280]{1,0:T(8,128)(2,1)S(1)} %get-tuple-element.60), channel_id=1, source_target_pairs={{0,8},{1,9},{2,10},{3,11},{4,12},{5,13},{6,14},{7,15},{8,0},{9,1},... | collective-permute-start | bytes 614408 | tf_op jit(solution)/shard_map/ppermute | solution.py:250
  50.9 7.7 %collective-permute-start.36 = (bf16[88,1280]{1,0:T(8,128)(2,1)S(1)}, bf16[88,1280]{1,0:T(8,128)(2,1)S(1)}, u32[]{:S(2)}, u32[]{:S(2)}) collective-permute-start(bf16[88,1280]{1,0:T(8,128)(2,1)S(1)} %collective-permute-done.1.refs_0_), channel_id=1, source_target_pairs={{0,16},{1,17},{2,18},{3,19},{4,20},{5,21},{6,22},{7,23},{8,9},{9,8... | collective-permute-start | bytes 675848 | tf_op jit(solution)/shard_map/ppermute | solution.py:243
  52.1 5.3 %collective-permute-start.32 = (bf16[88,1280]{1,0:T(8,128)(2,1)S(1)}, bf16[88,1280]{1,0:T(8,128)(2,1)S(1)}, u32[]{:S(2)}, u32[]{:S(2)}) collective-permute-start(bf16[88,1280]{1,0:T(8,128)(2,1)S(1)} %collective-permute-done.28.refs_2_), channel_id=1, source_target_pairs={{0,8},{1,9},{2,10},{3,11},{4,12},{5,13},{6,14},{7,15},{8,0},{9,1},... | collective-permute-start | bytes 675848 | tf_op jit(solution)/shard_map/ppermute | solution.py:245
  55.9 8.7 %collective-permute-start.6 = (bf16[80,1280]{1,0:T(8,128)(2,1)S(1)}, bf16[80,1280]{1,0:T(8,128)(2,1)S(1)}, u32[]{:S(2)}, u32[]{:S(2)}) collective-permute-start(bf16[80,1280]{1,0:T(8,128)(2,1)S(1)} %get-tuple-element.50), channel_id=1, source_target_pairs={{0,8},{1,9},{2,10},{3,11},{4,12},{5,13},{6,14},{7,15},{8,0},{9,1},... | collective-permute-start | bytes 614408 | tf_op jit(solution)/shard_map/ppermute | solution.py:250
  55.9 2.7 %collective-permute-start.33 = (bf16[88,1280]{1,0:T(8,128)(2,1)S(1)}, bf16[88,1280]{1,0:T(8,128)(2,1)S(1)}, u32[]{:S(2)}, u32[]{:S(2)}) collective-permute-start(bf16[88,1280]{1,0:T(8,128)(2,1)S(1)} %collective-permute-done.29.refs_3_), channel_id=1, source_target_pairs={{0,8},{1,9},{2,10},{3,11},{4,12},{5,13},{6,14},{7,15},{8,0},{9,1},... | collective-permute-start | bytes 675848 | tf_op jit(solution)/shard_map/ppermute | solution.py:245
  56.4 7.8 %collective-permute-start.11 = (bf16[80,1280]{1,0:T(8,128)(2,1)S(1)}, bf16[80,1280]{1,0:T(8,128)(2,1)S(1)}, u32[]{:S(2)}, u32[]{:S(2)}) collective-permute-start(bf16[80,1280]{1,0:T(8,128)(2,1)S(1)} %add_convert_fusion.10), channel_id=1, source_target_pairs={{0,1},{1,0},{2,3},{3,2},{4,5},{5,4},{6,7},{7,6},{8,24},{9,25},{10,... | collective-permute-start | bytes 614408 | tf_op jit(solution)/shard_map/ppermute | solution.py:258
  57.4 15.8 %collective-permute-start.37 = (bf16[88,1280]{1,0:T(8,128)(2,1)S(1)}, bf16[88,1280]{1,0:T(8,128)(2,1)S(1)}, u32[]{:S(2)}, u32[]{:S(2)}) collective-permute-start(bf16[88,1280]{1,0:T(8,128)(2,1)S(1)} %collective-permute-done.1.refs_0_), channel_id=1, source_target_pairs={{0,1},{1,0},{2,3},{3,2},{4,5},{5,4},{6,7},{7,6},{8,24},{9,25},{10,... | collective-permute-start | bytes 675848 | tf_op jit(solution)/shard_map/ppermute | solution.py:244
  58.6 15.5 %collective-permute-start.39 = (bf16[88,1280]{1,0:T(8,128)(2,1)S(1)}, bf16[88,1280]{1,0:T(8,128)(2,1)S(1)}, u32[]{:S(2)}, u32[]{:S(2)}) collective-permute-start(bf16[88,1280]{1,0:T(8,128)(2,1)S(1)} %collective-permute-done.1.refs_0_), channel_id=1, source_target_pairs={{0,8},{1,9},{2,10},{3,11},{4,12},{5,13},{6,14},{7,15},{8,0},{9,1},... | collective-permute-start | bytes 675848 | tf_op jit(solution)/shard_map/ppermute | solution.py:245
  58.7 15.9 %collective-permute-start.38 = (bf16[88,1280]{1,0:T(8,128)(2,1)S(1)}, bf16[88,1280]{1,0:T(8,128)(2,1)S(1)}, u32[]{:S(2)}, u32[]{:S(2)}) collective-permute-start(bf16[88,1280]{1,0:T(8,128)(2,1)S(1)} %collective-permute-done.36.refs_1_), channel_id=1, source_target_pairs={{0,1},{1,0},{2,3},{3,2},{4,5},{5,4},{6,7},{7,6},{8,24},{9,25},{10,... | collective-permute-start | bytes 675848 | tf_op jit(solution)/shard_map/ppermute | solution.py:244
  64.2 8.3 %collective-permute-start.24 = (bf16[80,1280]{1,0:T(8,128)(2,1)S(1)}, bf16[80,1280]{1,0:T(8,128)(2,1)S(1)}, u32[]{:S(2)}, u32[]{:S(2)}) collective-permute-start(bf16[80,1280]{1,0:T(8,128)(2,1)S(1)} %get-tuple-element.62), channel_id=1, source_target_pairs={{0,8},{1,9},{2,10},{3,11},{4,12},{5,13},{6,14},{7,15},{8,0},{9,1},... | collective-permute-start | bytes 614408 | tf_op jit(solution)/shard_map/ppermute | solution.py:250
  64.6 8.0 %collective-permute-start.23 = (bf16[160,1280]{1,0:T(8,128)(2,1)S(1)}, bf16[160,1280]{1,0:T(8,128)(2,1)S(1)}, u32[]{:S(2)}, u32[]{:S(2)}) collective-permute-start(bf16[160,1280]{1,0:T(8,128)(2,1)S(1)} %add_convert_fusion.2), channel_id=1, source_target_pairs={{0,16},{1,17},{2,18},{3,19},{4,20},{5,21},{6,22},{7,23},{8,9},{9,8... | collective-permute-start | bytes 1228808 | tf_op jit(solution)/shard_map/ppermute | solution.py:255
  72.5 1.5 %collective-permute-start.34 = (bf16[80,1280]{1,0:T(8,128)(2,1)S(1)}, bf16[80,1280]{1,0:T(8,128)(2,1)S(1)}, u32[]{:S(2)}, u32[]{:S(2)}) collective-permute-start(bf16[80,1280]{1,0:T(8,128)(2,1)S(1)} %get-tuple-element.65), channel_id=1, source_target_pairs={{0,8},{1,9},{2,10},{3,11},{4,12},{5,13},{6,14},{7,15},{8,0},{9,1},... | collective-permute-start | bytes 614408 | tf_op jit(solution)/shard_map/ppermute | solution.py:250
  72.6 2.1 %collective-permute-start.35 = (bf16[80,1280]{1,0:T(8,128)(2,1)S(1)}, bf16[80,1280]{1,0:T(8,128)(2,1)S(1)}, u32[]{:S(2)}, u32[]{:S(2)}) collective-permute-start(bf16[80,1280]{1,0:T(8,128)(2,1)S(1)} %get-tuple-element.67), channel_id=1, source_target_pairs={{0,8},{1,9},{2,10},{3,11},{4,12},{5,13},{6,14},{7,15},{8,0},{9,1},... | collective-permute-start | bytes 614408 | tf_op jit(solution)/shard_map/ppermute | solution.py:250
  73.2 3.3 %collective-permute-start.40 = (bf16[88,1280]{1,0:T(8,128)(2,1)S(1)}, bf16[88,1280]{1,0:T(8,128)(2,1)S(1)}, u32[]{:S(2)}, u32[]{:S(2)}) collective-permute-start(bf16[88,1280]{1,0:T(8,128)(2,1)S(1)} %collective-permute-done.36.refs_1_), channel_id=1, source_target_pairs={{0,8},{1,9},{2,10},{3,11},{4,12},{5,13},{6,14},{7,15},{8,0},{9,1},... | collective-permute-start | bytes 675848 | tf_op jit(solution)/shard_map/ppermute | solution.py:245
  74.0 2.6 %collective-permute-start.41 = (bf16[88,1280]{1,0:T(8,128)(2,1)S(1)}, bf16[88,1280]{1,0:T(8,128)(2,1)S(1)}, u32[]{:S(2)}, u32[]{:S(2)}) collective-permute-start(bf16[88,1280]{1,0:T(8,128)(2,1)S(1)} %collective-permute-done.37.refs_2_), channel_id=1, source_target_pairs={{0,8},{1,9},{2,10},{3,11},{4,12},{5,13},{6,14},{7,15},{8,0},{9,1},... | collective-permute-start | bytes 675848 | tf_op jit(solution)/shard_map/ppermute | solution.py:245
  74.1 8.3 %collective-permute-start.20 = (bf16[80,1280]{1,0:T(8,128)(2,1)S(1)}, bf16[80,1280]{1,0:T(8,128)(2,1)S(1)}, u32[]{:S(2)}, u32[]{:S(2)}) collective-permute-start(bf16[80,1280]{1,0:T(8,128)(2,1)S(1)} %get-tuple-element.57), channel_id=1, source_target_pairs={{0,8},{1,9},{2,10},{3,11},{4,12},{5,13},{6,14},{7,15},{8,0},{9,1},... | collective-permute-start | bytes 614408 | tf_op jit(solution)/shard_map/ppermute | solution.py:250
  74.5 2.6 %collective-permute-start.42 = (bf16[88,1280]{1,0:T(8,128)(2,1)S(1)}, bf16[88,1280]{1,0:T(8,128)(2,1)S(1)}, u32[]{:S(2)}, u32[]{:S(2)}) collective-permute-start(bf16[88,1280]{1,0:T(8,128)(2,1)S(1)} %collective-permute-done.38.refs_3_), channel_id=1, source_target_pairs={{0,8},{1,9},{2,10},{3,11},{4,12},{5,13},{6,14},{7,15},{8,0},{9,1},... | collective-permute-start | bytes 675848 | tf_op jit(solution)/shard_map/ppermute | solution.py:245
  74.7 7.7 %collective-permute-start.25 = (bf16[80,1280]{1,0:T(8,128)(2,1)S(1)}, bf16[80,1280]{1,0:T(8,128)(2,1)S(1)}, u32[]{:S(2)}, u32[]{:S(2)}) collective-permute-start(bf16[80,1280]{1,0:T(8,128)(2,1)S(1)} %add_convert_fusion.9), channel_id=1, source_target_pairs={{0,1},{1,0},{2,3},{3,2},{4,5},{5,4},{6,7},{7,6},{8,24},{9,25},{10,... | collective-permute-start | bytes 614408 | tf_op jit(solution)/shard_map/ppermute | solution.py:258
  76.5 8.5 %collective-permute-start.44 = (bf16[80,1280]{1,0:T(8,128)(2,1)S(1)}, bf16[80,1280]{1,0:T(8,128)(2,1)S(1)}, u32[]{:S(2)}, u32[]{:S(2)}) collective-permute-start(bf16[80,1280]{1,0:T(8,128)(2,1)S(1)} %get-tuple-element.71), channel_id=1, source_target_pairs={{0,8},{1,9},{2,10},{3,11},{4,12},{5,13},{6,14},{7,15},{8,0},{9,1},... | collective-permute-start | bytes 614408 | tf_op jit(solution)/shard_map/ppermute | solution.py:250
  76.6 17.8 %collective-permute-start.47 = (bf16[80,1280]{1,0:T(8,128)(2,1)S(1)}, bf16[80,1280]{1,0:T(8,128)(2,1)S(1)}, u32[]{:S(2)}, u32[]{:S(2)}) collective-permute-start(bf16[80,1280]{1,0:T(8,128)(2,1)S(1)} %get-tuple-element.85), channel_id=1, source_target_pairs={{0,8},{1,9},{2,10},{3,11},{4,12},{5,13},{6,14},{7,15},{8,0},{9,1},... | collective-permute-start | bytes 614408 | tf_op jit(solution)/shard_map/ppermute | solution.py:250
  77.1 8.0 %collective-permute-start.45 = (bf16[160,1280]{1,0:T(8,128)(2,1)S(1)}, bf16[160,1280]{1,0:T(8,128)(2,1)S(1)}, u32[]{:S(2)}, u32[]{:S(2)}) collective-permute-start(bf16[160,1280]{1,0:T(8,128)(2,1)S(1)} %add_convert_fusion.1), channel_id=1, source_target_pairs={{0,16},{1,17},{2,18},{3,19},{4,20},{5,21},{6,22},{7,23},{8,9},{9,8... | collective-permute-start | bytes 1228808 | tf_op jit(solution)/shard_map/ppermute | solution.py:255
  82.3 6.4 %copy-start.2 = (bf16[704,1280]{1,0:T(8,128)(2,1)S(1)}, bf16[704,1280]{1,0:T(8,128)(2,1)}, u32[]{:S(2)}) copy-start(bf16[704,1280]{1,0:T(8,128)(2,1)} %rows_ref.5) | copy-start | bytes 5406724
  82.3 6.4 %copy-start.5 = (f32[1280]{0:T(1024)S(1)}, f32[1280]{0:T(1024)}, u32[]{:S(2)}) copy-start(f32[1280]{0:T(1024)} %gamma_ref.5) | copy-start | bytes 15364
  82.3 4.1 %collective-permute-start.43 = (bf16[80,1280]{1,0:T(8,128)(2,1)S(1)}, bf16[80,1280]{1,0:T(8,128)(2,1)S(1)}, u32[]{:S(2)}, u32[]{:S(2)}) collective-permute-start(bf16[80,1280]{1,0:T(8,128)(2,1)S(1)} %get-tuple-element.70), channel_id=1, source_target_pairs={{0,8},{1,9},{2,10},{3,11},{4,12},{5,13},{6,14},{7,15},{8,0},{9,1},... | collective-permute-start | bytes 614408 | tf_op jit(solution)/shard_map/ppermute | solution.py:250
  82.4 5.4 %collective-permute-start.46 = (bf16[80,1280]{1,0:T(8,128)(2,1)S(1)}, bf16[80,1280]{1,0:T(8,128)(2,1)S(1)}, u32[]{:S(2)}, u32[]{:S(2)}) collective-permute-start(bf16[80,1280]{1,0:T(8,128)(2,1)S(1)} %get-tuple-element.74), channel_id=1, source_target_pairs={{0,8},{1,9},{2,10},{3,11},{4,12},{5,13},{6,14},{7,15},{8,0},{9,1},... | collective-permute-start | bytes 614408 | tf_op jit(solution)/shard_map/ppermute | solution.py:250
  85.1 10.9 %collective-permute-start.52 = (bf16[80,1280]{1,0:T(8,128)(2,1)S(1)}, bf16[80,1280]{1,0:T(8,128)(2,1)S(1)}, u32[]{:S(2)}, u32[]{:S(2)}) collective-permute-start(bf16[80,1280]{1,0:T(8,128)(2,1)S(1)} %get-tuple-element.89), channel_id=1, source_target_pairs={{0,8},{1,9},{2,10},{3,11},{4,12},{5,13},{6,14},{7,15},{8,0},{9,1},... | collective-permute-start | bytes 614408 | tf_op jit(solution)/shard_map/ppermute | solution.py:250
  85.1 8.7 %collective-permute-start.26 = (bf16[80,1280]{1,0:T(8,128)(2,1)S(1)}, bf16[80,1280]{1,0:T(8,128)(2,1)S(1)}, u32[]{:S(2)}, u32[]{:S(2)}) collective-permute-start(bf16[80,1280]{1,0:T(8,128)(2,1)S(1)} %add_convert_fusion.8), channel_id=1, source_target_pairs={{0,6},{1,7},{2,0},{3,1},{4,2},{5,3},{6,4},{7,5},{8,14},{9,15},{10,... | collective-permute-start | bytes 614408 | tf_op jit(solution)/shard_map/ppermute | solution.py:262
  86.4 8.0 %collective-permute-start.48 = (bf16[80,1280]{1,0:T(8,128)(2,1)S(1)}, bf16[80,1280]{1,0:T(8,128)(2,1)S(1)}, u32[]{:S(2)}, u32[]{:S(2)}) collective-permute-start(bf16[80,1280]{1,0:T(8,128)(2,1)S(1)} %add_convert_fusion.7), channel_id=1, source_target_pairs={{0,1},{1,0},{2,3},{3,2},{4,5},{5,4},{6,7},{7,6},{8,24},{9,25},{10,... | collective-permute-start | bytes 614408 | tf_op jit(solution)/shard_map/ppermute | solution.py:258
  87.9 8.0 %collective-permute-start.51 = (bf16[160,1280]{1,0:T(8,128)(2,1)S(1)}, bf16[160,1280]{1,0:T(8,128)(2,1)S(1)}, u32[]{:S(2)}, u32[]{:S(2)}) collective-permute-start(bf16[160,1280]{1,0:T(8,128)(2,1)S(1)} %add_convert_fusion), channel_id=1, source_target_pairs={{0,16},{1,17},{2,18},{3,19},{4,20},{5,21},{6,22},{7,23},{8,9},{9,8... | collective-permute-start | bytes 1228808 | tf_op jit(solution)/shard_map/ppermute | solution.py:255
  96.0 5.8 %collective-permute-start.53 = (bf16[80,1280]{1,0:T(8,128)(2,1)S(1)}, bf16[80,1280]{1,0:T(8,128)(2,1)S(1)}, u32[]{:S(2)}, u32[]{:S(2)}) collective-permute-start(bf16[80,1280]{1,0:T(8,128)(2,1)S(1)} %add_convert_fusion.5), channel_id=1, source_target_pairs={{0,1},{1,0},{2,3},{3,2},{4,5},{5,4},{6,7},{7,6},{8,24},{9,25},{10,... | collective-permute-start | bytes 614408 | tf_op jit(solution)/shard_map/ppermute | solution.py:258
  96.9 4.9 %collective-permute-start.50 = (bf16[80,1280]{1,0:T(8,128)(2,1)S(1)}, bf16[80,1280]{1,0:T(8,128)(2,1)S(1)}, u32[]{:S(2)}, u32[]{:S(2)}) collective-permute-start(bf16[80,1280]{1,0:T(8,128)(2,1)S(1)} %get-tuple-element.87), channel_id=1, source_target_pairs={{0,8},{1,9},{2,10},{3,11},{4,12},{5,13},{6,14},{7,15},{8,0},{9,1},... | collective-permute-start | bytes 614408 | tf_op jit(solution)/shard_map/ppermute | solution.py:250
  97.5 9.7 %collective-permute-start.49 = (bf16[80,1280]{1,0:T(8,128)(2,1)S(1)}, bf16[80,1280]{1,0:T(8,128)(2,1)S(1)}, u32[]{:S(2)}, u32[]{:S(2)}) collective-permute-start(bf16[80,1280]{1,0:T(8,128)(2,1)S(1)} %add_convert_fusion.6), channel_id=1, source_target_pairs={{0,2},{1,3},{2,4},{3,5},{4,6},{5,7},{6,0},{7,1},{8,10},{9,11},{10,... | collective-permute-start | bytes 614408 | tf_op jit(solution)/shard_map/ppermute | solution.py:262
  102.0 13.1 %collective-permute-start.54 = (bf16[80,1280]{1,0:T(8,128)(2,1)S(1)}, bf16[80,1280]{1,0:T(8,128)(2,1)S(1)}, u32[]{:S(2)}, u32[]{:S(2)}) collective-permute-start(bf16[80,1280]{1,0:T(8,128)(2,1)S(1)} %add_convert_fusion.4), channel_id=1, source_target_pairs={{0,4},{1,5},{2,6},{3,7},{4,0},{5,1},{6,2},{7,3},{8,12},{9,13},{10,... | collective-permute-start | bytes 614408 | tf_op jit(solution)/shard_map/ppermute | solution.py:262
  115.2 7.1 %collective-permute-start.56 = (bf16[80,1280]{1,0:T(8,128)(2,1)S(1)}, bf16[80,1280]{1,0:T(8,128)(2,1)S(1)}, u32[]{:S(2)}, u32[]{:S(2)}) collective-permute-start(bf16[80,1280]{1,0:T(8,128)(2,1)S(1)} %multiply_convert_fusion), channel_id=1, source_target_pairs={{0,16},{1,17},{2,18},{3,19},{4,20},{5,21},{6,22},{7,23},{8,24},{9,... | collective-permute-start | bytes 614408 | tf_op jit(solution)/shard_map/ppermute | solution.py:322
  116.4 5.9 %collective-permute-start.55 = (bf16[80,1280]{1,0:T(8,128)(2,1)S(1)}, bf16[80,1280]{1,0:T(8,128)(2,1)S(1)}, u32[]{:S(2)}, u32[]{:S(2)}) collective-permute-start(bf16[80,1280]{1,0:T(8,128)(2,1)S(1)} %multiply_convert_fusion), channel_id=1, source_target_pairs={{0,8},{1,9},{2,10},{3,11},{4,12},{5,13},{6,14},{7,15},{8,0},{9,1},... | collective-permute-start | bytes 614408 | tf_op jit(solution)/shard_map/ppermute | solution.py:323
  122.3 1.5 %collective-permute-start.57 = (bf16[80,1280]{1,0:T(8,128)(2,1)S(1)}, bf16[80,1280]{1,0:T(8,128)(2,1)S(1)}, u32[]{:S(2)}, u32[]{:S(2)}) collective-permute-start(bf16[80,1280]{1,0:T(8,128)(2,1)S(1)} %collective-permute-done.56), channel_id=1, source_target_pairs={{0,8},{1,9},{2,10},{3,11},{4,12},{5,13},{6,14},{7,15},{8,0},{9,1},... | collective-permute-start | bytes 614408 | tf_op jit(solution)/shard_map/ppermute | solution.py:323
  (3 other events, 2.9 us)

commit v4 on v3

--- a/solution.py
+++ b/solution.py
@@ -237,7 +237,7 @@
     from_z[1] = tied(from_z[1], [from_z[3], normed_rows])
     diagonal = along_x(beside)
     pieces = {0: [w_in, beside, diagonal, core(beside), core(diagonal)]}
-    arrival = [1, 3, 2]
+    arrival = [3, 1, 2]
     for s in arrival:
         a0 = from_z[s]
         a1 = first(a0)
@@ -282,7 +282,7 @@
         weights.append(w)
         moving.append(homeward(s, keep, *sends))
         next(moving[-1])
-        after = advance([[0],[0,1],[0,1,2],[1,2,3],[1,2,3],[3]][at])
+        after = advance([[0],[0,1],[0,2,1],[0,1,2,3],[1,2,3],[2,3]][at])
 
     def call_rows(part, after, out):
         whole = lambda shape: pl.BlockSpec(shape, lambda i, t, c: (0,) * len(shape))
@@ -312,7 +312,7 @@
 
     grad_rows = call_rows(0, after, [])
     after = [grad_rows]
-    for steps in [[0],[0,1],[0,1,2],[1,2,3],[1,2,3],[3]][4:]:
+    for steps in [[0],[0,1],[0,2,1],[0,1,2,3],[1,2,3],[2,3]][4:]:
         after = advance(steps, after)
     grad_rows = call_rows(1, after, [grad_rows])
     scale = 1.0 / math.sqrt(VIS_DEV * n_patch * 4)

time: 125 us -> 121 us (0.968)
  waiting for transfers between devices: 43.5 us -> 41.3 us
    ppermute x2, waiting for transfers between devices: 1.42 us -> 5.11 us  [fast_device(): from_z = {s: up(s)(mine) for s in (1, plan.nz - 1)}]
    ppermute x4, starting transfers between devices: 4.85 us -> 2.7 us  [homeward(): two = tied(second(v), gate)]
    ppermute x1, waiting for transfers between devices: 2.02 us -> 0.01 us  [fast_device(): from_z[2] = up(1)(from_z[1])]
    ppermute x3, waiting for transfers between devices: 6.72 us -> 8.54 us  [homeward(): term = plane if s == 0 else tied(up(-s)(plane), gate or [])]
    ppermute x3, waiting for transfers between devices: 4.8 us -> 3.07 us  [fast_device(): a1 = first(a0)]
    unnamed x18 -> x14, local copies, waits for them, and re-layouts: 4.92 us -> 3.41 us
    ppermute x4, waiting for transfers between devices: 4.11 us -> 2.63 us  [homeward(): two = tied(second(v), gate)]
    ppermute x4, waiting for transfers between devices: 9.62 us -> 8.35 us  [homeward(): one = tied(first(t), gate)]
where the time goes in v4:
time: 121 us
  waiting for transfers between devices  41.3 us (34%)
  starting transfers between devices  38.9 us (32%)
  Pallas kernels  30.2 us (25%)
  local copies, waits for them, and re-layouts  5.82 us (5%)
  other arithmetic  3.54 us (3%)
    pallas_call x4, Pallas kernels, call_chunk(): pl.pallas_call(functools.partial(chunk_kernel, where, len(pieces), len(af...  18.4 us
    pallas_call x2, Pallas kernels, call_rows(): pl.pallas_call(functools.partial(rows_kernel, places, plan.nz, 2 * part),...  10.4 us
    ppermute x3, waiting for transfers between devices, homeward(): term = plane if s == 0 else tied(up(-s)(plane), gate or [])  8.54 us
    ppermute x4, waiting for transfers between devices, homeward(): one = tied(first(t), gate)  8.35 us
    ppermute x6, starting transfers between devices, fast_device(): a2, a3 = (second(a0), second(a1))  5.2 us
    ppermute x1, waiting for transfers between devices, fast_device(): done_x = along_x(done)  5.14 us
    ppermute x2, waiting for transfers between devices, fast_device(): from_z = {s: up(s)(mine) for s in (1, plan.nz - 1)}  5.11 us
    ppermute x16, starting transfers between devices, homeward(): got = [core(send) for send in sends]  4.82 us
  transfers between devices with their start and end apart: 58, of which 19 were waited for; matrix products, arithmetic and copies ran while one was open for 2% of the time, Pallas kernels for 25%

profile of v4, /device:TPU:0, one launch (start us, length us, event | category | flops | bytes accessed | tf_op | source)
XLA Modules:
  0.0 120.7 jit_solution(10768699532451597761)
XLA Ops:
  0.6 0.7 fusion.2
  1.4 1.0 constant_dynamic-slice_fusion
  2.5 3.0 %collective-permute-start.2 = (bf16[88,1280]{1,0:T(8,128)(2,1)S(1)}, bf16[88,1280]{1,0:T(8,128)(2,1)S(1)}, u32[]{:S(2)}, u32[]{:S(2)}) collective-permute-start(bf16[88,1280]{1,0:T(8,128)(2,1)S(1)} %pad_maximum_fusion), channel_id=1, source_target_pairs={{0,1},{1,0},{2,3},{3,2},{4,5},{5,4},{6,7},{7,6},{8,9},{9,8},{10,11... | collective-permute-start | bytes 675848 | tf_op jit(solution)/shard_map/ppermute | solution.py:221
  5.5 3.6 %collective-permute-start.12 = (bf16[88,1280]{1,0:T(8,128)(2,1)S(1)}, bf16[88,1280]{1,0:T(8,128)(2,1)S(1)}, u32[]{:S(2)}, u32[]{:S(2)}) collective-permute-start(bf16[88,1280]{1,0:T(8,128)(2,1)S(1)} %pad_maximum_fusion), channel_id=1, source_target_pairs={{0,6},{1,7},{2,0},{3,1},{4,2},{5,3},{6,4},{7,5},{8,14},{9,15},{10,... | collective-permute-start | bytes 675848 | tf_op jit(solution)/shard_map/ppermute | solution.py:220
  9.1 1.9 %collective-permute-done.2.refs_1_ = bf16[88,1280]{1,0:T(8,128)(2,1)S(1)} collective-permute-done((bf16[88,1280]{1,0:T(8,128)(2,1)S(1)}, bf16[88,1280]{1,0:T(8,128)(2,1)S(1)}, u32[]{:S(2)}, u32[]{:S(2)}) %collective-permute-start.2) | collective-permute-done | bytes 225312 | tf_op jit(solution)/shard_map/ppermute | solution.py:221
  11.1 1.7 %collective-permute-start.3 = (bf16[88,1280]{1,0:T(8,128)(2,1)S(1)}, bf16[88,1280]{1,0:T(8,128)(2,1)S(1)}, u32[]{:S(2)}, u32[]{:S(2)}) collective-permute-start(bf16[88,1280]{1,0:T(8,128)(2,1)S(1)} %collective-permute-done.2.refs_1_), channel_id=1, source_target_pairs={{0,16},{1,17},{2,18},{3,19},{4,20},{5,21},{6,22},{7,23},{8,24},{9,... | collective-permute-start | bytes 675848 | tf_op jit(solution)/shard_map/ppermute | solution.py:238
  12.8 2.3 %collective-permute-done.12.refs_0_ = bf16[88,1280]{1,0:T(8,128)(2,1)S(1)} collective-permute-done((bf16[88,1280]{1,0:T(8,128)(2,1)S(1)}, bf16[88,1280]{1,0:T(8,128)(2,1)S(1)}, u32[]{:S(2)}, u32[]{:S(2)}) %collective-permute-start.12) | collective-permute-done | bytes 225312 | tf_op jit(solution)/shard_map/ppermute | solution.py:220
  15.1 1.5 %collective-permute-start.13 = (bf16[88,1280]{1,0:T(8,128)(2,1)S(1)}, bf16[88,1280]{1,0:T(8,128)(2,1)S(1)}, u32[]{:S(2)}, u32[]{:S(2)}) collective-permute-start(bf16[88,1280]{1,0:T(8,128)(2,1)S(1)} %collective-permute-done.12.refs_0_), channel_id=1, source_target_pairs={{0,16},{1,17},{2,18},{3,19},{4,20},{5,21},{6,22},{7,23},{8,9},{9,8... | collective-permute-start | bytes 675848 | tf_op jit(solution)/shard_map/ppermute | solution.py:243
  16.6 2.8 %collective-permute-done.refs_0_ = bf16[88,1280]{1,0:T(8,128)(2,1)S(1)} collective-permute-done((bf16[88,1280]{1,0:T(8,128)(2,1)S(1)}, bf16[88,1280]{1,0:T(8,128)(2,1)S(1)}, u32[]{:S(2)}, u32[]{:S(2)}) %collective-permute-start) | collective-permute-done | bytes 225312 | tf_op jit(solution)/shard_map/ppermute | solution.py:220
  19.4 1.6 %collective-permute-start.1 = (bf16[88,1280]{1,0:T(8,128)(2,1)S(1)}, bf16[88,1280]{1,0:T(8,128)(2,1)S(1)}, u32[]{:S(2)}, u32[]{:S(2)}) collective-permute-start(bf16[88,1280]{1,0:T(8,128)(2,1)S(1)} %collective-permute-done.refs_0_), channel_id=1, source_target_pairs={{0,2},{1,3},{2,4},{3,5},{4,6},{5,7},{6,0},{7,1},{8,10},{9,11},{10,... | collective-permute-start | bytes 675848 | tf_op jit(solution)/shard_map/ppermute | solution.py:236
  21.0 0.5 collective-permute-start.5
  21.5 0.7 reshape.20
  22.3 0.5 collective-permute-start.14
  22.8 1.5 %collective-permute-start.15 = (bf16[88,1280]{1,0:T(8,128)(2,1)S(1)}, bf16[88,1280]{1,0:T(8,128)(2,1)S(1)}, u32[]{:S(2)}, u32[]{:S(2)}) collective-permute-start(bf16[88,1280]{1,0:T(8,128)(2,1)S(1)} %collective-permute-done.13.refs_1_), channel_id=1, source_target_pairs={{0,1},{1,0},{2,3},{3,2},{4,5},{5,4},{6,7},{7,6},{8,24},{9,25},{10,... | collective-permute-start | bytes 675848 | tf_op jit(solution)/shard_map/ppermute | solution.py:244
  24.3 0.7 dynamic-slice_bitcast_fusion.table_ref
  25.0 1.5 %copy-done.1 = bf16[704,1280]{1,0:T(8,128)(2,1)S(1)} copy-done((bf16[704,1280]{1,0:T(8,128)(2,1)S(1)}, bf16[704,1280]{1,0:T(8,128)(2,1)}, u32[]{:S(2)}) %copy-start.1) | copy-done | bytes 1802264
  26.5 0.7 copy-done.3
  27.2 0.7 copy-done.6
  27.9 1.5 %norm.1.n_ref = bf16[704,1280]{1,0:T(8,128)(2,1)S(1)} custom-call(bf16[704,1280]{1,0:T(8,128)(2,1)S(1)} %copy-done.1, f32[1280]{0:T(1024)S(1)} %copy-done.3, f32[1280]{0:T(1024)S(1)} %copy-done.6), custom_call_target="tpu_custom_call" | custom-call | tf_op jit(solution)/shard_map/norm/pallas_call | solution.py:222
  29.4 0.5 copy-done
  29.9 4.5 %chunk_0.1 = (bf16[320,1280]{1,0:T(8,128)(2,1)S(1)}, bf16[80,1280]{1,0:T(8,128)(2,1)S(1)}, bf16[80,1280]{1,0:T(8,128)(2,1)S(1)}, bf16[80,1280]{1,0:T(8,128)(2,1)...) custom-call(s32[30]{0:T(128)S(1)} %dynamic-slice_bitcast_fusion.table_ref, ...), custom_call_target="tpu_custom_call" | custom-call | flops 450560 | tf_op jit(solution)/shard_map/chunk_0/pallas_call | solution.py:155
  34.5 0.5 collective-permute-start.8
  35.1 0.4 collective-permute-start.17
  36.4 1.6 %collective-permute-start.9 = (bf16[160,1280]{1,0:T(8,128)(2,1)S(1)}, bf16[160,1280]{1,0:T(8,128)(2,1)S(1)}, u32[]{:S(2)}, u32[]{:S(2)}) collective-permute-start(bf16[160,1280]{1,0:T(8,128)(2,1)S(1)} %add_convert_fusion.3), channel_id=1, source_target_pairs={{0,16},{1,17},{2,18},{3,19},{4,20},{5,21},{6,22},{7,23},{8,9},{9,8... | collective-permute-start | bytes 1228808 | tf_op jit(solution)/shard_map/ppermute | solution.py:255
  37.9 0.5 collective-permute-start.24
  38.5 4.6 %chunk_3.1 = (bf16[320,1280]{1,0:T(8,128)(2,1)S(1)}, bf16[80,1280]{1,0:T(8,128)(2,1)S(1)}, bf16[80,1280]{1,0:T(8,128)(2,1)S(1)}, bf16[80,1280]{1,0:T(8,128)(2,1)...) custom-call(s32[30]{0:T(128)S(1)} %dynamic-slice_bitcast_fusion.table_ref, ...), custom_call_target="tpu_custom_call" | custom-call | flops 450560 | tf_op jit(solution)/shard_map/chunk_3/pallas_call | solution.py:155
  43.1 0.6 collective-permute-start.21
  43.6 0.5 collective-permute-start.25
  44.1 3.1 %collective-permute-done.24.refs_1_ = bf16[88,1280]{1,0:T(8,128)(2,1)S(1)} collective-permute-done((bf16[88,1280]{1,0:T(8,128)(2,1)S(1)}, bf16[88,1280]{1,0:T(8,128)(2,1)S(1)}, u32[]{:S(2)}, u32[]{:S(2)}) %collective-permute-start.24) | collective-permute-done | bytes 225312 | tf_op jit(solution)/shard_map/ppermute | solution.py:243
  47.2 0.5 collective-permute-start.26
  47.7 1.2 %collective-permute-start.28 = (bf16[88,1280]{1,0:T(8,128)(2,1)S(1)}, bf16[88,1280]{1,0:T(8,128)(2,1)S(1)}, u32[]{:S(2)}, u32[]{:S(2)}) collective-permute-start(bf16[88,1280]{1,0:T(8,128)(2,1)S(1)} %collective-permute-done.24.refs_1_), channel_id=1, source_target_pairs={{0,8},{1,9},{2,10},{3,11},{4,12},{5,13},{6,14},{7,15},{8,0},{9,1},... | collective-permute-start | bytes 675848 | tf_op jit(solution)/shard_map/ppermute | solution.py:245
  49.1 0.5 collective-permute-done.25.refs_2_
  49.6 1.5 %collective-permute-start.36 = (bf16[88,1280]{1,0:T(8,128)(2,1)S(1)}, bf16[88,1280]{1,0:T(8,128)(2,1)S(1)}, u32[]{:S(2)}, u32[]{:S(2)}) collective-permute-start(bf16[88,1280]{1,0:T(8,128)(2,1)S(1)} %collective-permute-done.1.refs_0_), channel_id=1, source_target_pairs={{0,16},{1,17},{2,18},{3,19},{4,20},{5,21},{6,22},{7,23},{8,9},{9,8... | collective-permute-start | bytes 675848 | tf_op jit(solution)/shard_map/ppermute | solution.py:243
  51.1 3.0 %collective-permute-done.26.refs_3_ = bf16[88,1280]{1,0:T(8,128)(2,1)S(1)} collective-permute-done((bf16[88,1280]{1,0:T(8,128)(2,1)S(1)}, bf16[88,1280]{1,0:T(8,128)(2,1)S(1)}, u32[]{:S(2)}, u32[]{:S(2)}) %collective-permute-start.26) | collective-permute-done | bytes 225312 | tf_op jit(solution)/shard_map/ppermute | solution.py:244
  54.1 0.5 collective-permute-start.30
  54.7 0.5 collective-permute-start.11
  55.3 1.6 %collective-permute-start.37 = (bf16[88,1280]{1,0:T(8,128)(2,1)S(1)}, bf16[88,1280]{1,0:T(8,128)(2,1)S(1)}, u32[]{:S(2)}, u32[]{:S(2)}) collective-permute-start(bf16[88,1280]{1,0:T(8,128)(2,1)S(1)} %collective-permute-done.1.refs_0_), channel_id=1, source_target_pairs={{0,1},{1,0},{2,3},{3,2},{4,5},{5,4},{6,7},{7,6},{8,24},{9,25},{10,... | collective-permute-start | bytes 675848 | tf_op jit(solution)/shard_map/ppermute | solution.py:244
  56.9 0.6 collective-permute-start.38
  57.4 4.7 %chunk_1.1 = (bf16[320,1280]{1,0:T(8,128)(2,1)S(1)}, bf16[80,1280]{1,0:T(8,128)(2,1)S(1)}, bf16[80,1280]{1,0:T(8,128)(2,1)S(1)}, bf16[80,1280]{1,0:T(8,128)(2,1)...) custom-call(s32[30]{0:T(128)S(1)} %dynamic-slice_bitcast_fusion.table_ref, ...), custom_call_target="tpu_custom_call" | custom-call | flops 450560 | tf_op jit(solution)/shard_map/chunk_1/pallas_call | solution.py:155
  62.2 1.5 %collective-permute-start.31 = (bf16[80,1280]{1,0:T(8,128)(2,1)S(1)}, bf16[80,1280]{1,0:T(8,128)(2,1)S(1)}, u32[]{:S(2)}, u32[]{:S(2)}) collective-permute-start(bf16[80,1280]{1,0:T(8,128)(2,1)S(1)} %get-tuple-element.65), channel_id=1, source_target_pairs={{0,8},{1,9},{2,10},{3,11},{4,12},{5,13},{6,14},{7,15},{8,0},{9,1},... | collective-permute-start | bytes 614408 | tf_op jit(solution)/shard_map/ppermute | solution.py:250
  63.9 0.9 collective-permute-done.31
  64.8 0.4 collective-permute-start.33
  65.2 0.4 collective-permute-start.23
  65.8 0.5 collective-permute-start.41
  66.3 6.8 %collective-permute-done.23 = bf16[160,1280]{1,0:T(8,128)(2,1)S(1)} collective-permute-done((bf16[160,1280]{1,0:T(8,128)(2,1)S(1)}, bf16[160,1280]{1,0:T(8,128)(2,1)S(1)}, u32[]{:S(2)}, u32[]{:S(2)}) %collective-permute-start.23) | collective-permute-done | bytes 409632 | tf_op jit(solution)/shard_map/ppermute | solution.py:255
  73.2 0.4 collective-permute-start.34
  74.6 1.4 %collective-permute-start.45 = (bf16[160,1280]{1,0:T(8,128)(2,1)S(1)}, bf16[160,1280]{1,0:T(8,128)(2,1)S(1)}, u32[]{:S(2)}, u32[]{:S(2)}) collective-permute-start(bf16[160,1280]{1,0:T(8,128)(2,1)S(1)} %add_convert_fusion.1), channel_id=1, source_target_pairs={{0,16},{1,17},{2,18},{3,19},{4,20},{5,21},{6,22},{7,23},{8,9},{9,8... | collective-permute-start | bytes 1228808 | tf_op jit(solution)/shard_map/ppermute | solution.py:255
  76.0 4.5 %chunk_2.1 = (bf16[320,1280]{1,0:T(8,128)(2,1)S(1)}, bf16[80,1280]{1,0:T(8,128)(2,1)S(1)}, bf16[80,1280]{1,0:T(8,128)(2,1)S(1)}, bf16[80,1280]{1,0:T(8,128)(2,1)...) custom-call(s32[30]{0:T(128)S(1)} %dynamic-slice_bitcast_fusion.table_ref, ...), custom_call_target="tpu_custom_call" | custom-call | flops 450560 | tf_op jit(solution)/shard_map/chunk_2/pallas_call | solution.py:155
  80.8 0.5 collective-permute-start.46
  81.4 1.5 %collective-permute-done.45 = bf16[160,1280]{1,0:T(8,128)(2,1)S(1)} collective-permute-done((bf16[160,1280]{1,0:T(8,128)(2,1)S(1)}, bf16[160,1280]{1,0:T(8,128)(2,1)S(1)}, u32[]{:S(2)}, u32[]{:S(2)}) %collective-permute-start.45) | collective-permute-done | bytes 409632 | tf_op jit(solution)/shard_map/ppermute | solution.py:255
  83.4 1.0 collective-permute-start.48
  84.5 1.3 %collective-permute-start.51 = (bf16[160,1280]{1,0:T(8,128)(2,1)S(1)}, bf16[160,1280]{1,0:T(8,128)(2,1)S(1)}, u32[]{:S(2)}, u32[]{:S(2)}) collective-permute-start(bf16[160,1280]{1,0:T(8,128)(2,1)S(1)} %add_convert_fusion), channel_id=1, source_target_pairs={{0,16},{1,17},{2,18},{3,19},{4,20},{5,21},{6,22},{7,23},{8,9},{9,8... | collective-permute-start | bytes 1228808 | tf_op jit(solution)/shard_map/ppermute | solution.py:255
  85.8 5.2 %grad_rows_0.1.refs_8_ = bf16[704,1280]{1,0:T(8,128)(2,1)} custom-call(s32[30]{0:T(128)S(1)} %dynamic-slice_bitcast_fusion.table_ref, s32[1,8]{1,0:T(1,128)S(1)} %copy-done.5, bf16[704,1280]{1,0:T(8,128)(2,1)S(1)} %copy-done.1, f32[1280]{0:T(1024)S(1)} %copy-done.4, bf16[704,640]{1,0:T(8,128)(2,1)S(1)} %get-tuple-element.79.refs_0_, ...), custom_call_target="tpu_custom_call" | custom-call | flops 450560 | tf_op jit(solution)/shard_map/grad_rows_0/pallas_call | solution.py:291
  90.9 1.3 %collective-permute-done.35 = bf16[80,1280]{1,0:T(8,128)(2,1)S(1)} collective-permute-done((bf16[80,1280]{1,0:T(8,128)(2,1)S(1)}, bf16[80,1280]{1,0:T(8,128)(2,1)S(1)}, u32[]{:S(2)}, u32[]{:S(2)}) %collective-permute-start.35) | collective-permute-done | bytes 204832 | tf_op jit(solution)/shard_map/ppermute | solution.py:262
  92.4 3.0 %collective-permute-start.49 = (bf16[80,1280]{1,0:T(8,128)(2,1)S(1)}, bf16[80,1280]{1,0:T(8,128)(2,1)S(1)}, u32[]{:S(2)}, u32[]{:S(2)}) collective-permute-start(bf16[80,1280]{1,0:T(8,128)(2,1)S(1)} %add_convert_fusion.6), channel_id=1, source_target_pairs={{0,6},{1,7},{2,0},{3,1},{4,2},{5,3},{6,4},{7,5},{8,14},{9,15},{10,... | collective-permute-start | bytes 614408 | tf_op jit(solution)/shard_map/ppermute | solution.py:262
  95.4 0.8 collective-permute-start.53
  96.3 2.5 %collective-permute-done.49 = bf16[80,1280]{1,0:T(8,128)(2,1)S(1)} collective-permute-done((bf16[80,1280]{1,0:T(8,128)(2,1)S(1)}, bf16[80,1280]{1,0:T(8,128)(2,1)S(1)}, u32[]{:S(2)}, u32[]{:S(2)}) %collective-permute-start.49) | collective-permute-done | bytes 204832 | tf_op jit(solution)/shard_map/ppermute | solution.py:262
  98.8 2.4 %collective-permute-done.53 = bf16[80,1280]{1,0:T(8,128)(2,1)S(1)} collective-permute-done((bf16[80,1280]{1,0:T(8,128)(2,1)S(1)}, bf16[80,1280]{1,0:T(8,128)(2,1)S(1)}, u32[]{:S(2)}, u32[]{:S(2)}) %collective-permute-start.53) | collective-permute-done | bytes 204832 | tf_op jit(solution)/shard_map/ppermute | solution.py:258
  101.4 5.2 %grad_rows_1.1 = bf16[704,1280]{1,0:T(8,128)(2,1)} custom-call(s32[30]{0:T(128)S(1)} %dynamic-slice_bitcast_fusion.table_ref, s32[1,8]{1,0:T(1,128)S(1)} %copy-done.5, bf16[704,1280]{1,0:T(8,128)(2,1)S(1)} %copy-done.1, f32[1280]{0:T(1024)S(1)} %copy-done.4, bf16[704,640]{1,0:T(8,128)(2,1)S(1)} %get-tuple-element.79.refs_0_, ...), custom_call_target="tpu_custom_call", output_to_operand_aliasing={{}: (12, {})} | custom-call | flops 450560 | tf_op jit(solution)/shard_map/grad_rows_1/pallas_call | solution.py:291
  106.7 4.7 %collective-permute-done.54 = bf16[80,1280]{1,0:T(8,128)(2,1)S(1)} collective-permute-done((bf16[80,1280]{1,0:T(8,128)(2,1)S(1)}, bf16[80,1280]{1,0:T(8,128)(2,1)S(1)}, u32[]{:S(2)}, u32[]{:S(2)}) %collective-permute-start.54) | collective-permute-done | bytes 204832 | tf_op jit(solution)/shard_map/ppermute | solution.py:262
  111.5 1.2 %collective-permute-start.56 = (bf16[80,1280]{1,0:T(8,128)(2,1)S(1)}, bf16[80,1280]{1,0:T(8,128)(2,1)S(1)}, u32[]{:S(2)}, u32[]{:S(2)}) collective-permute-start(bf16[80,1280]{1,0:T(8,128)(2,1)S(1)} %multiply_convert_fusion), channel_id=1, source_target_pairs={{0,16},{1,17},{2,18},{3,19},{4,20},{5,21},{6,22},{7,23},{8,24},{9,... | collective-permute-start | bytes 614408 | tf_op jit(solution)/shard_map/ppermute | solution.py:322
  112.8 5.1 %collective-permute-done.56 = bf16[80,1280]{1,0:T(8,128)(2,1)S(1)} collective-permute-done((bf16[80,1280]{1,0:T(8,128)(2,1)S(1)}, bf16[80,1280]{1,0:T(8,128)(2,1)S(1)}, u32[]{:S(2)}, u32[]{:S(2)}) %collective-permute-start.56) | collective-permute-done | bytes 204832 | tf_op jit(solution)/shard_map/ppermute | solution.py:322
  117.9 1.4 %collective-permute-done.57 = bf16[80,1280]{1,0:T(8,128)(2,1)S(1)} collective-permute-done((bf16[80,1280]{1,0:T(8,128)(2,1)S(1)}, bf16[80,1280]{1,0:T(8,128)(2,1)S(1)}, u32[]{:S(2)}, u32[]{:S(2)}) %collective-permute-start.57) | collective-permute-done | bytes 204832 | tf_op jit(solution)/shard_map/ppermute | solution.py:323
  119.5 1.3 %maximum_convert_fusion = f32[320,1280]{1,0:T(8,128)} fusion(bf16[80,1280]{1,0:T(8,128)(2,1)S(1)} %get-tuple-element.99, bf16[80,1280]{1,0:T(8,128)(2,1)S(1)} %get-tuple-element.100, bf16[80,1280]{1,0:T(8,128)(2,1)S(1)} %get-tuple-element.101, bf16[80,1280]{1,0:T(8,128)(2,1)S(1)} %get-tuple-element.98), kind=kLoop, calls=%fused_computation | loop fusion | flops 3276800 | bytes 2457600 | tf_op jit(solution)/shard_map/concatenate | solution.py:325
  (99 shorter events, 4.4 us)
Async XLA Ops:
  1.4 27.9 %copy-start.2 = (bf16[320,1280]{1,0:T(8,128)(2,1)S(1)}, bf16[320,1280]{1,0:T(8,128)(2,1)}, u32[]{:S(2)}) copy-start(bf16[320,1280]{1,0:T(8,128)(2,1)} %refs_0_.1) | copy-start | bytes 2457604
  2.5 8.5 %collective-permute-start.2 = (bf16[88,1280]{1,0:T(8,128)(2,1)S(1)}, bf16[88,1280]{1,0:T(8,128)(2,1)S(1)}, u32[]{:S(2)}, u32[]{:S(2)}) collective-permute-start(bf16[88,1280]{1,0:T(8,128)(2,1)S(1)} %pad_maximum_fusion), channel_id=1, source_target_pairs={{0,1},{1,0},{2,3},{3,2},{4,5},{5,4},{6,7},{7,6},{8,9},{9,8},{10,11... | collective-permute-start | bytes 675848 | tf_op jit(solution)/shard_map/ppermute | solution.py:221
  5.5 9.6 %collective-permute-start.12 = (bf16[88,1280]{1,0:T(8,128)(2,1)S(1)}, bf16[88,1280]{1,0:T(8,128)(2,1)S(1)}, u32[]{:S(2)}, u32[]{:S(2)}) collective-permute-start(bf16[88,1280]{1,0:T(8,128)(2,1)S(1)} %pad_maximum_fusion), channel_id=1, source_target_pairs={{0,6},{1,7},{2,0},{3,1},{4,2},{5,3},{6,4},{7,5},{8,14},{9,15},{10,... | collective-permute-start | bytes 675848 | tf_op jit(solution)/shard_map/ppermute | solution.py:220
  9.1 10.2 %collective-permute-start = (bf16[88,1280]{1,0:T(8,128)(2,1)S(1)}, bf16[88,1280]{1,0:T(8,128)(2,1)S(1)}, u32[]{:S(2)}, u32[]{:S(2)}) collective-permute-start(bf16[88,1280]{1,0:T(8,128)(2,1)S(1)} %pad_maximum_fusion), channel_id=1, source_target_pairs={{0,2},{1,3},{2,4},{3,5},{4,6},{5,7},{6,0},{7,1},{8,10},{9,11},{10,... | collective-permute-start | bytes 675848 | tf_op jit(solution)/shard_map/ppermute | solution.py:220
  11.1 9.9 %collective-permute-start.3 = (bf16[88,1280]{1,0:T(8,128)(2,1)S(1)}, bf16[88,1280]{1,0:T(8,128)(2,1)S(1)}, u32[]{:S(2)}, u32[]{:S(2)}) collective-permute-start(bf16[88,1280]{1,0:T(8,128)(2,1)S(1)} %collective-permute-done.2.refs_1_), channel_id=1, source_target_pairs={{0,16},{1,17},{2,18},{3,19},{4,20},{5,21},{6,22},{7,23},{8,24},{9,... | collective-permute-start | bytes 675848 | tf_op jit(solution)/shard_map/ppermute | solution.py:238
  15.1 7.7 %collective-permute-start.13 = (bf16[88,1280]{1,0:T(8,128)(2,1)S(1)}, bf16[88,1280]{1,0:T(8,128)(2,1)S(1)}, u32[]{:S(2)}, u32[]{:S(2)}) collective-permute-start(bf16[88,1280]{1,0:T(8,128)(2,1)S(1)} %collective-permute-done.12.refs_0_), channel_id=1, source_target_pairs={{0,16},{1,17},{2,18},{3,19},{4,20},{5,21},{6,22},{7,23},{8,9},{9,8... | collective-permute-start | bytes 675848 | tf_op jit(solution)/shard_map/ppermute | solution.py:243
  19.4 10.0 %collective-permute-start.1 = (bf16[88,1280]{1,0:T(8,128)(2,1)S(1)}, bf16[88,1280]{1,0:T(8,128)(2,1)S(1)}, u32[]{:S(2)}, u32[]{:S(2)}) collective-permute-start(bf16[88,1280]{1,0:T(8,128)(2,1)S(1)} %collective-permute-done.refs_0_), channel_id=1, source_target_pairs={{0,2},{1,3},{2,4},{3,5},{4,6},{5,7},{6,0},{7,1},{8,10},{9,11},{10,... | collective-permute-start | bytes 675848 | tf_op jit(solution)/shard_map/ppermute | solution.py:236
  21.0 8.4 %collective-permute-start.4 = (bf16[88,1280]{1,0:T(8,128)(2,1)S(1)}, bf16[88,1280]{1,0:T(8,128)(2,1)S(1)}, u32[]{:S(2)}, u32[]{:S(2)}) collective-permute-start(bf16[88,1280]{1,0:T(8,128)(2,1)S(1)} %collective-permute-done.2.refs_1_), channel_id=1, source_target_pairs={{0,8},{1,9},{2,10},{3,11},{4,12},{5,13},{6,14},{7,15},{8,0},{9,1},... | collective-permute-start | bytes 675848 | tf_op jit(solution)/shard_map/ppermute | solution.py:239
  21.0 8.4 %collective-permute-start.5 = (bf16[88,1280]{1,0:T(8,128)(2,1)S(1)}, bf16[88,1280]{1,0:T(8,128)(2,1)S(1)}, u32[]{:S(2)}, u32[]{:S(2)}) collective-permute-start(bf16[88,1280]{1,0:T(8,128)(2,1)S(1)} %collective-permute-done.3.refs_2_), channel_id=1, source_target_pairs={{0,8},{1,9},{2,10},{3,11},{4,12},{5,13},{6,14},{7,15},{8,0},{9,1},... | collective-permute-start | bytes 675848 | tf_op jit(solution)/shard_map/ppermute | solution.py:239
  22.3 12.8 %collective-permute-start.14 = (bf16[88,1280]{1,0:T(8,128)(2,1)S(1)}, bf16[88,1280]{1,0:T(8,128)(2,1)S(1)}, u32[]{:S(2)}, u32[]{:S(2)}) collective-permute-start(bf16[88,1280]{1,0:T(8,128)(2,1)S(1)} %collective-permute-done.12.refs_0_), channel_id=1, source_target_pairs={{0,1},{1,0},{2,3},{3,2},{4,5},{5,4},{6,7},{7,6},{8,24},{9,25},{10,... | collective-permute-start | bytes 675848 | tf_op jit(solution)/shard_map/ppermute | solution.py:244
  22.8 12.7 %collective-permute-start.15 = (bf16[88,1280]{1,0:T(8,128)(2,1)S(1)}, bf16[88,1280]{1,0:T(8,128)(2,1)S(1)}, u32[]{:S(2)}, u32[]{:S(2)}) collective-permute-start(bf16[88,1280]{1,0:T(8,128)(2,1)S(1)} %collective-permute-done.13.refs_1_), channel_id=1, source_target_pairs={{0,1},{1,0},{2,3},{3,2},{4,5},{5,4},{6,7},{7,6},{8,24},{9,25},{10,... | collective-permute-start | bytes 675848 | tf_op jit(solution)/shard_map/ppermute | solution.py:244
  25.0 1.5 %copy-start.1 = (bf16[704,1280]{1,0:T(8,128)(2,1)S(1)}, bf16[704,1280]{1,0:T(8,128)(2,1)}, u32[]{:S(2)}) copy-start(bf16[704,1280]{1,0:T(8,128)(2,1)} %rows_ref.5) | copy-start | bytes 5406724
  26.5 0.7 copy-start.3
  27.9 2.0 %copy-start = (bf16[704,2560]{1,0:T(8,128)(2,1)S(1)}, bf16[704,2560]{1,0:T(8,128)(2,1)}, u32[]{:S(2)}) copy-start(bf16[704,2560]{1,0:T(8,128)(2,1)} %g_ref.7) | copy-start | bytes 10813444
  27.9 2.0 %copy-start.5 = (s32[1,8]{1,0:T(1,128)S(1)}, s32[1,8]{1,0:T(1,128)}, u32[]{:S(2)}) copy-start(s32[1,8]{1,0:T(1,128)} %counts_ref.11) | copy-start | bytes 100
  34.4 1.5 %collective-permute-start.7 = (bf16[80,1280]{1,0:T(8,128)(2,1)S(1)}, bf16[80,1280]{1,0:T(8,128)(2,1)S(1)}, u32[]{:S(2)}, u32[]{:S(2)}) collective-permute-start(bf16[80,1280]{1,0:T(8,128)(2,1)S(1)} %get-tuple-element.53), channel_id=1, source_target_pairs={{0,8},{1,9},{2,10},{3,11},{4,12},{5,13},{6,14},{7,15},{8,0},{9,1},... | collective-permute-start | bytes 614408 | tf_op jit(solution)/shard_map/ppermute | solution.py:250
  34.5 1.7 %collective-permute-start.8 = (bf16[80,1280]{1,0:T(8,128)(2,1)S(1)}, bf16[80,1280]{1,0:T(8,128)(2,1)S(1)}, u32[]{:S(2)}, u32[]{:S(2)}) collective-permute-start(bf16[80,1280]{1,0:T(8,128)(2,1)S(1)} %get-tuple-element.54), channel_id=1, source_target_pairs={{0,8},{1,9},{2,10},{3,11},{4,12},{5,13},{6,14},{7,15},{8,0},{9,1},... | collective-permute-start | bytes 614408 | tf_op jit(solution)/shard_map/ppermute | solution.py:250
  35.0 2.9 %collective-permute-start.16 = (bf16[88,1280]{1,0:T(8,128)(2,1)S(1)}, bf16[88,1280]{1,0:T(8,128)(2,1)S(1)}, u32[]{:S(2)}, u32[]{:S(2)}) collective-permute-start(bf16[88,1280]{1,0:T(8,128)(2,1)S(1)} %collective-permute-done.12.refs_0_), channel_id=1, source_target_pairs={{0,8},{1,9},{2,10},{3,11},{4,12},{5,13},{6,14},{7,15},{8,0},{9,1},... | collective-permute-start | bytes 675848 | tf_op jit(solution)/shard_map/ppermute | solution.py:245
  35.1 3.4 %collective-permute-start.17 = (bf16[88,1280]{1,0:T(8,128)(2,1)S(1)}, bf16[88,1280]{1,0:T(8,128)(2,1)S(1)}, u32[]{:S(2)}, u32[]{:S(2)}) collective-permute-start(bf16[88,1280]{1,0:T(8,128)(2,1)S(1)} %collective-permute-done.13.refs_1_), channel_id=1, source_target_pairs={{0,8},{1,9},{2,10},{3,11},{4,12},{5,13},{6,14},{7,15},{8,0},{9,1},... | collective-permute-start | bytes 675848 | tf_op jit(solution)/shard_map/ppermute | solution.py:245
  35.5 2.9 %collective-permute-start.18 = (bf16[88,1280]{1,0:T(8,128)(2,1)S(1)}, bf16[88,1280]{1,0:T(8,128)(2,1)S(1)}, u32[]{:S(2)}, u32[]{:S(2)}) collective-permute-start(bf16[88,1280]{1,0:T(8,128)(2,1)S(1)} %collective-permute-done.14.refs_2_), channel_id=1, source_target_pairs={{0,8},{1,9},{2,10},{3,11},{4,12},{5,13},{6,14},{7,15},{8,0},{9,1},... | collective-permute-start | bytes 675848 | tf_op jit(solution)/shard_map/ppermute | solution.py:245
  36.0 2.5 %collective-permute-start.19 = (bf16[88,1280]{1,0:T(8,128)(2,1)S(1)}, bf16[88,1280]{1,0:T(8,128)(2,1)S(1)}, u32[]{:S(2)}, u32[]{:S(2)}) collective-permute-start(bf16[88,1280]{1,0:T(8,128)(2,1)S(1)} %collective-permute-done.15.refs_3_), channel_id=1, source_target_pairs={{0,8},{1,9},{2,10},{3,11},{4,12},{5,13},{6,14},{7,15},{8,0},{9,1},... | collective-permute-start | bytes 675848 | tf_op jit(solution)/shard_map/ppermute | solution.py:245
  36.4 10.9 %collective-permute-start.9 = (bf16[160,1280]{1,0:T(8,128)(2,1)S(1)}, bf16[160,1280]{1,0:T(8,128)(2,1)S(1)}, u32[]{:S(2)}, u32[]{:S(2)}) collective-permute-start(bf16[160,1280]{1,0:T(8,128)(2,1)S(1)} %add_convert_fusion.3), channel_id=1, source_target_pairs={{0,16},{1,17},{2,18},{3,19},{4,20},{5,21},{6,22},{7,23},{8,9},{9,8... | collective-permute-start | bytes 1228808 | tf_op jit(solution)/shard_map/ppermute | solution.py:255
  37.9 9.3 %collective-permute-start.24 = (bf16[88,1280]{1,0:T(8,128)(2,1)S(1)}, bf16[88,1280]{1,0:T(8,128)(2,1)S(1)}, u32[]{:S(2)}, u32[]{:S(2)}) collective-permute-start(bf16[88,1280]{1,0:T(8,128)(2,1)S(1)} %collective-permute-done.refs_0_), channel_id=1, source_target_pairs={{0,16},{1,17},{2,18},{3,19},{4,20},{5,21},{6,22},{7,23},{8,9},{9,8... | collective-permute-start | bytes 675848 | tf_op jit(solution)/shard_map/ppermute | solution.py:243
  38.5 9.3 %collective-permute-start.10 = (bf16[80,1280]{1,0:T(8,128)(2,1)S(1)}, bf16[80,1280]{1,0:T(8,128)(2,1)S(1)}, u32[]{:S(2)}, u32[]{:S(2)}) collective-permute-start(bf16[80,1280]{1,0:T(8,128)(2,1)S(1)} %get-tuple-element.55), channel_id=1, source_target_pairs={{0,8},{1,9},{2,10},{3,11},{4,12},{5,13},{6,14},{7,15},{8,0},{9,1},... | collective-permute-start | bytes 614408 | tf_op jit(solution)/shard_map/ppermute | solution.py:250
  43.1 5.9 %collective-permute-start.21 = (bf16[80,1280]{1,0:T(8,128)(2,1)S(1)}, bf16[80,1280]{1,0:T(8,128)(2,1)S(1)}, u32[]{:S(2)}, u32[]{:S(2)}) collective-permute-start(bf16[80,1280]{1,0:T(8,128)(2,1)S(1)} %get-tuple-element.59), channel_id=1, source_target_pairs={{0,8},{1,9},{2,10},{3,11},{4,12},{5,13},{6,14},{7,15},{8,0},{9,1},... | collective-permute-start | bytes 614408 | tf_op jit(solution)/shard_map/ppermute | solution.py:250
  43.6 6.0 %collective-permute-start.25 = (bf16[88,1280]{1,0:T(8,128)(2,1)S(1)}, bf16[88,1280]{1,0:T(8,128)(2,1)S(1)}, u32[]{:S(2)}, u32[]{:S(2)}) collective-permute-start(bf16[88,1280]{1,0:T(8,128)(2,1)S(1)} %collective-permute-done.refs_0_), channel_id=1, source_target_pairs={{0,1},{1,0},{2,3},{3,2},{4,5},{5,4},{6,7},{7,6},{8,24},{9,25},{10,... | collective-permute-start | bytes 675848 | tf_op jit(solution)/shard_map/ppermute | solution.py:244
  47.2 3.9 %collective-permute-start.27 = (bf16[88,1280]{1,0:T(8,128)(2,1)S(1)}, bf16[88,1280]{1,0:T(8,128)(2,1)S(1)}, u32[]{:S(2)}, u32[]{:S(2)}) collective-permute-start(bf16[88,1280]{1,0:T(8,128)(2,1)S(1)} %collective-permute-done.refs_0_), channel_id=1, source_target_pairs={{0,8},{1,9},{2,10},{3,11},{4,12},{5,13},{6,14},{7,15},{8,0},{9,1},... | collective-permute-start | bytes 675848 | tf_op jit(solution)/shard_map/ppermute | solution.py:245
  47.2 6.9 %collective-permute-start.26 = (bf16[88,1280]{1,0:T(8,128)(2,1)S(1)}, bf16[88,1280]{1,0:T(8,128)(2,1)S(1)}, u32[]{:S(2)}, u32[]{:S(2)}) collective-permute-start(bf16[88,1280]{1,0:T(8,128)(2,1)S(1)} %collective-permute-done.24.refs_1_), channel_id=1, source_target_pairs={{0,1},{1,0},{2,3},{3,2},{4,5},{5,4},{6,7},{7,6},{8,24},{9,25},{10,... | collective-permute-start | bytes 675848 | tf_op jit(solution)/shard_map/ppermute | solution.py:244
  47.7 6.4 %collective-permute-start.28 = (bf16[88,1280]{1,0:T(8,128)(2,1)S(1)}, bf16[88,1280]{1,0:T(8,128)(2,1)S(1)}, u32[]{:S(2)}, u32[]{:S(2)}) collective-permute-start(bf16[88,1280]{1,0:T(8,128)(2,1)S(1)} %collective-permute-done.24.refs_1_), channel_id=1, source_target_pairs={{0,8},{1,9},{2,10},{3,11},{4,12},{5,13},{6,14},{7,15},{8,0},{9,1},... | collective-permute-start | bytes 675848 | tf_op jit(solution)/shard_map/ppermute | solution.py:245
  48.9 5.7 %collective-permute-start.22 = (bf16[80,1280]{1,0:T(8,128)(2,1)S(1)}, bf16[80,1280]{1,0:T(8,128)(2,1)S(1)}, u32[]{:S(2)}, u32[]{:S(2)}) collective-permute-start(bf16[80,1280]{1,0:T(8,128)(2,1)S(1)} %get-tuple-element.61), channel_id=1, source_target_pairs={{0,8},{1,9},{2,10},{3,11},{4,12},{5,13},{6,14},{7,15},{8,0},{9,1},... | collective-permute-start | bytes 614408 | tf_op jit(solution)/shard_map/ppermute | solution.py:250
  49.6 7.2 %collective-permute-start.36 = (bf16[88,1280]{1,0:T(8,128)(2,1)S(1)}, bf16[88,1280]{1,0:T(8,128)(2,1)S(1)}, u32[]{:S(2)}, u32[]{:S(2)}) collective-permute-start(bf16[88,1280]{1,0:T(8,128)(2,1)S(1)} %collective-permute-done.1.refs_0_), channel_id=1, source_target_pairs={{0,16},{1,17},{2,18},{3,19},{4,20},{5,21},{6,22},{7,23},{8,9},{9,8... | collective-permute-start | bytes 675848 | tf_op jit(solution)/shard_map/ppermute | solution.py:243
  51.1 4.2 %collective-permute-start.29 = (bf16[88,1280]{1,0:T(8,128)(2,1)S(1)}, bf16[88,1280]{1,0:T(8,128)(2,1)S(1)}, u32[]{:S(2)}, u32[]{:S(2)}) collective-permute-start(bf16[88,1280]{1,0:T(8,128)(2,1)S(1)} %collective-permute-done.25.refs_2_), channel_id=1, source_target_pairs={{0,8},{1,9},{2,10},{3,11},{4,12},{5,13},{6,14},{7,15},{8,0},{9,1},... | collective-permute-start | bytes 675848 | tf_op jit(solution)/shard_map/ppermute | solution.py:245
  54.1 9.6 %collective-permute-start.6 = (bf16[80,1280]{1,0:T(8,128)(2,1)S(1)}, bf16[80,1280]{1,0:T(8,128)(2,1)S(1)}, u32[]{:S(2)}, u32[]{:S(2)}) collective-permute-start(bf16[80,1280]{1,0:T(8,128)(2,1)S(1)} %get-tuple-element.52), channel_id=1, source_target_pairs={{0,8},{1,9},{2,10},{3,11},{4,12},{5,13},{6,14},{7,15},{8,0},{9,1},... | collective-permute-start | bytes 614408 | tf_op jit(solution)/shard_map/ppermute | solution.py:250
  54.1 2.7 %collective-permute-start.30 = (bf16[88,1280]{1,0:T(8,128)(2,1)S(1)}, bf16[88,1280]{1,0:T(8,128)(2,1)S(1)}, u32[]{:S(2)}, u32[]{:S(2)}) collective-permute-start(bf16[88,1280]{1,0:T(8,128)(2,1)S(1)} %collective-permute-done.26.refs_3_), channel_id=1, source_target_pairs={{0,8},{1,9},{2,10},{3,11},{4,12},{5,13},{6,14},{7,15},{8,0},{9,1},... | collective-permute-start | bytes 675848 | tf_op jit(solution)/shard_map/ppermute | solution.py:245
  54.7 7.5 %collective-permute-start.11 = (bf16[80,1280]{1,0:T(8,128)(2,1)S(1)}, bf16[80,1280]{1,0:T(8,128)(2,1)S(1)}, u32[]{:S(2)}, u32[]{:S(2)}) collective-permute-start(bf16[80,1280]{1,0:T(8,128)(2,1)S(1)} %add_convert_fusion.10), channel_id=1, source_target_pairs={{0,1},{1,0},{2,3},{3,2},{4,5},{5,4},{6,7},{7,6},{8,24},{9,25},{10,... | collective-permute-start | bytes 614408 | tf_op jit(solution)/shard_map/ppermute | solution.py:258
  55.3 10.4 %collective-permute-start.37 = (bf16[88,1280]{1,0:T(8,128)(2,1)S(1)}, bf16[88,1280]{1,0:T(8,128)(2,1)S(1)}, u32[]{:S(2)}, u32[]{:S(2)}) collective-permute-start(bf16[88,1280]{1,0:T(8,128)(2,1)S(1)} %collective-permute-done.1.refs_0_), channel_id=1, source_target_pairs={{0,1},{1,0},{2,3},{3,2},{4,5},{5,4},{6,7},{7,6},{8,24},{9,25},{10,... | collective-permute-start | bytes 675848 | tf_op jit(solution)/shard_map/ppermute | solution.py:244
  56.9 16.8 %collective-permute-start.39 = (bf16[88,1280]{1,0:T(8,128)(2,1)S(1)}, bf16[88,1280]{1,0:T(8,128)(2,1)S(1)}, u32[]{:S(2)}, u32[]{:S(2)}) collective-permute-start(bf16[88,1280]{1,0:T(8,128)(2,1)S(1)} %collective-permute-done.1.refs_0_), channel_id=1, source_target_pairs={{0,8},{1,9},{2,10},{3,11},{4,12},{5,13},{6,14},{7,15},{8,0},{9,1},... | collective-permute-start | bytes 675848 | tf_op jit(solution)/shard_map/ppermute | solution.py:245
  56.9 8.9 %collective-permute-start.38 = (bf16[88,1280]{1,0:T(8,128)(2,1)S(1)}, bf16[88,1280]{1,0:T(8,128)(2,1)S(1)}, u32[]{:S(2)}, u32[]{:S(2)}) collective-permute-start(bf16[88,1280]{1,0:T(8,128)(2,1)S(1)} %collective-permute-done.36.refs_1_), channel_id=1, source_target_pairs={{0,1},{1,0},{2,3},{3,2},{4,5},{5,4},{6,7},{7,6},{8,24},{9,25},{10,... | collective-permute-start | bytes 675848 | tf_op jit(solution)/shard_map/ppermute | solution.py:244
  62.2 2.6 %collective-permute-start.31 = (bf16[80,1280]{1,0:T(8,128)(2,1)S(1)}, bf16[80,1280]{1,0:T(8,128)(2,1)S(1)}, u32[]{:S(2)}, u32[]{:S(2)}) collective-permute-start(bf16[80,1280]{1,0:T(8,128)(2,1)S(1)} %get-tuple-element.65), channel_id=1, source_target_pairs={{0,8},{1,9},{2,10},{3,11},{4,12},{5,13},{6,14},{7,15},{8,0},{9,1},... | collective-permute-start | bytes 614408 | tf_op jit(solution)/shard_map/ppermute | solution.py:250
  63.7 1.5 %collective-permute-start.32 = (bf16[80,1280]{1,0:T(8,128)(2,1)S(1)}, bf16[80,1280]{1,0:T(8,128)(2,1)S(1)}, u32[]{:S(2)}, u32[]{:S(2)}) collective-permute-start(bf16[80,1280]{1,0:T(8,128)(2,1)S(1)} %get-tuple-element.67), channel_id=1, source_target_pairs={{0,8},{1,9},{2,10},{3,11},{4,12},{5,13},{6,14},{7,15},{8,0},{9,1},... | collective-permute-start | bytes 614408 | tf_op jit(solution)/shard_map/ppermute | solution.py:250
  64.8 8.3 %collective-permute-start.33 = (bf16[80,1280]{1,0:T(8,128)(2,1)S(1)}, bf16[80,1280]{1,0:T(8,128)(2,1)S(1)}, u32[]{:S(2)}, u32[]{:S(2)}) collective-permute-start(bf16[80,1280]{1,0:T(8,128)(2,1)S(1)} %get-tuple-element.69), channel_id=1, source_target_pairs={{0,8},{1,9},{2,10},{3,11},{4,12},{5,13},{6,14},{7,15},{8,0},{9,1},... | collective-permute-start | bytes 614408 | tf_op jit(solution)/shard_map/ppermute | solution.py:250
  65.2 8.0 %collective-permute-start.23 = (bf16[160,1280]{1,0:T(8,128)(2,1)S(1)}, bf16[160,1280]{1,0:T(8,128)(2,1)S(1)}, u32[]{:S(2)}, u32[]{:S(2)}) collective-permute-start(bf16[160,1280]{1,0:T(8,128)(2,1)S(1)} %add_convert_fusion.2), channel_id=1, source_target_pairs={{0,16},{1,17},{2,18},{3,19},{4,20},{5,21},{6,22},{7,23},{8,9},{9,8... | collective-permute-start | bytes 1228808 | tf_op jit(solution)/shard_map/ppermute | solution.py:255
  65.7 8.2 %collective-permute-start.40 = (bf16[88,1280]{1,0:T(8,128)(2,1)S(1)}, bf16[88,1280]{1,0:T(8,128)(2,1)S(1)}, u32[]{:S(2)}, u32[]{:S(2)}) collective-permute-start(bf16[88,1280]{1,0:T(8,128)(2,1)S(1)} %collective-permute-done.36.refs_1_), channel_id=1, source_target_pairs={{0,8},{1,9},{2,10},{3,11},{4,12},{5,13},{6,14},{7,15},{8,0},{9,1},... | collective-permute-start | bytes 675848 | tf_op jit(solution)/shard_map/ppermute | solution.py:245
  65.8 8.3 %collective-permute-start.41 = (bf16[88,1280]{1,0:T(8,128)(2,1)S(1)}, bf16[88,1280]{1,0:T(8,128)(2,1)S(1)}, u32[]{:S(2)}, u32[]{:S(2)}) collective-permute-start(bf16[88,1280]{1,0:T(8,128)(2,1)S(1)} %collective-permute-done.37.refs_2_), channel_id=1, source_target_pairs={{0,8},{1,9},{2,10},{3,11},{4,12},{5,13},{6,14},{7,15},{8,0},{9,1},... | collective-permute-start | bytes 675848 | tf_op jit(solution)/shard_map/ppermute | solution.py:245
  73.1 1.5 %collective-permute-start.42 = (bf16[88,1280]{1,0:T(8,128)(2,1)S(1)}, bf16[88,1280]{1,0:T(8,128)(2,1)S(1)}, u32[]{:S(2)}, u32[]{:S(2)}) collective-permute-start(bf16[88,1280]{1,0:T(8,128)(2,1)S(1)} %collective-permute-done.38.refs_3_), channel_id=1, source_target_pairs={{0,8},{1,9},{2,10},{3,11},{4,12},{5,13},{6,14},{7,15},{8,0},{9,1},... | collective-permute-start | bytes 675848 | tf_op jit(solution)/shard_map/ppermute | solution.py:245
  73.2 7.6 %collective-permute-start.34 = (bf16[80,1280]{1,0:T(8,128)(2,1)S(1)}, bf16[80,1280]{1,0:T(8,128)(2,1)S(1)}, u32[]{:S(2)}, u32[]{:S(2)}) collective-permute-start(bf16[80,1280]{1,0:T(8,128)(2,1)S(1)} %add_convert_fusion.9), channel_id=1, source_target_pairs={{0,1},{1,0},{2,3},{3,2},{4,5},{5,4},{6,7},{7,6},{8,24},{9,25},{10,... | collective-permute-start | bytes 614408 | tf_op jit(solution)/shard_map/ppermute | solution.py:258
  73.6 7.2 %collective-permute-start.20 = (bf16[80,1280]{1,0:T(8,128)(2,1)S(1)}, bf16[80,1280]{1,0:T(8,128)(2,1)S(1)}, u32[]{:S(2)}, u32[]{:S(2)}) collective-permute-start(bf16[80,1280]{1,0:T(8,128)(2,1)S(1)} %get-tuple-element.58), channel_id=1, source_target_pairs={{0,8},{1,9},{2,10},{3,11},{4,12},{5,13},{6,14},{7,15},{8,0},{9,1},... | collective-permute-start | bytes 614408 | tf_op jit(solution)/shard_map/ppermute | solution.py:250
  73.9 9.3 %collective-permute-start.44 = (bf16[80,1280]{1,0:T(8,128)(2,1)S(1)}, bf16[80,1280]{1,0:T(8,128)(2,1)S(1)}, u32[]{:S(2)}, u32[]{:S(2)}) collective-permute-start(bf16[80,1280]{1,0:T(8,128)(2,1)S(1)} %get-tuple-element.74), channel_id=1, source_target_pairs={{0,8},{1,9},{2,10},{3,11},{4,12},{5,13},{6,14},{7,15},{8,0},{9,1},... | collective-permute-start | bytes 614408 | tf_op jit(solution)/shard_map/ppermute | solution.py:250
  74.1 18.1 %collective-permute-start.47 = (bf16[80,1280]{1,0:T(8,128)(2,1)S(1)}, bf16[80,1280]{1,0:T(8,128)(2,1)S(1)}, u32[]{:S(2)}, u32[]{:S(2)}) collective-permute-start(bf16[80,1280]{1,0:T(8,128)(2,1)S(1)} %get-tuple-element.88), channel_id=1, source_target_pairs={{0,8},{1,9},{2,10},{3,11},{4,12},{5,13},{6,14},{7,15},{8,0},{9,1},... | collective-permute-start | bytes 614408 | tf_op jit(solution)/shard_map/ppermute | solution.py:250
  74.6 8.4 %collective-permute-start.45 = (bf16[160,1280]{1,0:T(8,128)(2,1)S(1)}, bf16[160,1280]{1,0:T(8,128)(2,1)S(1)}, u32[]{:S(2)}, u32[]{:S(2)}) collective-permute-start(bf16[160,1280]{1,0:T(8,128)(2,1)S(1)} %add_convert_fusion.1), channel_id=1, source_target_pairs={{0,16},{1,17},{2,18},{3,19},{4,20},{5,21},{6,22},{7,23},{8,9},{9,8... | collective-permute-start | bytes 1228808 | tf_op jit(solution)/shard_map/ppermute | solution.py:255
  80.6 5.2 %copy-start.4 = (f32[1280]{0:T(1024)S(1)}, f32[1280]{0:T(1024)}, u32[]{:S(2)}) copy-start(f32[1280]{0:T(1024)} %gamma_ref.5) | copy-start | bytes 15364
  80.8 2.6 %collective-permute-start.43 = (bf16[80,1280]{1,0:T(8,128)(2,1)S(1)}, bf16[80,1280]{1,0:T(8,128)(2,1)S(1)}, u32[]{:S(2)}, u32[]{:S(2)}) collective-permute-start(bf16[80,1280]{1,0:T(8,128)(2,1)S(1)} %get-tuple-element.73), channel_id=1, source_target_pairs={{0,8},{1,9},{2,10},{3,11},{4,12},{5,13},{6,14},{7,15},{8,0},{9,1},... | collective-permute-start | bytes 614408 | tf_op jit(solution)/shard_map/ppermute | solution.py:250
  80.8 3.6 %collective-permute-start.46 = (bf16[80,1280]{1,0:T(8,128)(2,1)S(1)}, bf16[80,1280]{1,0:T(8,128)(2,1)S(1)}, u32[]{:S(2)}, u32[]{:S(2)}) collective-permute-start(bf16[80,1280]{1,0:T(8,128)(2,1)S(1)} %get-tuple-element.77), channel_id=1, source_target_pairs={{0,8},{1,9},{2,10},{3,11},{4,12},{5,13},{6,14},{7,15},{8,0},{9,1},... | collective-permute-start | bytes 614408 | tf_op jit(solution)/shard_map/ppermute | solution.py:250
  83.0 12.4 %collective-permute-start.50 = (bf16[80,1280]{1,0:T(8,128)(2,1)S(1)}, bf16[80,1280]{1,0:T(8,128)(2,1)S(1)}, u32[]{:S(2)}, u32[]{:S(2)}) collective-permute-start(bf16[80,1280]{1,0:T(8,128)(2,1)S(1)} %get-tuple-element.90), channel_id=1, source_target_pairs={{0,8},{1,9},{2,10},{3,11},{4,12},{5,13},{6,14},{7,15},{8,0},{9,1},... | collective-permute-start | bytes 614408 | tf_op jit(solution)/shard_map/ppermute | solution.py:250
  83.2 9.0 %collective-permute-start.35 = (bf16[80,1280]{1,0:T(8,128)(2,1)S(1)}, bf16[80,1280]{1,0:T(8,128)(2,1)S(1)}, u32[]{:S(2)}, u32[]{:S(2)}) collective-permute-start(bf16[80,1280]{1,0:T(8,128)(2,1)S(1)} %add_convert_fusion.8), channel_id=1, source_target_pairs={{0,2},{1,3},{2,4},{3,5},{4,6},{5,7},{6,0},{7,1},{8,10},{9,11},{10,... | collective-permute-start | bytes 614408 | tf_op jit(solution)/shard_map/ppermute | solution.py:262
  83.4 8.9 %collective-permute-start.48 = (bf16[80,1280]{1,0:T(8,128)(2,1)S(1)}, bf16[80,1280]{1,0:T(8,128)(2,1)S(1)}, u32[]{:S(2)}, u32[]{:S(2)}) collective-permute-start(bf16[80,1280]{1,0:T(8,128)(2,1)S(1)} %add_convert_fusion.7), channel_id=1, source_target_pairs={{0,1},{1,0},{2,3},{3,2},{4,5},{5,4},{6,7},{7,6},{8,24},{9,25},{10,... | collective-permute-start | bytes 614408 | tf_op jit(solution)/shard_map/ppermute | solution.py:258
  84.5 10.9 %collective-permute-start.51 = (bf16[160,1280]{1,0:T(8,128)(2,1)S(1)}, bf16[160,1280]{1,0:T(8,128)(2,1)S(1)}, u32[]{:S(2)}, u32[]{:S(2)}) collective-permute-start(bf16[160,1280]{1,0:T(8,128)(2,1)S(1)} %add_convert_fusion), channel_id=1, source_target_pairs={{0,16},{1,17},{2,18},{3,19},{4,20},{5,21},{6,22},{7,23},{8,9},{9,8... | collective-permute-start | bytes 1228808 | tf_op jit(solution)/shard_map/ppermute | solution.py:255
  92.4 6.4 %collective-permute-start.49 = (bf16[80,1280]{1,0:T(8,128)(2,1)S(1)}, bf16[80,1280]{1,0:T(8,128)(2,1)S(1)}, u32[]{:S(2)}, u32[]{:S(2)}) collective-permute-start(bf16[80,1280]{1,0:T(8,128)(2,1)S(1)} %add_convert_fusion.6), channel_id=1, source_target_pairs={{0,6},{1,7},{2,0},{3,1},{4,2},{5,3},{6,4},{7,5},{8,14},{9,15},{10,... | collective-permute-start | bytes 614408 | tf_op jit(solution)/shard_map/ppermute | solution.py:262
  95.4 5.8 %collective-permute-start.53 = (bf16[80,1280]{1,0:T(8,128)(2,1)S(1)}, bf16[80,1280]{1,0:T(8,128)(2,1)S(1)}, u32[]{:S(2)}, u32[]{:S(2)}) collective-permute-start(bf16[80,1280]{1,0:T(8,128)(2,1)S(1)} %add_convert_fusion.5), channel_id=1, source_target_pairs={{0,1},{1,0},{2,3},{3,2},{4,5},{5,4},{6,7},{7,6},{8,24},{9,25},{10,... | collective-permute-start | bytes 614408 | tf_op jit(solution)/shard_map/ppermute | solution.py:258
  96.3 5.0 %collective-permute-start.52 = (bf16[80,1280]{1,0:T(8,128)(2,1)S(1)}, bf16[80,1280]{1,0:T(8,128)(2,1)S(1)}, u32[]{:S(2)}, u32[]{:S(2)}) collective-permute-start(bf16[80,1280]{1,0:T(8,128)(2,1)S(1)} %get-tuple-element.93), channel_id=1, source_target_pairs={{0,8},{1,9},{2,10},{3,11},{4,12},{5,13},{6,14},{7,15},{8,0},{9,1},... | collective-permute-start | bytes 614408 | tf_op jit(solution)/shard_map/ppermute | solution.py:250
  101.4 10.0 %collective-permute-start.54 = (bf16[80,1280]{1,0:T(8,128)(2,1)S(1)}, bf16[80,1280]{1,0:T(8,128)(2,1)S(1)}, u32[]{:S(2)}, u32[]{:S(2)}) collective-permute-start(bf16[80,1280]{1,0:T(8,128)(2,1)S(1)} %add_convert_fusion.4), channel_id=1, source_target_pairs={{0,4},{1,5},{2,6},{3,7},{4,0},{5,1},{6,2},{7,3},{8,12},{9,13},{10,... | collective-permute-start | bytes 614408 | tf_op jit(solution)/shard_map/ppermute | solution.py:262
  111.5 6.4 %collective-permute-start.56 = (bf16[80,1280]{1,0:T(8,128)(2,1)S(1)}, bf16[80,1280]{1,0:T(8,128)(2,1)S(1)}, u32[]{:S(2)}, u32[]{:S(2)}) collective-permute-start(bf16[80,1280]{1,0:T(8,128)(2,1)S(1)} %multiply_convert_fusion), channel_id=1, source_target_pairs={{0,16},{1,17},{2,18},{3,19},{4,20},{5,21},{6,22},{7,23},{8,24},{9,... | collective-permute-start | bytes 614408 | tf_op jit(solution)/shard_map/ppermute | solution.py:322
  112.8 5.2 %collective-permute-start.55 = (bf16[80,1280]{1,0:T(8,128)(2,1)S(1)}, bf16[80,1280]{1,0:T(8,128)(2,1)S(1)}, u32[]{:S(2)}, u32[]{:S(2)}) collective-permute-start(bf16[80,1280]{1,0:T(8,128)(2,1)S(1)} %multiply_convert_fusion), channel_id=1, source_target_pairs={{0,8},{1,9},{2,10},{3,11},{4,12},{5,13},{6,14},{7,15},{8,0},{9,1},... | collective-permute-start | bytes 614408 | tf_op jit(solution)/shard_map/ppermute | solution.py:323
  117.9 1.5 %collective-permute-start.57 = (bf16[80,1280]{1,0:T(8,128)(2,1)S(1)}, bf16[80,1280]{1,0:T(8,128)(2,1)S(1)}, u32[]{:S(2)}, u32[]{:S(2)}) collective-permute-start(bf16[80,1280]{1,0:T(8,128)(2,1)S(1)} %collective-permute-done.56), channel_id=1, source_target_pairs={{0,8},{1,9},{2,10},{3,11},{4,12},{5,13},{6,14},{7,15},{8,0},{9,1},... | collective-permute-start | bytes 614408 | tf_op jit(solution)/shard_map/ppermute | solution.py:323
  (1 other events, 0.7 us)
